TPU v7x, 1024 devices: a whole 4x8x16 slice. The times are simulated.
1024 devices in a mesh: lon: 128 (over z, y), lat: 8 (over x, core).
Axes of the slice: x: 4, y: 8, z: 16, core: 2. Of those that a mesh axis runs over, the one named last changes fastest.
Arguments:
- features: bfloat16 [32, 2048, 1024], P(None, 'lon', 'lat'), may hold values from -6 to 6
- velocity: float32 [8, 2048, 1024], P(None, 'lon', 'lat'), may hold values from -6 to 6
- velocity_cot: float32 [8, 2048, 1024], P(None, 'lon', 'lat'), may hold values from -6 to 6
- surface_cot: float32 [2048, 1024], P('lon', 'lat'), may hold values from -6 to 6
- damping: float32 [2048, 1024], P('lon', 'lat'), may hold values from 0.05 to 1
- wet_mask: int32 [2048, 1024], P('lon', 'lat'), may hold values 0 or 1
- aggregate_map: int32 [2048, 1024], P('lon', 'lat'), may hold values from 0 to 7
- coarse_inverse: float32 [8192, 8192], P(('lon', 'lat')), as said below
- conv_weight: bfloat16 [64, 288], replicated, may hold values from -0.375 to 0.375
- conv_bias: float32 [64], replicated, may hold values from -3 to 3
- out_weight: float32 [64], replicated, may hold values from -0.75 to 0.75
- level_weight: float32 [8], replicated, may hold values from 0.5 to 1.5
Outputs:
- grad_velocity: float32 [8, 2048, 1024], P(None, 'lon', 'lat')
- grad_conv_weight: float32 [64, 288], replicated
- grad_conv_bias: float32 [64], replicated
- grad_out_weight: float32 [64], replicated
Inputs may be any that keep to these rules, and one draw needn't show every extreme that they name: `coarse_inverse`: symmetric and positive definite.
All inputs are finite; a program needn't handle non-finite values. No bound on the sum of `wet_mask` on one device may be relied on, other than what follows from the above.
Results may differ from a plain program's by a relative error of at most 0.013.
Values sent between devices are 32-bit elements; how exact they have to be, the bound alone decides.
No kernel may reach another device: no remote copies, remote signals or barrier semaphores. Data moves between devices by JAX's collectives and lax.ppermute only.
A program may use at most 32 MiB of HBM per device.

v0:
```python
import math

import jax
import jax.numpy as jnp
from jax import lax
from jax.sharding import PartitionSpec as P

CIN = 32
HID = 64
ITERS = 2
AGG = 8
CNT = 256


time_step = 0.1


def with_halo(block, sides, width, periodic):
    for axis, dim in sides:
        count = lax.axis_size(axis)
        forward = [(i, i + 1) for i in range(count - 1)]
        if periodic:
            forward.append((count - 1, 0))
        backward = [(target, source) for source, target in forward]
        low = lax.ppermute(
            lax.slice_in_dim(block, block.shape[dim] - width, None, axis=dim), axis, forward
        )
        high = lax.ppermute(lax.slice_in_dim(block, 0, width, axis=dim), axis, backward)
        block = jnp.concatenate([low, block, high], axis=dim)
    return block


def widen(field):
    rows = with_halo(field, (("lon", 1),), 1, True)
    return with_halo(rows, (("lat", 2),), 1, False)


def neighbours(padded):
    return (
        padded[..., 2:, 1:-1],
        padded[..., :-2, 1:-1],
        padded[..., 1:-1, 2:],
        padded[..., 1:-1, :-2],
    )


def side_total(padded):
    north, south, east, west = neighbours(padded)
    return north + south + east + west


def patches_of(block):
    rows = block.shape[-2] - 2
    width = block.shape[-1] - 2
    taps = [
        block[:, first : first + rows, second : second + width]
        for first in range(3)
        for second in range(3)
    ]
    return jnp.concatenate(taps, axis=0).reshape(-1, rows * width)


def total(values):
    return lax.psum(lax.psum(values, "lat"), "lon")


def shards(
    features,
    velocity,
    velocity_cot,
    surface_cot,
    damping,
    wet_mask,
    aggregate_map,
    coarse_inverse,
    conv_weight,
    conv_bias,
    out_weight,
    level_weight,
):
    wet = wet_mask.astype(jnp.float32)
    diagonal = 4.0 + damping
    early = widen(jnp.concatenate([features.astype(jnp.float32), velocity], axis=0))
    feat_pad = early[:CIN].astype(jnp.bfloat16)
    vel_pad = early[CIN:]
    columns = patches_of(feat_pad)
    hidden = jnp.tanh(
        jnp.dot(conv_weight, columns, preferred_element_type=jnp.float32) + conv_bias[:, None]
    )
    logits = jnp.sum(out_weight[:, None] * hidden, axis=0).reshape(damping.shape)
    viscosity = jax.nn.softplus(logits)
    labels = jnp.arange(AGG, dtype=jnp.int32)[:, None, None]
    onehot = (aggregate_map[None] == labels).astype(jnp.float32)

    def precondition(residual):
        local = jnp.sum(onehot * residual[None], axis=(1, 2)) / math.sqrt(CNT)
        every = lax.all_gather(local, ("lon", "lat"), axis=0, tiled=True)
        own = jnp.dot(coarse_inverse, every, precision=lax.Precision.HIGHEST)
        return residual / diagonal + jnp.sum(onehot * own[:, None, None], axis=0)

    solution = jnp.zeros_like(surface_cot)
    residual = surface_cot
    search = precondition(residual)
    energy = total(jnp.sum(residual * search)[None])[0]
    for step in range(ITERS):
        padded = widen((wet * search)[None])[0]
        image = diagonal * search - wet * side_total(padded)
        step_size = energy / total(jnp.sum(search * image)[None])[0]
        solution = solution + step_size * search
        residual = residual - step_size * image
        if step + 1 < ITERS:
            smoothed = precondition(residual)
            energy_next = total(jnp.sum(residual * smoothed)[None])[0]
            search = smoothed + energy_next / energy * search
            energy = energy_next
    middle = widen(jnp.stack([wet * solution, viscosity]))
    forcing = side_total(middle[0]) - 4.0 * wet * solution
    visc_pad = middle[1]
    adjoint_vel = velocity_cot + level_weight[:, None, None] * forcing[None]
    adj_pad = widen(adjoint_vel)
    spread = jnp.zeros_like(adjoint_vel)
    grad_visc = jnp.zeros_like(viscosity)
    for visc_side, vel_side, adj_side in zip(
        neighbours(visc_pad), neighbours(vel_pad), neighbours(adj_pad)
    ):
        change = adj_side - adjoint_vel
        spread = spread + 0.5 * (viscosity + visc_side)[None] * change
        grad_visc = grad_visc + jnp.sum((vel_side - velocity) * change, axis=0)
    grad_velocity = adjoint_vel + time_step * spread
    grad_visc = -0.5 * time_step * grad_visc
    cells_all = damping.shape[0] * damping.shape[1] * lax.axis_size("lon") * lax.axis_size("lat")
    grad_logit = (grad_visc * jax.nn.sigmoid(logits)).reshape(-1) / math.sqrt(cells_all)
    out_grad = jnp.sum(hidden * grad_logit[None], axis=1)
    grad_pre = (grad_logit[None] * out_weight[:, None] * (1.0 - hidden * hidden)).astype(
        jnp.bfloat16
    )
    bias_grad = jnp.sum(grad_pre.astype(jnp.float32), axis=1)
    weight_grad = lax.dot_general(
        grad_pre, columns, (((1,), (1,)), ((), ())), preferred_element_type=jnp.float32
    )
    packed = total(jnp.concatenate([weight_grad.reshape(-1), bias_grad, out_grad]))
    weight_count = HID * 9 * CIN
    grad_conv_weight = packed[:weight_count].reshape(HID, 9 * CIN)
    grad_conv_bias = packed[weight_count : weight_count + HID]
    grad_out_weight = packed[weight_count + HID :]
    return (grad_velocity, grad_conv_weight, grad_conv_bias, grad_out_weight)


def solution(mesh):
    in_specs = (
        P(None, "lon", "lat"),
        P(None, "lon", "lat"),
        P(None, "lon", "lat"),
        P("lon", "lat"),
        P("lon", "lat"),
        P("lon", "lat"),
        P("lon", "lat"),
        P(("lon", "lat"), None),
        P(),
        P(),
        P(),
        P(),
    )
    out_specs = (P(None, "lon", "lat"), P(), P(), P())
    return jax.shard_map(shards, mesh=mesh, in_specs=in_specs, out_specs=out_specs, check_vma=False)
```

profile of v0, /device:TPU:1, one launch (start us, length us, event | category | flops | bytes accessed | tf_op | source)
XLA Modules:
  0.0 1570.2 jit_solution(11211023359165281687)
XLA Ops:
  8.3 136.9 %all-reduce = f32[8192]{0:T(1024)S(1)} all-reduce(f32[8192]{0:T(1024)S(1)} %multiply_dynamic-update-slice_fusion.1), channel_id=1, replica_groups=mesh['lon'=128,'lat'=8] {'lon','lat'}, use_global_device_ids=true, to_apply=%add | all-reduce | flops 8192 | bytes 65536
  152.8 4.2 collective-permute-done
  157.1 3.7 collective-permute-start.3
  165.5 12.5 all-reduce.3
  177.9 221.0 %all-reduce.2 = (f32[1]{0:T(128)}, f32[1]{0:T(128)}) all-reduce(f32[1]{0:T(128)} %get-tuple-element.12, f32[1]{0:T(128)} %get-tuple-element.13), channel_id=1, replica_groups=mesh['lon'=128,'lat'=8] {'lon'}, use_global_device_ids=true, to_apply=%region_4.5 | all-reduce | flops 2 | bytes 16 | tf_op jit(solution)/shard_map/psum | solution.py:64
  401.9 171.5 %all-reduce.1 = f32[8192]{0:T(1024)S(1)} all-reduce(f32[8192]{0:T(1024)S(1)} %multiply_dynamic-update-slice_fusion), channel_id=1, replica_groups=mesh['lon'=128,'lat'=8] {'lon','lat'}, use_global_device_ids=true, to_apply=%add.1 | all-reduce | flops 8192 | bytes 65536
  575.5 13.1 psum.74
  588.6 220.8 %psum.75 = f32[1]{0:T(128)} all-reduce(f32[1]{0:T(128)} %psum.74), channel_id=1, replica_groups=mesh['lon'=128,'lat'=8] {'lon'}, use_global_device_ids=true, to_apply=%region_12.13 | all-reduce | flops 1 | bytes 8 | tf_op jit(solution)/shard_map/psum | solution.py:64
  810.8 3.4 collective-permute-start.5
  816.2 6.7 collective-permute-start.9
  823.0 59.5 %collective-permute-start.7 = (f32[1,18,1]{2,1,0:T(8,128)S(1)}, f32[1,18,1]{2,1,0:T(8,128)S(1)}, u32[]{:S(2)}, u32[]{:S(2)}) collective-permute-start(f32[1,18,1]{2,1,0:T(8,128)S(1)} %get-tuple-element.40), channel_id=1, source_target_pairs={{1,0},{2,1},{3,2},{4,3},{5,4},{6,5},{7,6},{9,8},{10,9},{11,10},{12... | collective-permute-start | bytes 224 | tf_op jit(solution)/shard_map/ppermute | solution.py:28
  886.4 12.6 psum.76
  900.8 225.8 %psum.77 = f32[1]{0:T(128)} all-reduce(f32[1]{0:T(128)} %psum.76), channel_id=1, replica_groups=mesh['lon'=128,'lat'=8] {'lon'}, use_global_device_ids=true, to_apply=%region_15.16 | all-reduce | flops 1 | bytes 8 | tf_op jit(solution)/shard_map/psum | solution.py:64
  1128.3 57.0 %collective-permute-start.10 = (f32[40,18,1]{2,1,0:T(8,128)S(1)}, f32[40,18,1]{2,1,0:T(8,128)S(1)}, u32[]{:S(2)}, u32[]{:S(2)}) collective-permute-start(f32[40,18,1]{2,1,0:T(8,128)S(1)} %get-tuple-element.20), channel_id=1, source_target_pairs={{0,1},{1,2},{2,3},{3,4},{4,5},{5,6},{6,7},{8,9},{9,10},{10,11},{11... | collective-permute-start | bytes 8648 | tf_op jit(solution)/shard_map/ppermute | solution.py:25
  1187.4 3.7 collective-permute-done.10
  1191.3 4.2 collective-permute-done.11
  1202.4 4.3 collective-permute-done.12
  1208.7 3.6 collective-permute-start.14
  1215.5 3.4 collective-permute-start.17
  1218.9 4.3 collective-permute-done.17
  1223.3 5.4 collective-permute-start.19
  1230.8 3.9 collective-permute-done.18
  1236.7 65.3 %all-reduce.7.cloned.1.call-done = f32[18560]{0:T(1024)} async-done(((f32[18560]{0:T(1024)}), f32[18560]{0:T(1024)}) %all-reduce.7.cloned.1.call-update) | async-done | bytes 74256 | tf_op jit(solution)/shard_map/psum | solution.py:64
  1302.8 257.6 %all-reduce.9.cloned.1.call-done = f32[18560]{0:T(1024)} async-done(((f32[18560]{0:T(1024)}), f32[18560]{0:T(1024)}) %all-reduce.9.cloned.1.call-update) | async-done | bytes 74256 | tf_op jit(solution)/shard_map/psum | solution.py:64
  (116 shorter events, 47.3 us)
Async XLA Ops:
  7.2 803.6 %copy-start.2 = (s32[16,128]{1,0:T(8,128)S(1)}, s32[16,128]{1,0:T(8,128)}, u32[]{:S(2)}) copy-start(s32[16,128]{1,0:T(8,128)} %param.17) | copy-start | bytes 24580
  7.2 809.0 %copy-start.1 = (f32[8,16,128]{2,1,0:T(8,128)S(1)}, f32[8,16,128]{2,1,0:T(8,128)}, u32[]{:S(2)}) copy-start(f32[8,16,128]{2,1,0:T(8,128)} %param.13) | copy-start | bytes 196612
  7.2 1294.7 %all-reduce.7.cloned.1.call-start = ((), (), s32[]{:S(2)}) async-start(), calls=%async_computation | async-start | bytes 155648 | tf_op jit(solution)/shard_map/psum | solution.py:64
  147.5 5.3 collective-permute-start.1
  149.4 7.6 collective-permute-start
  157.1 6.1 collective-permute-start.3
  160.8 3.1 collective-permute-start.2
  810.8 12.1 collective-permute-start.5
  814.2 8.7 collective-permute-start.4
  816.2 311.8 %collective-permute-start.9 = (f32[40,1,128]{2,1,0:T(1,128)S(1)}, f32[40,1,128]{2,1,0:T(1,128)S(1)}, u32[]{:S(2)}, u32[]{:S(2)}) collective-permute-start(f32[40,1,128]{2,1,0:T(1,128)S(1)} %get-tuple-element.22), channel_id=1, source_target_pairs={{8,0},{16,8},{24,16},{32,24},{40,32},{48,40},{56,48},{64,56},{72,6... | collective-permute-start | bytes 61448 | tf_op jit(solution)/shard_map/ppermute | solution.py:28
  823.0 61.4 %collective-permute-start.7 = (f32[1,18,1]{2,1,0:T(8,128)S(1)}, f32[1,18,1]{2,1,0:T(8,128)S(1)}, u32[]{:S(2)}, u32[]{:S(2)}) collective-permute-start(f32[1,18,1]{2,1,0:T(8,128)S(1)} %get-tuple-element.40), channel_id=1, source_target_pairs={{1,0},{2,1},{3,2},{4,3},{5,4},{6,5},{7,6},{9,8},{10,9},{11,10},{12... | collective-permute-start | bytes 224 | tf_op jit(solution)/shard_map/ppermute | solution.py:28
  882.5 3.1 collective-permute-start.6
  898.9 229.1 %collective-permute-start.8 = (f32[40,1,128]{2,1,0:T(1,128)S(1)}, f32[40,1,128]{2,1,0:T(1,128)S(1)}, u32[]{:S(2)}, u32[]{:S(2)}) collective-permute-start(f32[40,1,128]{2,1,0:T(1,128)S(1)} %get-tuple-element.21), channel_id=1, source_target_pairs={{0,8},{8,16},{16,24},{24,32},{32,40},{40,48},{48,56},{56,64},{64,7... | collective-permute-start | bytes 61448 | tf_op jit(solution)/shard_map/ppermute | solution.py:25
  1128.3 62.8 %collective-permute-start.10 = (f32[40,18,1]{2,1,0:T(8,128)S(1)}, f32[40,18,1]{2,1,0:T(8,128)S(1)}, u32[]{:S(2)}, u32[]{:S(2)}) collective-permute-start(f32[40,18,1]{2,1,0:T(8,128)S(1)} %get-tuple-element.20), channel_id=1, source_target_pairs={{0,1},{1,2},{2,3},{3,4},{4,5},{5,6},{6,7},{8,9},{9,10},{10,11},{11... | collective-permute-start | bytes 8648 | tf_op jit(solution)/shard_map/ppermute | solution.py:25
  1185.3 10.1 collective-permute-start.11
  1197.1 5.3 collective-permute-start.13
  1199.1 7.6 collective-permute-start.12
  1206.8 5.6 collective-permute-start.15
  1208.7 4.6 collective-permute-start.14
  1213.6 5.3 collective-permute-start.16
  1215.5 7.7 collective-permute-start.17
  1223.3 7.3 collective-permute-start.19
  1228.7 5.9 collective-permute-start.18
  1236.6 323.8 %all-reduce.9.cloned.1.call-start = ((), (), s32[]{:S(2)}) async-start(), calls=%async_computation.1 | async-start | bytes 155648 | tf_op jit(solution)/shard_map/psum | solution.py:64
  (8 other events, 1323.1 us)
Sparse Core Ops, SparseCore 0:
  1236.7 65.2 all-reduce.6
  1305.8 254.5 all-reduce.8
where the time goes:
time: 1580 us; the launch traced here: 1570 us
  blocking collectives  1010 us (64%)
  waiting for transfers between devices  350 us (22%)
  starting transfers between devices  169 us (11%)
  between operations  18.6 us (1%)
    psum x6, blocking collectives, total(): return lax.psum(lax.psum(values, 'lat'), 'lon')  706 us
    psum x2, waiting for transfers between devices, total(): return lax.psum(lax.psum(values, 'lat'), 'lon')  323 us
    unnamed x2, blocking collectives  308 us
    ppermute x10, starting transfers between devices, with_halo(): lax.ppermute(lax.slice_in_dim(block, 0, width, axis=dim), axis, backward)  84.9 us
    ppermute x10, starting transfers between devices, with_halo(): lax.ppermute(lax.slice_in_dim(block, block.shape[dim] - width, None, axis...  84.2 us
  transfers between devices with their start and end apart: 22, of which 11 were waited for; matrix products, arithmetic and copies ran while one was open for 0% of the time, Pallas kernels for 0%

commit v1 on v0

v1 whole, which is shorter than its diff:
```python
import math

import jax
import jax.numpy as jnp
import numpy as np
from jax import lax
from jax.experimental import pallas as pl
from jax.experimental.pallas import tpu as pltpu
from jax.sharding import Mesh
from jax.sharding import PartitionSpec as P

CIN = 32
HID = 64
AGG = 8
CNT = 256
TAPS = 9 * CIN
time_step = 0.1

CLON = 16
CLAT = 128
HALO = 3
ROWS = 24
LANES = 256
LON = ("z", "y")
LAT = ("x", "c")
PLANE = ("y", "x")
COLUMN = ("z", "c")


def exchange(values, axes):
    return lax.all_to_all(values, axes, 0, 0, tiled=True)


def shifted(block, axes, periodic):
    count = lax.axis_size(axes)
    forward = [(i, i + 1) for i in range(count - 1)]
    if periodic:
        forward.append((count - 1, 0))
    return forward, [(target, source) for source, target in forward]


def ring_lanes(own, right, left):
    gap = LANES - CLAT - right.shape[-1] - left.shape[-1]
    return jnp.concatenate([own, right, jnp.zeros(own.shape[:-1] + (gap,), own.dtype), left], axis=-1)


def ring_rows(own, below, above):
    gap = ROWS - CLON - below.shape[-2] - above.shape[-2]
    shape = own.shape[:-2] + (gap, own.shape[-1])
    return jnp.concatenate([own, below, jnp.zeros(shape, own.dtype), above], axis=-2)


def roll(value, shift, axis):
    return pltpu.roll(value, shift % value.shape[axis], axis)


def sides(value):
    return (roll(value, -1, 0), roll(value, 1, 0), roll(value, -1, 1), roll(value, 1, 1))


def side_sum(value):
    a, b, c, d = sides(value)
    return (a + b) + (c + d)


def coarse_column(tiles, groups, vector):
    count = vector.shape[0]
    out = []
    for group in range(groups):
        acc = tiles[group * count] * vector[0:1]
        for k in range(1, count):
            acc = acc + tiles[group * count + k] * vector[k : k + 1]
        out.append(jnp.sum(acc, axis=1, keepdims=True))
    return out


def coarse_field(agg, above, middle, below):
    lane = lax.broadcasted_iota(jnp.int32, (1, CLAT), 1)
    row = lax.broadcasted_iota(jnp.int32, (ROWS - CLON, LANES), 0)

    def across(columns, k):
        left, own, right = (column[k : k + 1] for column in columns)
        side = jnp.where(lane < CLAT // 2, right, left)
        return jnp.concatenate([jnp.broadcast_to(own, (1, CLAT)), side], axis=1)

    field = jnp.zeros((ROWS, LANES), jnp.float32)
    for k in range(AGG):
        inner = jnp.broadcast_to(across(middle, k), (CLON, LANES))
        outer = jnp.where(row < (ROWS - CLON) // 2, across(below, k), across(above, k))
        field = jnp.where(agg == float(k), jnp.concatenate([inner, outer], axis=0), field)
    return field


def total(value):
    return jnp.sum(jnp.sum(value, axis=0, keepdims=True), axis=1, keepdims=True)


def restricted(value, agg, first):
    parts = [jnp.sum(jnp.where(agg == float(k), value, 0.0), axis=0, keepdims=True) for k in range(AGG)]
    sums = jnp.sum(jnp.concatenate(parts, axis=0), axis=1, keepdims=True) * (1.0 / math.sqrt(CNT))
    lane = lax.broadcasted_iota(jnp.int32, (AGG, 128), 1)
    row = lax.broadcasted_iota(jnp.int32, (AGG, 128), 0)
    return jnp.sum(jnp.where(lane == first + row, sums, 0.0), axis=0, keepdims=True)


def vector_of(ref, packed):
    count = ref.shape[0] // packed
    value = ref[pl.ds(0, count, stride=packed), :]
    for t in range(1, packed):
        value = value + ref[pl.ds(t, count, stride=packed), :]
    return value


def solve_first(packed, place, gathered, tiles_own, tiles_below, tiles_above, fields, w_ref, f_ref, z_ref, row_ref, sum_ref):
    vector = vector_of(gathered, packed)
    rhs, damp, wet, agg = (fields[k] for k in range(4))
    diagonal = 4.0 + damp
    middle = coarse_column(tiles_own, 3, vector)
    below = coarse_column(tiles_below, 3, vector)
    above = coarse_column(tiles_above, 3, vector)
    z = rhs / diagonal + coarse_field(agg, above, middle, below)
    spread = side_sum(wet * z)
    w = diagonal * z - wet * spread
    w_ref[...] = w
    f_ref[...] = spread - 4.0 * wet * z
    own = (slice(0, CLON), slice(0, CLAT))
    z_own, w_own = z[own], w[own]
    z_ref[...] = z_own
    row_ref[...] = restricted(w_own, agg[own], place[0])
    lane = lax.broadcasted_iota(jnp.int32, (1, 128), 1)
    sum_ref[...] = jnp.where(lane == 0, total(rhs[own] * z_own), 0.0) + jnp.where(lane == 1, total(z_own * w_own), 0.0)


def solve_second(
    packed, gathered, tiles_own, tiles_below, tiles_above, fields, w_ref, f_ref, visc_ref, valid_ref, weight_ref,
    slope_ref, first_ref, sum_in, grad_ref, spread_ref, sum_ref,
):
    vector = vector_of(gathered, packed)
    rhs, damp, wet, agg = (fields[k] for k in range(4))
    diagonal = 4.0 + damp
    w = w_ref[...]
    middle = coarse_column(tiles_own, 3, vector)
    below = coarse_column(tiles_below, 3, vector)
    above = coarse_column(tiles_above, 3, vector)
    y = w / diagonal + coarse_field(agg, above, middle, below)
    around = side_sum(wet * y)
    image = diagonal * y - wet * around
    own = (slice(0, CLON), slice(0, CLAT))
    y_own = y[own]
    lane = lax.broadcasted_iota(jnp.int32, (1, 128), 1)
    sums = sum_in[...]
    for at, value in ((2, rhs[own] * y_own), (3, w[own] * y_own), (4, y_own * image[own])):
        sums = sums + jnp.where(lane == at, total(value), 0.0)
    sum_ref[...] = sums
    visc = visc_ref[...]
    visc_own = visc[own]
    visc_sides = [0.5 * (visc_own + side[own]) for side in sides(visc)]
    valid = valid_ref[...]
    weight = weight_ref[...]
    grad_ref[0] = first_ref[...] * weight
    for at, force in ((0, f_ref[...] * valid), (1, (around - 4.0 * wet * y) * valid)):
        force_own = force[own]
        bend = jnp.zeros((CLON, CLAT), jnp.float32)
        slope = jnp.zeros((CLON, CLAT), jnp.float32)
        for n, side in enumerate(sides(force)):
            change = side[own] - force_own
            bend = bend + visc_sides[n] * change
            slope = slope + slope_ref[n] * change
        spread_ref[at] = force_own + time_step * bend
        grad_ref[at + 1] = slope * weight


def neighbours(padded):
    return (padded[..., 2:, 1:-1], padded[..., :-2, 1:-1], padded[..., 1:-1, 2:], padded[..., 1:-1, :-2])


def patches_of(block):
    rows = block.shape[-2] - 2
    width = block.shape[-1] - 2
    taps = [
        block[:, first : first + rows, second : second + width]
        for first in range(3)
        for second in range(3)
    ]
    return jnp.concatenate(taps, axis=0).reshape(-1, rows * width)


def tiles_of(rows):
    count, width = rows.shape
    return rows.reshape(count // 8, 8, width // 128, 128).transpose(0, 2, 1, 3).reshape(-1, 8, 128)


def rows_of(tiles, count):
    return tiles.reshape(count // 8, -1, 8, 128).transpose(0, 2, 1, 3).reshape(count, -1)


def kernel_call(body, shapes, *args, smem=0):
    specs = [pl.BlockSpec(memory_space=pltpu.SMEM)] * smem + [pl.BlockSpec(memory_space=pltpu.VMEM)] * (len(args) - smem)
    return pl.pallas_call(
        body,
        out_shape=[jax.ShapeDtypeStruct(shape, jnp.float32) for shape in shapes],
        in_specs=specs,
        out_specs=[pl.BlockSpec(memory_space=pltpu.VMEM)] * len(shapes),
        compiler_params=pltpu.CompilerParams(vmem_limit_bytes=24 * 1024 * 1024),
    )(*args)


def shards(
    features,
    velocity,
    velocity_cot,
    surface_cot,
    damping,
    wet_mask,
    aggregate_map,
    coarse_inverse,
    conv_weight,
    conv_bias,
    out_weight,
    level_weight,
):
    f32 = jnp.float32
    n_lon, n_lat = lax.axis_size(LON), lax.axis_size(LAT)
    lon, lat = lax.axis_index(LON), lax.axis_index(LAT)
    per = n_lat * AGG
    packed = 128 // per
    place = (lat * AGG + (lon % packed) * per).astype(jnp.int32)

    single = jnp.concatenate([features.astype(f32), velocity, velocity_cot], axis=0)
    several = jnp.stack([surface_cot, damping, wet_mask.astype(f32), aggregate_map.astype(f32)])
    n_single, n_several = single.shape[0], several.shape[0]
    coarse = tiles_of(coarse_inverse)

    def side_tiles(line, block):
        edge = jnp.concatenate([line, block.transpose(0, 2, 1).reshape(-1, CLON)], axis=0)
        edge = jnp.pad(edge, ((0, 64 - edge.shape[0]), (0, 0))).reshape(1, 8, 128)
        return jnp.concatenate([coarse, edge], axis=0)

    forward, backward = shifted(single, LAT, False)
    left = lax.ppermute(side_tiles(single[:, :, -1], several[:, :, -HALO:]), LAT, forward)
    right = lax.ppermute(side_tiles(single[:, :, 0], several[:, :, :HALO]), LAT, backward)

    local = restricted(surface_cot, aggregate_map.astype(f32), place)

    def across_lat(rows):
        return exchange(rows, LAT)

    row = jnp.sum(across_lat(jnp.broadcast_to(local[None], (n_lat, 1, 128))), axis=0)
    row, left, right = lax.optimization_barrier((row, left, right))

    def unpack(tiles):
        edge = tiles[-1].reshape(64, CLON)
        block = edge[n_single : n_single + n_several * HALO].reshape(n_several, HALO, CLON)
        return tiles[:-1], edge[:n_single], block.transpose(0, 2, 1)

    coarse_left, line_left, block_left = unpack(left)
    coarse_right, line_right, block_right = unpack(right)
    band = jnp.concatenate([coarse_left, coarse, coarse_right], axis=0)
    several = ring_lanes(several, block_right, block_left)

    def end_tiles(at, block):
        line = ring_lanes(single[:, at, :], line_right[:, at : at + 1], line_left[:, at : at + 1])
        edge = jnp.concatenate([line, block.reshape(-1, LANES)], axis=0)
        edge = jnp.pad(edge, ((0, 64 - edge.shape[0]), (0, 0)))
        return jnp.concatenate([band, tiles_of(edge)], axis=0)

    forward, backward = shifted(single, LON, True)
    above = lax.ppermute(end_tiles(CLON - 1, several[:, -HALO:]), LON, forward)
    below = lax.ppermute(end_tiles(0, several[:, :HALO]), LON, backward)
    gathered = exchange(jnp.broadcast_to(row[None], (n_lon, 1, 128)), LON).reshape(n_lon, 128)
    gathered, above, below = lax.optimization_barrier((gathered, above, below))

    count = band.shape[0]

    def unpack_rows(tiles):
        edge = rows_of(tiles[count:], 64)
        block = edge[n_single : n_single + n_several * HALO].reshape(n_several, HALO, LANES)
        return tiles[:count], edge[:n_single], block

    band_above, line_above, block_above = unpack_rows(above)
    band_below, line_below, block_below = unpack_rows(below)
    fields = ring_rows(several, block_below, block_above)

    def padded(first, last):
        def ends(line):
            line = line[first:last]
            return jnp.concatenate([line[:, -1:], line[:, : CLAT + 1]], axis=1)[:, None]

        middle = jnp.concatenate(
            [line_left[first:last, :, None], single[first:last], line_right[first:last, :, None]], axis=2
        )
        return jnp.concatenate([ends(line_above), middle, ends(line_below)], axis=1)

    levels = velocity.shape[0]
    feat_pad = padded(0, CIN).astype(jnp.bfloat16)
    vel_pad = padded(CIN, CIN + levels)
    cot_pad = padded(CIN + levels, CIN + 2 * levels)

    w, force, z, row, sums = kernel_call(
        lambda *refs: solve_first(packed, *refs),
        [(ROWS, LANES), (ROWS, LANES), (CLON, CLAT), (1, 128), (1, 128)],
        place[None],
        gathered,
        band,
        band_below,
        band_above,
        fields,
        smem=1,
    )

    columns = patches_of(feat_pad)
    hidden = jnp.tanh(jnp.dot(conv_weight, columns, preferred_element_type=f32) + conv_bias[:, None])
    logits = jnp.sum(out_weight[:, None] * hidden, axis=0).reshape(CLON, CLAT)
    viscosity = jax.nn.softplus(logits)

    to = jnp.arange(n_lat)[:, None]
    first_col = jnp.pad(viscosity[:, 0], (0, 128 - CLON))[None]
    last_col = jnp.pad(viscosity[:, -1], (0, 128 - CLON))[None]
    edge = jnp.where(to == lat + 1, last_col, 0.0) + jnp.where(to == lat - 1, first_col, 0.0)
    sent = jnp.stack([jnp.broadcast_to(row, (n_lat, 128)), edge], axis=1)
    got = across_lat(sent)
    row = jnp.sum(got[:, 0], axis=0)
    visc_left = jnp.sum(jnp.where(to == lat - 1, got[:, 1], 0.0), axis=0)[:CLON, None]
    visc_right = jnp.sum(jnp.where(to == lat + 1, got[:, 1], 0.0), axis=0)[:CLON, None]
    to = jnp.arange(n_lon)[:, None]
    after, before = to == (lon + 1) % n_lon, to == (lon + n_lon - 1) % n_lon
    edge = jnp.where(after, viscosity[-1:], 0.0) + jnp.where(before, viscosity[:1], 0.0)
    sent = jnp.stack([jnp.broadcast_to(row[None], (n_lon, 128)), edge], axis=1)
    got = exchange(sent, LON)
    gathered = got[:, 0]
    visc_above = jnp.sum(jnp.where(before, got[:, 1], 0.0), axis=0)[None]
    visc_below = jnp.sum(jnp.where(after, got[:, 1], 0.0), axis=0)[None]

    def rim(line):
        return jnp.pad(line, ((0, 0), (0, LANES - CLAT)))

    visc = ring_rows(ring_lanes(viscosity, visc_right, visc_left), rim(visc_below), rim(visc_above))
    visc_pad = jnp.concatenate([visc[-1:], visc[: CLON + 1]], axis=0)
    visc_pad = jnp.concatenate([visc_pad[:, -1:], visc_pad[:, : CLAT + 1]], axis=1)

    lane = jnp.arange(LANES)[None]
    valid = jnp.where(lane < CLAT, 1.0, jnp.where(lane < CLAT + LANES // 4, lat < n_lat - 1, lat > 0).astype(f32))

    level = level_weight[:, None, None]
    base = jnp.zeros_like(velocity_cot)
    first = jnp.zeros_like(viscosity)
    slopes = []
    for visc_side, vel_side, cot_side in zip(neighbours(visc_pad), neighbours(vel_pad), neighbours(cot_pad)):
        change = cot_side - velocity_cot
        slope = vel_side - velocity
        base = base + 0.5 * (viscosity + visc_side)[None] * change
        first = first + jnp.sum(slope * change, axis=0)
        slopes.append(jnp.sum(level * slope, axis=0))
    base = velocity_cot + time_step * base
    cells_all = CLON * CLAT * n_lon * n_lat
    weight = jax.nn.sigmoid(logits) * (-0.5 * time_step / math.sqrt(cells_all))

    grads, spreads, sums = kernel_call(
        lambda *refs: solve_second(packed, *refs),
        [(3, CLON, CLAT), (2, CLON, CLAT), (1, 128)],
        gathered,
        band,
        band_below,
        band_above,
        fields,
        w,
        force,
        visc,
        valid,
        weight,
        jnp.stack(slopes),
        first,
        sums,
    )

    lines = grads.reshape(3, 1, CLON * CLAT)
    out_grad = jnp.sum(hidden[None] * lines, axis=2)
    pre = lines * (out_weight[:, None] * (1.0 - hidden * hidden))[None]
    bias_grad = jnp.sum(pre, axis=2)
    rounded = lax.reduce_precision(pre, 8, 7)
    high = rounded.astype(jnp.bfloat16)
    low = (pre - rounded).astype(jnp.bfloat16)

    def against(part):
        return lax.dot_general(
            part.reshape(3 * HID, -1), columns, (((1,), (1,)), ((), ())), preferred_element_type=f32
        )

    weight_grad = (against(high) + against(low)).reshape(3, HID, TAPS)
    table = jnp.concatenate([weight_grad, bias_grad[..., None], out_grad[..., None]], axis=2)
    width = table.shape[2]

    n_plane, n_column = lax.axis_size(PLANE), lax.axis_size(COLUMN)
    each = HID // n_plane
    sent = table.reshape(3, n_plane, each, width).transpose(1, 0, 2, 3).reshape(n_plane, 3 * each, width)
    sent = jnp.pad(sent, ((0, 0), (0, 0), (0, 384 - width)))
    extra = jnp.broadcast_to(jnp.pad(sums, ((0, 0), (0, 256)))[None], (n_plane, 1, 384))
    sent = jnp.concatenate([sent, extra], axis=1)
    sent = jnp.pad(sent, ((0, 0), (0, -sent.shape[1] % 8), (0, 0)))
    part = jnp.sum(exchange(sent, PLANE), axis=0)
    whole = jnp.sum(exchange(jnp.broadcast_to(part[None], (n_column,) + part.shape), COLUMN), axis=0)

    e0, d0, cross, ww, g = (whole[3 * each, k] for k in range(5))
    step0 = e0 / d0
    e1 = e0 - step0 * d0 - step0 * cross + step0 * step0 * ww
    beta = e1 / e0
    lead = 1.0 + beta
    pw = lead * lead * d0 - 2.0 * lead * step0 * ww + step0 * step0 * g
    step1 = e1 / pw
    on_z = step0 + step1 * lead
    on_y = -step1 * step0

    mine = whole[:each] + on_z * whole[each : 2 * each] + on_y * whole[2 * each : 3 * each]
    final = exchange(jnp.broadcast_to(mine[None], (n_plane,) + mine.shape), PLANE).reshape(HID, 384)
    grad_velocity = base + level * (on_z * spreads[0] + on_y * spreads[1])[None]
    return (grad_velocity, final[:, :TAPS], final[:, TAPS], final[:, TAPS + 1])


def solution(mesh):
    n_lon, n_lat = mesh.shape["lon"], mesh.shape["lat"]
    y = min(8, n_lon // 2)
    shape = (n_lon // y, y, n_lat // 2, 2)
    grid = Mesh(np.asarray(mesh.devices).reshape(shape), LON + LAT)
    tile = P(None, LON, LAT)
    flat = P(LON, LAT)
    in_specs = (tile, tile, tile, flat, flat, flat, flat, P(LON + LAT, None), P(), P(), P(), P())
    out_specs = (tile, P(), P(), P())
    return jax.shard_map(shards, mesh=grid, in_specs=in_specs, out_specs=out_specs, check_vma=False)
```

time: 1580 us -> 206 us (0.13)
  blocking collectives: 1010 us -> 16.3 us
  waiting for transfers between devices: 350 us -> 72.4 us
  starting transfers between devices: 169 us -> 76 us
    psum x6 -> x0, blocking collectives: 706 us -> none  [total(): return lax.psum(lax.psum(values, 'lat'), 'lon')]
    psum x2 -> x0, waiting for transfers between devices: 323 us -> none  [total(): return lax.psum(lax.psum(values, 'lat'), 'lon')]
    unnamed x2 -> x0, blocking collectives: 308 us -> none
    ppermute x20 -> x4, starting transfers between devices: 169 us -> 31.5 us  [the longest x1 12.9 us: shards(): lax.ppermute(side_tiles(single[:, :, 0], several[:, :, :HALO]), LAT, back...]
    all_to_all x0 -> x6, waiting for transfers between devices: none -> 72.4 us  [exchange(): return lax.all_to_all(values, axes, 0, 0, tiled=True)]
    all_to_all x0 -> x6, starting transfers between devices: none -> 44.5 us  [exchange(): return lax.all_to_all(values, axes, 0, 0, tiled=True)]
    ppermute x20 -> x4, waiting for transfers between devices: 27.4 us -> 0.01 us  [the longest x1 0.01 us: shards(): lax.ppermute(side_tiles(single[:, :, -1], several[:, :, -HALO:]), LAT, fo...]
    all_to_all x0 -> x1, blocking collectives: none -> 16.3 us  [exchange(): return lax.all_to_all(values, axes, 0, 0, tiled=True)]
  transfers between devices with their start and end apart: 22 -> 10, of which waited for: 11 -> 6; matrix products, arithmetic and copies ran while one was open for 0% -> 2% of each run, Pallas kernels for 0% -> 0%
where the time goes in v1:
time: 206 us; the launch traced here: 205 us
  starting transfers between devices  76 us (37%)
  waiting for transfers between devices  72.4 us (35%)
  local copies, waits for them, and re-layouts  17.1 us (8%)
  blocking collectives  16.3 us (8%)
  other arithmetic  10.9 us (5%)
  between operations  8.24 us (4%)
  matrix products  2.84 us (1%)
    all_to_all x6, waiting for transfers between devices, exchange(): return lax.all_to_all(values, axes, 0, 0, tiled=True)  72.4 us
    all_to_all x6, starting transfers between devices, exchange(): return lax.all_to_all(values, axes, 0, 0, tiled=True)  44.5 us
    all_to_all x1, blocking collectives, exchange(): return lax.all_to_all(values, axes, 0, 0, tiled=True)  16.3 us
    ppermute x1, starting transfers between devices, shards(): lax.ppermute(side_tiles(single[:, :, 0], several[:, :, :HALO]), LAT, back...  12.9 us
    ppermute x1, starting transfers between devices, shards(): below = lax.ppermute(end_tiles(0, several[:, :HALO]), LON, backward)  12.2 us
    ppermute x1, starting transfers between devices, shards(): lax.ppermute(side_tiles(single[:, :, -1], several[:, :, -HALO:]), LAT, fo...  4.51 us
    unnamed x48, local copies, waits for them, and re-layouts  4.39 us
  transfers between devices with their start and end apart: 10, of which 6 were waited for; matrix products, arithmetic and copies ran while one was open for 2% of the time, Pallas kernels for 0%

profile of v1, /device:TPU:1, one launch (start us, length us, event | category | flops | bytes accessed | tf_op | source)
XLA Modules:
  0.0 205.2 jit_solution(11270238421043449624)
XLA Ops:
  2.4 0.9 convert_element_type.67
  3.3 0.9 pad_maximum_fusion.4
  5.7 4.5 %collective-permute-start = (f32[65,8,128]{2,1,0:T(8,128)S(1)}, f32[65,8,128]{2,1,0:T(8,128)S(1)}, u32[]{:S(2)}, u32[]{:S(2)}) collective-permute-start(f32[65,8,128]{2,1,0:T(8,128)S(1)} %get-tuple-element.73), channel_id=1, source_target_pairs={{0,1},{1,2},{2,3},{3,4},{4,5},{5,6},{6,7},{8,9},{9,10},{10,11},{11... | collective-permute-start | bytes 798728 | tf_op jit(solution)/shard_map/ppermute | solution.py:240
  10.2 12.9 %collective-permute-start.1 = (f32[65,8,128]{2,1,0:T(8,128)S(1)}, f32[65,8,128]{2,1,0:T(8,128)S(1)}, u32[]{:S(2)}, u32[]{:S(2)}) collective-permute-start(f32[65,8,128]{2,1,0:T(8,128)S(1)} %get-tuple-element.72), channel_id=1, source_target_pairs={{1,0},{2,1},{3,2},{4,3},{5,4},{6,5},{7,6},{9,8},{10,9},{11,10},{12... | collective-permute-start | bytes 798728 | tf_op jit(solution)/shard_map/ppermute | solution.py:241
  24.0 3.3 %all-to-all-start = ((f32[8,1,128]{2,1,0:T(1,128)}), f32[8,1,128]{2,1,0:T(1,128)S(1)}, u32[]{:S(2)}, u32[]{:S(2)}) async-start(f32[8,1,128]{2,1,0:T(1,128)} %broadcast_in_dim.283), calls=%async_computation | async-start | bytes 8192 | tf_op jit(solution)/shard_map/all_to_all | solution.py:31
  27.3 3.8 %all-to-all-done = f32[8,1,128]{2,1,0:T(1,128)S(1)} async-done(((f32[8,1,128]{2,1,0:T(1,128)}), f32[8,1,128]{2,1,0:T(1,128)S(1)}, u32[]{:S(2)}, u32[]{:S(2)}) %all-to-all-start) | async-done | bytes 4128 | tf_op jit(solution)/shard_map/all_to_all | solution.py:31
  32.2 1.3 pad_maximum_fusion.2
  33.5 1.9 collective-permute-start.2
  35.4 12.2 %collective-permute-start.3 = (f32[208,8,128]{2,1,0:T(8,128)}, f32[208,8,128]{2,1,0:T(8,128)}, u32[]{:S(2)}, u32[]{:S(2)}) collective-permute-start(f32[208,8,128]{2,1,0:T(8,128)} %get-tuple-element.60), channel_id=1, source_target_pairs={{8,0},{16,8},{24,16},{32,24},{40,32},{48,40},{56,48},{64,56},{72,6... | collective-permute-start | bytes 2555912 | tf_op jit(solution)/shard_map/ppermute | solution.py:269
  48.5 9.7 %all-to-all-start.1 = ((f32[128,1,128]{2,1,0:T(1,128)}), f32[128,1,128]{2,1,0:T(1,128)S(1)}, u32[]{:S(2)}, u32[]{:S(2)}) async-start(f32[128,1,128]{2,1,0:T(1,128)} %broadcast_in_dim.285), calls=%async_computation.1 | async-start | bytes 131072 | tf_op jit(solution)/shard_map/all_to_all | solution.py:31
  59.7 13.5 %all-to-all-done.1 = f32[128,1,128]{2,1,0:T(1,128)S(1)} async-done(((f32[128,1,128]{2,1,0:T(1,128)}), f32[128,1,128]{2,1,0:T(1,128)S(1)}, u32[]{:S(2)}, u32[]{:S(2)}) %all-to-all-start.1) | async-done | bytes 65568 | tf_op jit(solution)/shard_map/all_to_all | solution.py:31
  73.2 0.9 copy-done.5
  75.0 1.3 slice.416.refs_3_.refs_2_
  78.8 1.5 subtract_multiply_fusion
  81.4 0.9 shard_map.147
  82.9 5.9 %all-to-all-start.2 = ((f32[8,2,128]{2,1,0:T(2,128)}), f32[8,2,128]{2,1,0:T(2,128)S(1)}, u32[]{:S(2)}, u32[]{:S(2)}) async-start(f32[8,2,128]{2,1,0:T(2,128)} %pad_maximum_fusion.56), calls=%async_computation.2 | async-start | bytes 16384 | tf_op jit(solution)/shard_map/all_to_all | solution.py:31
  89.6 3.9 %all-to-all-done.2 = f32[8,2,128]{2,1,0:T(2,128)S(1)} async-done(((f32[8,2,128]{2,1,0:T(2,128)}), f32[8,2,128]{2,1,0:T(2,128)S(1)}, u32[]{:S(2)}, u32[]{:S(2)}) %all-to-all-start.2) | async-done | bytes 8224 | tf_op jit(solution)/shard_map/all_to_all | solution.py:31
  94.3 12.3 %all-to-all-start.3 = ((f32[128,2,128]{2,1,0:T(2,128)}), f32[128,2,128]{2,1,0:T(2,128)S(1)}, u32[]{:S(2)}, u32[]{:S(2)}) async-start(f32[128,2,128]{2,1,0:T(2,128)} %pad_maximum_fusion.11), calls=%async_computation.3 | async-start | bytes 262144 | tf_op jit(solution)/shard_map/all_to_all | solution.py:31
  106.8 15.0 %all-to-all-done.3 = f32[128,2,128]{2,1,0:T(2,128)S(1)} async-done(((f32[128,2,128]{2,1,0:T(2,128)}), f32[128,2,128]{2,1,0:T(2,128)S(1)}, u32[]{:S(2)}, u32[]{:S(2)}) %all-to-all-start.3) | async-done | bytes 131104 | tf_op jit(solution)/shard_map/all_to_all | solution.py:31
  128.7 16.3 %all_to_all.35 = f32[32,8,384]{2,1,0:T(8,128)S(1)} all-to-all(f32[32,8,384]{2,1,0:T(8,128)S(1)} %pad.50.clone), channel_id=1, replica_groups=mesh['z'=16,'y'=8,'x'=4,'c'=2] {'y','x'}, dimensions={0} | all-to-all | bytes 786432 | tf_op jit(solution)/shard_map/all_to_all | solution.py:31
  145.7 9.6 %all-to-all-start.5 = ((f32[32,8,384]{2,1,0:T(8,128)}), f32[32,8,384]{2,1,0:T(8,128)S(1)}, u32[]{:S(2)}, u32[]{:S(2)}) async-start(f32[32,8,384]{2,1,0:T(8,128)} %broadcast_in_dim.327), calls=%async_computation.5 | async-start | bytes 786432 | tf_op jit(solution)/shard_map/all_to_all | solution.py:31
  155.4 27.9 %all-to-all-done.5 = f32[32,8,384]{2,1,0:T(8,128)S(1)} async-done(((f32[32,8,384]{2,1,0:T(8,128)}), f32[32,8,384]{2,1,0:T(8,128)S(1)}, u32[]{:S(2)}, u32[]{:S(2)}) %all-to-all-start.5) | async-done | bytes 393248 | tf_op jit(solution)/shard_map/all_to_all | solution.py:31
  191.4 3.9 %all-to-all-start.6 = ((f32[32,2,384]{2,1,0:T(2,128)}), f32[32,2,384]{2,1,0:T(2,128)S(1)}, u32[]{:S(2)}, u32[]{:S(2)}) async-start(f32[32,2,384]{2,1,0:T(2,128)} %broadcast_in_dim.328), calls=%async_computation.6 | async-start | bytes 196608 | tf_op jit(solution)/shard_map/all_to_all | solution.py:31
  196.1 8.3 %all-to-all-done.6 = f32[32,2,384]{2,1,0:T(2,128)S(1)} async-done(((f32[32,2,384]{2,1,0:T(2,128)}), f32[32,2,384]{2,1,0:T(2,128)S(1)}, u32[]{:S(2)}, u32[]{:S(2)}) %all-to-all-start.6) | async-done | bytes 98336 | tf_op jit(solution)/shard_map/all_to_all | solution.py:31
  (212 shorter events, 24.6 us)
Async XLA Ops:
  0.6 78.2 %copy-start = (bf16[64,288]{1,0:T(8,128)(2,1)S(1)}, bf16[64,288]{1,0:T(8,128)(2,1)}, u32[]{:S(2)}) copy-start(bf16[64,288]{1,0:T(8,128)(2,1)} %param.20) | copy-start | bytes 110596
  4.2 1.4 copy-start.2
  4.4 18.7 %copy-start.10 = (f32[16,128]{1,0:T(8,128)S(1)}, f32[16,128]{1,0:T(8,128)}, u32[]{:S(2)}) copy-start(f32[16,128]{1,0:T(8,128)} %param.15) | copy-start | bytes 24580
  4.4 18.7 %copy-start.12 = (s32[16,128]{1,0:T(8,128)S(1)}, s32[16,128]{1,0:T(8,128)}, u32[]{:S(2)}) copy-start(s32[16,128]{1,0:T(8,128)} %param.18) | copy-start | bytes 24580
  4.4 22.8 %copy-start.3 = (f32[8,16,128]{2,1,0:T(8,128)S(1)}, f32[8,16,128]{2,1,0:T(8,128)}, u32[]{:S(2)}) copy-start(f32[8,16,128]{2,1,0:T(8,128)} %param.14) | copy-start | bytes 196612
  4.4 22.8 %copy-start.4 = (f32[8,16,128]{2,1,0:T(8,128)S(1)}, f32[8,16,128]{2,1,0:T(8,128)}, u32[]{:S(2)}) copy-start(f32[8,16,128]{2,1,0:T(8,128)} %param.13) | copy-start | bytes 196612
  5.6 26.0 %copy-start.11 = (f32[16,128]{1,0:T(8,128)S(1)}, f32[16,128]{1,0:T(8,128)}, u32[]{:S(2)}) copy-start(f32[16,128]{1,0:T(8,128)} %param.16) | copy-start | bytes 24580
  5.7 25.4 %collective-permute-start = (f32[65,8,128]{2,1,0:T(8,128)S(1)}, f32[65,8,128]{2,1,0:T(8,128)S(1)}, u32[]{:S(2)}, u32[]{:S(2)}) collective-permute-start(f32[65,8,128]{2,1,0:T(8,128)S(1)} %get-tuple-element.73), channel_id=1, source_target_pairs={{0,1},{1,2},{2,3},{3,4},{4,5},{5,6},{6,7},{8,9},{9,10},{10,11},{11... | collective-permute-start | bytes 798728 | tf_op jit(solution)/shard_map/ppermute | solution.py:240
  10.2 20.9 %collective-permute-start.1 = (f32[65,8,128]{2,1,0:T(8,128)S(1)}, f32[65,8,128]{2,1,0:T(8,128)S(1)}, u32[]{:S(2)}, u32[]{:S(2)}) collective-permute-start(f32[65,8,128]{2,1,0:T(8,128)S(1)} %get-tuple-element.72), channel_id=1, source_target_pairs={{1,0},{2,1},{3,2},{4,3},{5,4},{6,5},{7,6},{9,8},{10,9},{11,10},{12... | collective-permute-start | bytes 798728 | tf_op jit(solution)/shard_map/ppermute | solution.py:241
  24.0 7.1 %all-to-all-start = ((f32[8,1,128]{2,1,0:T(1,128)}), f32[8,1,128]{2,1,0:T(1,128)S(1)}, u32[]{:S(2)}, u32[]{:S(2)}) async-start(f32[8,1,128]{2,1,0:T(1,128)} %broadcast_in_dim.283), calls=%async_computation | async-start | bytes 8192 | tf_op jit(solution)/shard_map/all_to_all | solution.py:31
  33.5 39.8 %collective-permute-start.2 = (f32[208,8,128]{2,1,0:T(8,128)}, f32[208,8,128]{2,1,0:T(8,128)S(1)}, u32[]{:S(2)}, u32[]{:S(2)}) collective-permute-start(f32[208,8,128]{2,1,0:T(8,128)} %get-tuple-element.61), channel_id=1, source_target_pairs={{0,8},{8,16},{16,24},{24,32},{32,40},{40,48},{48,56},{56,64},{64,7... | collective-permute-start | bytes 2555912 | tf_op jit(solution)/shard_map/ppermute | solution.py:268
  35.4 37.9 %collective-permute-start.3 = (f32[208,8,128]{2,1,0:T(8,128)}, f32[208,8,128]{2,1,0:T(8,128)}, u32[]{:S(2)}, u32[]{:S(2)}) collective-permute-start(f32[208,8,128]{2,1,0:T(8,128)} %get-tuple-element.60), channel_id=1, source_target_pairs={{8,0},{16,8},{24,16},{32,24},{40,32},{48,40},{56,48},{64,56},{72,6... | collective-permute-start | bytes 2555912 | tf_op jit(solution)/shard_map/ppermute | solution.py:269
  48.5 24.7 %all-to-all-start.1 = ((f32[128,1,128]{2,1,0:T(1,128)}), f32[128,1,128]{2,1,0:T(1,128)S(1)}, u32[]{:S(2)}, u32[]{:S(2)}) async-start(f32[128,1,128]{2,1,0:T(1,128)} %broadcast_in_dim.285), calls=%async_computation.1 | async-start | bytes 131072 | tf_op jit(solution)/shard_map/all_to_all | solution.py:31
  75.0 1.4 copy-start.6
  77.7 1.1 copy-start.16
  77.8 1.1 copy-start.17
  78.8 1.9 copy-start.13
  81.4 7.4 %copy-start.15 = (f32[8]{0:T(128)S(1)}, f32[8]{0:T(128)}, u32[]{:S(2)}) copy-start(f32[8]{0:T(128)} %param.23) | copy-start | bytes 100
  82.9 10.5 %all-to-all-start.2 = ((f32[8,2,128]{2,1,0:T(2,128)}), f32[8,2,128]{2,1,0:T(2,128)S(1)}, u32[]{:S(2)}, u32[]{:S(2)}) async-start(f32[8,2,128]{2,1,0:T(2,128)} %pad_maximum_fusion.56), calls=%async_computation.2 | async-start | bytes 16384 | tf_op jit(solution)/shard_map/all_to_all | solution.py:31
  94.3 27.6 %all-to-all-start.3 = ((f32[128,2,128]{2,1,0:T(2,128)}), f32[128,2,128]{2,1,0:T(2,128)S(1)}, u32[]{:S(2)}, u32[]{:S(2)}) async-start(f32[128,2,128]{2,1,0:T(2,128)} %pad_maximum_fusion.11), calls=%async_computation.3 | async-start | bytes 262144 | tf_op jit(solution)/shard_map/all_to_all | solution.py:31
  122.5 1.2 copy-start.8
  123.7 1.3 copy-start.14
  145.7 37.5 %all-to-all-start.5 = ((f32[32,8,384]{2,1,0:T(8,128)}), f32[32,8,384]{2,1,0:T(8,128)S(1)}, u32[]{:S(2)}, u32[]{:S(2)}) async-start(f32[32,8,384]{2,1,0:T(8,128)} %broadcast_in_dim.327), calls=%async_computation.5 | async-start | bytes 786432 | tf_op jit(solution)/shard_map/all_to_all | solution.py:31
  191.4 13.0 %all-to-all-start.6 = ((f32[32,2,384]{2,1,0:T(2,128)}), f32[32,2,384]{2,1,0:T(2,128)S(1)}, u32[]{:S(2)}, u32[]{:S(2)}) async-start(f32[32,2,384]{2,1,0:T(2,128)} %broadcast_in_dim.328), calls=%async_computation.6 | async-start | bytes 196608 | tf_op jit(solution)/shard_map/all_to_all | solution.py:31
  (4 other events, 3.6 us)

commit v2 on v1

--- a/solution.py
+++ b/solution.py
@@ -23,8 +23,9 @@
 LANES = 256
 LON = ("z", "y")
 LAT = ("x", "c")
-PLANE = ("y", "x")
-COLUMN = ("z", "c")
+LAYER = ("y", "x", "c")
+DEPTH = ("z",)
+SPARE = 34
 
 
 def exchange(values, axes):
@@ -103,16 +104,8 @@
     return jnp.sum(jnp.where(lane == first + row, sums, 0.0), axis=0, keepdims=True)
 
 
-def vector_of(ref, packed):
-    count = ref.shape[0] // packed
-    value = ref[pl.ds(0, count, stride=packed), :]
-    for t in range(1, packed):
-        value = value + ref[pl.ds(t, count, stride=packed), :]
-    return value
-
-
-def solve_first(packed, place, gathered, tiles_own, tiles_below, tiles_above, fields, w_ref, f_ref, z_ref, row_ref, sum_ref):
-    vector = vector_of(gathered, packed)
+def solve_first(place, gathered, tiles_own, tiles_below, tiles_above, fields, w_ref, f_ref, z_ref, row_ref, sum_ref):
+    vector = gathered[...]
     rhs, damp, wet, agg = (fields[k] for k in range(4))
     diagonal = 4.0 + damp
     middle = coarse_column(tiles_own, 3, vector)
@@ -132,10 +125,10 @@
 
 
 def solve_second(
-    packed, gathered, tiles_own, tiles_below, tiles_above, fields, w_ref, f_ref, visc_ref, valid_ref, weight_ref,
+    gathered, tiles_own, tiles_below, tiles_above, fields, w_ref, f_ref, visc_ref, valid_ref, weight_ref,
     slope_ref, first_ref, sum_in, grad_ref, spread_ref, sum_ref,
 ):
-    vector = vector_of(gathered, packed)
+    vector = gathered[...]
     rhs, damp, wet, agg = (fields[k] for k in range(4))
     diagonal = 4.0 + damp
     w = w_ref[...]
@@ -170,6 +163,30 @@
         grad_ref[at + 1] = slope * weight
 
 
+def finish(parts, spreads, mine_ref, spread_ref):
+    row = jnp.sum(parts[...], axis=0)
+    main, tail = 2 * 128, 6 * 128
+
+    def scalar(k):
+        at = tail + 3 * SPARE + k
+        return row[:1, at : at + 1]
+
+    e0, d0, cross, ww, g = (scalar(k) for k in range(5))
+    step0 = e0 / d0
+    e1 = e0 - step0 * d0 - step0 * cross + step0 * step0 * ww
+    beta = e1 / e0
+    lead = 1.0 + beta
+    pw = lead * lead * d0 - 2.0 * lead * step0 * ww + step0 * step0 * g
+    step1 = e1 / pw
+    on_z = step0 + step1 * lead
+    on_y = -step1 * step0
+    front = row[:, :main] + on_z * row[:, main : 2 * main] + on_y * row[:, 2 * main : 3 * main]
+    last = row[:, tail:]
+    back = last + on_z * roll(last, -SPARE, 1) + on_y * roll(last, -2 * SPARE, 1)
+    mine_ref[...] = jnp.concatenate([front, back], axis=1)
+    spread_ref[...] = on_z * spreads[0] + on_y * spreads[1]
+
+
 def neighbours(padded):
     return (padded[..., 2:, 1:-1], padded[..., :-2, 1:-1], padded[..., 1:-1, 2:], padded[..., 1:-1, :-2])
 
@@ -222,11 +239,14 @@
     f32 = jnp.float32
     n_lon, n_lat = lax.axis_size(LON), lax.axis_size(LAT)
     lon, lat = lax.axis_index(LON), lax.axis_index(LAT)
-    per = n_lat * AGG
-    packed = 128 // per
-    place = (lat * AGG + (lon % packed) * per).astype(jnp.int32)
+    n_layer, n_depth = lax.axis_size(LAYER), lax.axis_size(DEPTH)
+    rank = lax.axis_index(LAYER)
+    slot = rank % 16
+    place = (slot * AGG).astype(jnp.int32)
+    spot = jnp.where(slot < 8, 64, 0)
 
     single = jnp.concatenate([features.astype(f32), velocity, velocity_cot], axis=0)
+    inner = features.astype(f32)
     several = jnp.stack([surface_cot, damping, wet_mask.astype(f32), aggregate_map.astype(f32)])
     n_single, n_several = single.shape[0], several.shape[0]
     coarse = tiles_of(coarse_inverse)
@@ -242,10 +262,15 @@
 
     local = restricted(surface_cot, aggregate_map.astype(f32), place)
 
-    def across_lat(rows):
-        return exchange(rows, LAT)
-
-    row = jnp.sum(across_lat(jnp.broadcast_to(local[None], (n_lat, 1, 128))), axis=0)
+    def merged(got):
+        lane_slot = jnp.arange(128)[None, None] // AGG
+        kept = jnp.where(lane_slot == jnp.arange(16)[None, :, None], got.reshape(-1, 16, 128), 0.0)
+        return jnp.sum(kept, axis=1)
+
+    def to_all(block, axes):
+        return exchange(jnp.broadcast_to(block[None], (lax.axis_size(axes),) + block.shape), axes)
+
+    row = merged(to_all(local, LAYER))
     row, left, right = lax.optimization_barrier((row, left, right))
 
     def unpack(tiles):
@@ -258,33 +283,39 @@
     band = jnp.concatenate([coarse_left, coarse, coarse_right], axis=0)
     several = ring_lanes(several, block_right, block_left)
 
-    def end_tiles(at, block):
+    def end_tiles(at, second, block):
         line = ring_lanes(single[:, at, :], line_right[:, at : at + 1], line_left[:, at : at + 1])
-        edge = jnp.concatenate([line, block.reshape(-1, LANES)], axis=0)
-        edge = jnp.pad(edge, ((0, 64 - edge.shape[0]), (0, 0)))
+        more = ring_lanes(
+            inner[:, second, :], line_right[:CIN, second : second + 1], line_left[:CIN, second : second + 1]
+        )
+        edge = jnp.concatenate([line, block.reshape(-1, LANES), more], axis=0)
+        edge = jnp.pad(edge, ((0, 96 - edge.shape[0]), (0, 0)))
         return jnp.concatenate([band, tiles_of(edge)], axis=0)
 
     forward, backward = shifted(single, LON, True)
-    above = lax.ppermute(end_tiles(CLON - 1, several[:, -HALO:]), LON, forward)
-    below = lax.ppermute(end_tiles(0, several[:, :HALO]), LON, backward)
-    gathered = exchange(jnp.broadcast_to(row[None], (n_lon, 1, 128)), LON).reshape(n_lon, 128)
+    above = lax.ppermute(end_tiles(CLON - 1, CLON - 2, several[:, -HALO:]), LON, forward)
+    below = lax.ppermute(end_tiles(0, 1, several[:, :HALO]), LON, backward)
+    gathered = to_all(row, DEPTH).reshape(-1, 128)
     gathered, above, below = lax.optimization_barrier((gathered, above, below))
 
     count = band.shape[0]
 
     def unpack_rows(tiles):
-        edge = rows_of(tiles[count:], 64)
-        block = edge[n_single : n_single + n_several * HALO].reshape(n_several, HALO, LANES)
-        return tiles[:count], edge[:n_single], block
-
-    band_above, line_above, block_above = unpack_rows(above)
-    band_below, line_below, block_below = unpack_rows(below)
+        edge = rows_of(tiles[count:], 96)
+        last = n_single + n_several * HALO
+        block = edge[n_single:last].reshape(n_several, HALO, LANES)
+        return tiles[:count], edge[:n_single], block, edge[last : last + CIN]
+
+    band_above, line_above, block_above, more_above = unpack_rows(above)
+    band_below, line_below, block_below, more_below = unpack_rows(below)
     fields = ring_rows(several, block_below, block_above)
+
+    def unringed(line):
+        return jnp.concatenate([line[:, -1:], line[:, : CLAT + 1]], axis=1)[:, None]
 
     def padded(first, last):
         def ends(line):
-            line = line[first:last]
-            return jnp.concatenate([line[:, -1:], line[:, : CLAT + 1]], axis=1)[:, None]
+            return unringed(line[first:last])
 
         middle = jnp.concatenate(
             [line_left[first:last, :, None], single[first:last], line_right[first:last, :, None]], axis=2
@@ -292,12 +323,12 @@
         return jnp.concatenate([ends(line_above), middle, ends(line_below)], axis=1)
 
     levels = velocity.shape[0]
-    feat_pad = padded(0, CIN).astype(jnp.bfloat16)
+    feat_pad = jnp.concatenate([unringed(more_above), padded(0, CIN), unringed(more_below)], axis=1).astype(jnp.bfloat16)
     vel_pad = padded(CIN, CIN + levels)
     cot_pad = padded(CIN + levels, CIN + 2 * levels)
 
     w, force, z, row, sums = kernel_call(
-        lambda *refs: solve_first(packed, *refs),
+        solve_first,
         [(ROWS, LANES), (ROWS, LANES), (CLON, CLAT), (1, 128), (1, 128)],
         place[None],
         gathered,
@@ -308,28 +339,31 @@
         smem=1,
     )
 
-    columns = patches_of(feat_pad)
-    hidden = jnp.tanh(jnp.dot(conv_weight, columns, preferred_element_type=f32) + conv_bias[:, None])
-    logits = jnp.sum(out_weight[:, None] * hidden, axis=0).reshape(CLON, CLAT)
-    viscosity = jax.nn.softplus(logits)
-
-    to = jnp.arange(n_lat)[:, None]
-    first_col = jnp.pad(viscosity[:, 0], (0, 128 - CLON))[None]
-    last_col = jnp.pad(viscosity[:, -1], (0, 128 - CLON))[None]
-    edge = jnp.where(to == lat + 1, last_col, 0.0) + jnp.where(to == lat - 1, first_col, 0.0)
-    sent = jnp.stack([jnp.broadcast_to(row, (n_lat, 128)), edge], axis=1)
-    got = across_lat(sent)
-    row = jnp.sum(got[:, 0], axis=0)
-    visc_left = jnp.sum(jnp.where(to == lat - 1, got[:, 1], 0.0), axis=0)[:CLON, None]
-    visc_right = jnp.sum(jnp.where(to == lat + 1, got[:, 1], 0.0), axis=0)[:CLON, None]
-    to = jnp.arange(n_lon)[:, None]
-    after, before = to == (lon + 1) % n_lon, to == (lon + n_lon - 1) % n_lon
-    edge = jnp.where(after, viscosity[-1:], 0.0) + jnp.where(before, viscosity[:1], 0.0)
-    sent = jnp.stack([jnp.broadcast_to(row[None], (n_lon, 128)), edge], axis=1)
-    got = exchange(sent, LON)
-    gathered = got[:, 0]
-    visc_above = jnp.sum(jnp.where(before, got[:, 1], 0.0), axis=0)[None]
-    visc_below = jnp.sum(jnp.where(after, got[:, 1], 0.0), axis=0)[None]
+    around = patches_of(feat_pad)
+    hidden = jnp.tanh(jnp.dot(conv_weight, around, preferred_element_type=f32) + conv_bias[:, None])
+    logits = jnp.sum(out_weight[:, None] * hidden, axis=0).reshape(CLON + 2, CLAT)
+    visc_rows = jax.nn.softplus(logits)
+    logits, viscosity = logits[1:-1], visc_rows[1:-1]
+    columns, hidden = around[:, CLAT:-CLAT], hidden[:, CLAT:-CLAT]
+
+    to = jnp.arange(n_layer)[:, None]
+    before, after = (to == rank - 1) & (lat > 0), (to == rank + 1) & (lat < n_lat - 1)
+
+    def at_spot(line):
+        line = jnp.pad(line, (0, 64 - CLON))
+        blank = jnp.zeros_like(line)
+        return jnp.where(spot > 0, jnp.concatenate([blank, line]), jnp.concatenate([line, blank]))[None]
+
+    edge = jnp.where(after, at_spot(viscosity[:, -1]), 0.0) + jnp.where(before, at_spot(viscosity[:, 0]), 0.0)
+    got = exchange((row + edge)[:, None], LAYER)
+
+    def from_spot(mask):
+        line = jnp.sum(jnp.where(mask, got[:, 0], 0.0), axis=0)
+        return jnp.where(spot > 0, line[64 : 64 + CLON], line[:CLON])[:, None]
+
+    visc_left, visc_right = from_spot(before), from_spot(after)
+    gathered = to_all(merged(got), DEPTH).reshape(-1, 128)
+    visc_above, visc_below = visc_rows[:1], visc_rows[-1:]
 
     def rim(line):
         return jnp.pad(line, ((0, 0), (0, LANES - CLAT)))
@@ -356,7 +390,7 @@
     weight = jax.nn.sigmoid(logits) * (-0.5 * time_step / math.sqrt(cells_all))
 
     grads, spreads, sums = kernel_call(
-        lambda *refs: solve_second(packed, *refs),
+        solve_second,
         [(3, CLON, CLAT), (2, CLON, CLAT), (1, 128)],
         gathered,
         band,
@@ -387,32 +421,18 @@
         )
 
     weight_grad = (against(high) + against(low)).reshape(3, HID, TAPS)
-    table = jnp.concatenate([weight_grad, bias_grad[..., None], out_grad[..., None]], axis=2)
-    width = table.shape[2]
-
-    n_plane, n_column = lax.axis_size(PLANE), lax.axis_size(COLUMN)
-    each = HID // n_plane
-    sent = table.reshape(3, n_plane, each, width).transpose(1, 0, 2, 3).reshape(n_plane, 3 * each, width)
-    sent = jnp.pad(sent, ((0, 0), (0, 0), (0, 384 - width)))
-    extra = jnp.broadcast_to(jnp.pad(sums, ((0, 0), (0, 256)))[None], (n_plane, 1, 384))
-    sent = jnp.concatenate([sent, extra], axis=1)
-    sent = jnp.pad(sent, ((0, 0), (0, -sent.shape[1] % 8), (0, 0)))
-    part = jnp.sum(exchange(sent, PLANE), axis=0)
-    whole = jnp.sum(exchange(jnp.broadcast_to(part[None], (n_column,) + part.shape), COLUMN), axis=0)
-
-    e0, d0, cross, ww, g = (whole[3 * each, k] for k in range(5))
-    step0 = e0 / d0
-    e1 = e0 - step0 * d0 - step0 * cross + step0 * step0 * ww
-    beta = e1 / e0
-    lead = 1.0 + beta
-    pw = lead * lead * d0 - 2.0 * lead * step0 * ww + step0 * step0 * g
-    step1 = e1 / pw
-    on_z = step0 + step1 * lead
-    on_y = -step1 * step0
-
-    mine = whole[:each] + on_z * whole[each : 2 * each] + on_y * whole[2 * each : 3 * each]
-    final = exchange(jnp.broadcast_to(mine[None], (n_plane,) + mine.shape), PLANE).reshape(HID, 384)
-    grad_velocity = base + level * (on_z * spreads[0] + on_y * spreads[1])[None]
+    rest = jnp.concatenate([weight_grad[..., 256:], bias_grad[..., None], out_grad[..., None]], axis=2)
+    table = jnp.concatenate(
+        [weight_grad[k, :, :256] for k in range(3)]
+        + [rest[k] for k in range(3)]
+        + [jnp.broadcast_to(sums[:, : 128 - 3 * SPARE], (HID, 128 - 3 * SPARE))],
+        axis=1,
+    )
+    each = HID // n_layer
+    part = jnp.sum(exchange(table.reshape(n_layer, each, table.shape[1]), LAYER), axis=0)
+    mine, spread = kernel_call(finish, [(each, 384), (CLON, CLAT)], to_all(part, DEPTH), spreads)
+    final = to_all(mine, LAYER).reshape(HID, 384)
+    grad_velocity = base + level * spread[None]
     return (grad_velocity, final[:, :TAPS], final[:, TAPS], final[:, TAPS + 1])
 
 

time: 206 us -> 189 us (0.917)
  blocking collectives: 16.3 us -> 0 us
  waiting for transfers between devices: 72.4 us -> 59.9 us
  local copies, waits for them, and re-layouts: 17.1 us -> 27.5 us
  between operations: 8.24 us -> 1.76 us
  other arithmetic: 10.9 us -> 16.6 us
  starting transfers between devices: 76 us -> 78.9 us
    all_to_all x6 -> x7, waiting for transfers between devices: 72.4 us -> 55.1 us  [exchange(): return lax.all_to_all(values, axes, 0, 0, tiled=True)]
    all_to_all x1 -> x0, blocking collectives: 16.3 us -> none  [exchange(): return lax.all_to_all(values, axes, 0, 0, tiled=True)]
    all_to_all x6 -> x7, starting transfers between devices: 44.5 us -> 57.8 us  [exchange(): return lax.all_to_all(values, axes, 0, 0, tiled=True)]
    ppermute x1, starting transfers between devices: 12.9 us -> 1.92 us  [shards(): lax.ppermute(side_tiles(single[:, :, 0], several[:, :, :HALO]), LAT, back...]
    ppermute x1, waiting for transfers between devices: 0.01 us -> 4.4 us  [shards(): lax.ppermute(side_tiles(single[:, :, 0], several[:, :, :HALO]), LAT, back...]
    broadcast_in_dim x15 -> x19, local copies, waits for them, and re-layouts: 2.97 us -> 6.16 us  [the longest x5 3.21 us: to_all(): jnp.broadcast_to(block[None], (lax.axis_size(axes),) + block.shape)]
    pad x2, local copies, waits for them, and re-layouts: 0.01 us -> 2.34 us  [rim(): return jnp.pad(line, ((0, 0), (0, LANES - CLAT)))]
    slice x18 -> x25, local copies, waits for them, and re-layouts: 3.58 us -> 5.18 us  [the longest x2 1.24 us: unpack_rows(): return (tiles[:count], edge[:n_single], block, edge[last:last + CIN])]
  transfers between devices with their start and end apart: 10 -> 11, of which waited for: 6 -> 8; matrix products, arithmetic and copies ran while one was open for 2% -> 11% of each run, Pallas kernels for 0% -> 0%
where the time goes in v2:
time: 189 us; the launch traced here: 188 us
  starting transfers between devices  78.9 us (42%)
  waiting for transfers between devices  59.9 us (32%)
  local copies, waits for them, and re-layouts  27.5 us (15%)
  other arithmetic  16.6 us (9%)
    all_to_all x7, starting transfers between devices, exchange(): return lax.all_to_all(values, axes, 0, 0, tiled=True)  57.8 us
    all_to_all x7, waiting for transfers between devices, exchange(): return lax.all_to_all(values, axes, 0, 0, tiled=True)  55.1 us
    ppermute x1, starting transfers between devices, shards(): below = lax.ppermute(end_tiles(0, 1, several[:, :HALO]), LON, backward)  12.5 us
    unnamed x97, local copies, waits for them, and re-layouts  4.43 us
    ppermute x1, waiting for transfers between devices, shards(): lax.ppermute(side_tiles(single[:, :, 0], several[:, :, :HALO]), LAT, back...  4.4 us
  transfers between devices with their start and end apart: 11, of which 8 were waited for; matrix products, arithmetic and copies ran while one was open for 11% of the time, Pallas kernels for 0%

profile of v2, /device:TPU:1, one launch (start us, length us, event | category | flops | bytes accessed | tf_op | source)
XLA Modules:
  0.0 188.0 jit_solution(12642038861625762839)
XLA Ops:
  2.3 18.2 %all-to-all-start = ((f32[64,1,128]{2,1,0:T(1,128)}), f32[64,1,128]{2,1,0:T(1,128)S(1)}, u32[]{:S(2)}, u32[]{:S(2)}) async-start(f32[64,1,128]{2,1,0:T(1,128)} %broadcast_in_dim.269), calls=%async_computation | async-start | bytes 65536 | tf_op jit(solution)/shard_map/all_to_all | solution.py:32
  25.5 3.5 %collective-permute-start = (f32[65,8,128]{2,1,0:T(8,128)S(1)}, f32[65,8,128]{2,1,0:T(8,128)S(1)}, u32[]{:S(2)}, u32[]{:S(2)}) collective-permute-start(f32[65,8,128]{2,1,0:T(8,128)S(1)} %get-tuple-element.80), channel_id=1, source_target_pairs={{0,1},{1,2},{2,3},{3,4},{4,5},{5,6},{6,7},{8,9},{9,10},{10,11},{11... | collective-permute-start | bytes 798728 | tf_op jit(solution)/shard_map/ppermute | solution.py:260
  29.1 1.9 %collective-permute-start.1 = (f32[65,8,128]{2,1,0:T(8,128)S(1)}, f32[65,8,128]{2,1,0:T(8,128)S(1)}, u32[]{:S(2)}, u32[]{:S(2)}) collective-permute-start(f32[65,8,128]{2,1,0:T(8,128)S(1)} %get-tuple-element.79), channel_id=1, source_target_pairs={{1,0},{2,1},{3,2},{4,3},{5,4},{6,5},{7,6},{9,8},{10,9},{11,10},{12... | collective-permute-start | bytes 798728 | tf_op jit(solution)/shard_map/ppermute | solution.py:261
  32.4 4.4 %collective-permute-done.1 = f32[65,8,128]{2,1,0:T(8,128)S(1)} collective-permute-done((f32[65,8,128]{2,1,0:T(8,128)S(1)}, f32[65,8,128]{2,1,0:T(8,128)S(1)}, u32[]{:S(2)}, u32[]{:S(2)}) %collective-permute-start.1) | collective-permute-done | bytes 266272 | tf_op jit(solution)/shard_map/ppermute | solution.py:261
  38.7 1.3 pad_maximum_fusion.2
  40.0 3.1 %collective-permute-start.2 = (f32[216,8,128]{2,1,0:T(8,128)}, f32[216,8,128]{2,1,0:T(8,128)S(1)}, u32[]{:S(2)}, u32[]{:S(2)}) collective-permute-start(f32[216,8,128]{2,1,0:T(8,128)} %get-tuple-element.65), channel_id=1, source_target_pairs={{0,8},{8,16},{16,24},{24,32},{32,40},{40,48},{48,56},{56,64},{64,7... | collective-permute-start | bytes 2654216 | tf_op jit(solution)/shard_map/ppermute | solution.py:296
  43.1 12.5 %collective-permute-start.3 = (f32[216,8,128]{2,1,0:T(8,128)}, f32[216,8,128]{2,1,0:T(8,128)}, u32[]{:S(2)}, u32[]{:S(2)}) collective-permute-start(f32[216,8,128]{2,1,0:T(8,128)} %get-tuple-element.64), channel_id=1, source_target_pairs={{8,0},{16,8},{24,16},{32,24},{40,32},{48,40},{56,48},{64,56},{72,6... | collective-permute-start | bytes 2654216 | tf_op jit(solution)/shard_map/ppermute | solution.py:297
  58.1 4.9 %all-to-all-start.1 = ((f32[16,4,128]{2,1,0:T(4,128)}), f32[16,4,128]{2,1,0:T(4,128)S(1)}, u32[]{:S(2)}, u32[]{:S(2)}) async-start(f32[16,4,128]{2,1,0:T(4,128)} %broadcast_in_dim.271), calls=%async_computation.1 | async-start | bytes 65536 | tf_op jit(solution)/shard_map/all_to_all | solution.py:32
  67.7 6.8 %all-to-all-done.1 = f32[16,4,128]{2,1,0:T(4,128)S(1)} async-done(((f32[16,4,128]{2,1,0:T(4,128)}), f32[16,4,128]{2,1,0:T(4,128)S(1)}, u32[]{:S(2)}, u32[]{:S(2)}) %all-to-all-start.1) | async-done | bytes 32800 | tf_op jit(solution)/shard_map/all_to_all | solution.py:32
  75.4 1.2 slice.473.tiles_below
  87.2 8.7 %all-to-all-start.2 = ((f32[64,1,128]{2,1,0:T(1,128)}), f32[64,1,128]{2,1,0:T(1,128)S(1)}, u32[]{:S(2)}, u32[]{:S(2)}) async-start(f32[64,1,128]{2,1,0:T(1,128)} %fusion.24), calls=%async_computation.2 | async-start | bytes 65536 | tf_op jit(solution)/shard_map/all_to_all | solution.py:32
  95.9 1.2 pad.38
  97.1 1.1 pad.39
  98.2 1.7 fusion.48
  99.9 1.1 fusion.18
  101.3 3.9 %all-to-all-done.2 = f32[64,1,128]{2,1,0:T(1,128)S(1)} async-done(((f32[64,1,128]{2,1,0:T(1,128)}), f32[64,1,128]{2,1,0:T(1,128)S(1)}, u32[]{:S(2)}, u32[]{:S(2)}) %all-to-all-start.2) | async-done | bytes 32800 | tf_op jit(solution)/shard_map/all_to_all | solution.py:32
  107.7 8.8 %all-to-all-start.3 = ((f32[16,4,128]{2,1,0:T(4,128)}), f32[16,4,128]{2,1,0:T(4,128)S(1)}, u32[]{:S(2)}, u32[]{:S(2)}) async-start(f32[16,4,128]{2,1,0:T(4,128)} %broadcast_in_dim.296), calls=%async_computation.3 | async-start | bytes 65536 | tf_op jit(solution)/shard_map/all_to_all | solution.py:32
  117.3 10.7 %all-to-all-done.3 = f32[16,4,128]{2,1,0:T(4,128)S(1)} async-done(((f32[16,4,128]{2,1,0:T(4,128)}), f32[16,4,128]{2,1,0:T(4,128)S(1)}, u32[]{:S(2)}, u32[]{:S(2)}) %all-to-all-start.3) | async-done | bytes 32800 | tf_op jit(solution)/shard_map/all_to_all | solution.py:32
  133.4 7.7 %all-to-all-start.4 = ((f32[64,1,896]{2,1,0:T(1,128)}), f32[64,1,896]{2,1,0:T(1,128)S(1)}, u32[]{:S(2)}, u32[]{:S(2)}) async-start(f32[64,1,896]{2,1,0:T(1,128)} %reshape.418), calls=%async_computation.4 | async-start | bytes 458752 | tf_op jit(solution)/shard_map/all_to_all | solution.py:32
  141.5 12.3 %all-to-all-done.4 = f32[64,1,896]{2,1,0:T(1,128)S(1)} async-done(((f32[64,1,896]{2,1,0:T(1,128)}), f32[64,1,896]{2,1,0:T(1,128)S(1)}, u32[]{:S(2)}, u32[]{:S(2)}) %all-to-all-start.4) | async-done | bytes 229408 | tf_op jit(solution)/shard_map/all_to_all | solution.py:32
  154.6 3.5 %all-to-all-start.5 = ((f32[16,1,896]{2,1,0:T(1,128)}), f32[16,1,896]{2,1,0:T(1,128)S(1)}, u32[]{:S(2)}, u32[]{:S(2)}) async-start(f32[16,1,896]{2,1,0:T(1,128)} %broadcast_in_dim.309), calls=%async_computation.5 | async-start | bytes 114688 | tf_op jit(solution)/shard_map/all_to_all | solution.py:32
  158.2 11.5 %all-to-all-done.5.parts = f32[16,1,896]{2,1,0:T(1,128)S(1)} async-done(((f32[16,1,896]{2,1,0:T(1,128)}), f32[16,1,896]{2,1,0:T(1,128)S(1)}, u32[]{:S(2)}, u32[]{:S(2)}) %all-to-all-start.5) | async-done | bytes 57376 | tf_op jit(solution)/shard_map/all_to_all | solution.py:32
  170.6 5.9 %all-to-all-start.6 = ((f32[64,1,384]{2,1,0:T(1,128)}), f32[64,1,384]{2,1,0:T(1,128)S(1)}, u32[]{:S(2)}, u32[]{:S(2)}) async-start(f32[64,1,384]{2,1,0:T(1,128)} %broadcast_in_dim.311), calls=%async_computation.6 | async-start | bytes 196608 | tf_op jit(solution)/shard_map/all_to_all | solution.py:32
  177.4 9.9 %all-to-all-done.6 = f32[64,1,384]{2,1,0:T(1,128)S(1)} async-done(((f32[64,1,384]{2,1,0:T(1,128)}), f32[64,1,384]{2,1,0:T(1,128)S(1)}, u32[]{:S(2)}, u32[]{:S(2)}) %all-to-all-start.6) | async-done | bytes 98336 | tf_op jit(solution)/shard_map/all_to_all | solution.py:32
  (271 shorter events, 40.1 us)
Async XLA Ops:
  0.6 79.3 %copy-start = (bf16[64,288]{1,0:T(8,128)(2,1)S(1)}, bf16[64,288]{1,0:T(8,128)(2,1)}, u32[]{:S(2)}) copy-start(bf16[64,288]{1,0:T(8,128)(2,1)} %param.20) | copy-start | bytes 110596
  2.3 29.7 %all-to-all-start = ((f32[64,1,128]{2,1,0:T(1,128)}), f32[64,1,128]{2,1,0:T(1,128)S(1)}, u32[]{:S(2)}, u32[]{:S(2)}) async-start(f32[64,1,128]{2,1,0:T(1,128)} %broadcast_in_dim.269), calls=%async_computation | async-start | bytes 65536 | tf_op jit(solution)/shard_map/all_to_all | solution.py:32
  25.5 6.9 %collective-permute-start = (f32[65,8,128]{2,1,0:T(8,128)S(1)}, f32[65,8,128]{2,1,0:T(8,128)S(1)}, u32[]{:S(2)}, u32[]{:S(2)}) collective-permute-start(f32[65,8,128]{2,1,0:T(8,128)S(1)} %get-tuple-element.80), channel_id=1, source_target_pairs={{0,1},{1,2},{2,3},{3,4},{4,5},{5,6},{6,7},{8,9},{9,10},{10,11},{11... | collective-permute-start | bytes 798728 | tf_op jit(solution)/shard_map/ppermute | solution.py:260
  29.1 7.7 %collective-permute-start.1 = (f32[65,8,128]{2,1,0:T(8,128)S(1)}, f32[65,8,128]{2,1,0:T(8,128)S(1)}, u32[]{:S(2)}, u32[]{:S(2)}) collective-permute-start(f32[65,8,128]{2,1,0:T(8,128)S(1)} %get-tuple-element.79), channel_id=1, source_target_pairs={{1,0},{2,1},{3,2},{4,3},{5,4},{6,5},{7,6},{9,8},{10,9},{11,10},{12... | collective-permute-start | bytes 798728 | tf_op jit(solution)/shard_map/ppermute | solution.py:261
  40.0 34.5 %collective-permute-start.2 = (f32[216,8,128]{2,1,0:T(8,128)}, f32[216,8,128]{2,1,0:T(8,128)S(1)}, u32[]{:S(2)}, u32[]{:S(2)}) collective-permute-start(f32[216,8,128]{2,1,0:T(8,128)} %get-tuple-element.65), channel_id=1, source_target_pairs={{0,8},{8,16},{16,24},{24,32},{32,40},{40,48},{48,56},{56,64},{64,7... | collective-permute-start | bytes 2654216 | tf_op jit(solution)/shard_map/ppermute | solution.py:296
  43.1 31.4 %collective-permute-start.3 = (f32[216,8,128]{2,1,0:T(8,128)}, f32[216,8,128]{2,1,0:T(8,128)}, u32[]{:S(2)}, u32[]{:S(2)}) collective-permute-start(f32[216,8,128]{2,1,0:T(8,128)} %get-tuple-element.64), channel_id=1, source_target_pairs={{8,0},{16,8},{24,16},{32,24},{40,32},{48,40},{56,48},{64,56},{72,6... | collective-permute-start | bytes 2654216 | tf_op jit(solution)/shard_map/ppermute | solution.py:297
  57.5 28.8 %copy-start.36 = (pred[64]{0:T(512)(128)(4,1)}, pred[64]{0:T(512)(128)(4,1)S(1)}, u32[]{:S(2)}) copy-start(pred[64]{0:T(512)(128)(4,1)S(1)} %get-tuple-element.117) | copy-start | bytes 196
  58.1 16.4 %all-to-all-start.1 = ((f32[16,4,128]{2,1,0:T(4,128)}), f32[16,4,128]{2,1,0:T(4,128)S(1)}, u32[]{:S(2)}, u32[]{:S(2)}) async-start(f32[16,4,128]{2,1,0:T(4,128)} %broadcast_in_dim.271), calls=%async_computation.1 | async-start | bytes 65536 | tf_op jit(solution)/shard_map/all_to_all | solution.py:32
  85.4 14.5 %copy-start.10 = (f32[8,16,1]{2,1,0:T(8,128)S(1)}, f32[8,16,1]{2,1,0:T(8,128)}, u32[]{:S(2)}) copy-start(f32[8,16,1]{2,1,0:T(8,128)} %broadcast_in_dim.317) | copy-start | bytes 1540
  85.5 15.6 %copy-start.9 = (f32[8,16,1]{2,1,0:T(8,128)S(1)}, f32[8,16,1]{2,1,0:T(8,128)}, u32[]{:S(2)}) copy-start(f32[8,16,1]{2,1,0:T(8,128)} %broadcast_in_dim.315) | copy-start | bytes 1540
  86.3 14.7 %copy-start.25 = (f32[8,1,130]{2,1,0:T(1,128)S(1)}, f32[8,1,130]{2,1,0:T(1,128)}, u32[]{:S(2)}) copy-start(f32[8,1,130]{2,1,0:T(1,128)} %copy.184) | copy-start | bytes 12484
  86.3 14.8 %copy-start.27 = (f32[8,1,130]{2,1,0:T(1,128)S(1)}, f32[8,1,130]{2,1,0:T(1,128)}, u32[]{:S(2)}) copy-start(f32[8,1,130]{2,1,0:T(1,128)} %copy.185) | copy-start | bytes 12484
  86.3 14.8 %copy-start.34 = (f32[8]{0:T(128)S(1)}, f32[8]{0:T(128)}, u32[]{:S(2)}) copy-start(f32[8]{0:T(128)} %param.23) | copy-start | bytes 100
  86.3 30.2 %copy-start.23 = (f32[16,128]{1,0:T(8,128)S(1)}, f32[16,128]{1,0:T(8,128)}, u32[]{:S(2)}) copy-start(f32[16,128]{1,0:T(8,128)} %slice.570) | copy-start | bytes 24580
  87.2 18.1 %all-to-all-start.2 = ((f32[64,1,128]{2,1,0:T(1,128)}), f32[64,1,128]{2,1,0:T(1,128)S(1)}, u32[]{:S(2)}, u32[]{:S(2)}) async-start(f32[64,1,128]{2,1,0:T(1,128)} %fusion.24), calls=%async_computation.2 | async-start | bytes 65536 | tf_op jit(solution)/shard_map/all_to_all | solution.py:32
  101.1 27.4 %copy-start.4 = (f32[64,2048]{1,0:T(8,128)S(1)}, f32[64,2048]{1,0:T(8,128)}, u32[]{:S(2)}) copy-start(f32[64,2048]{1,0:T(8,128)} %get-tuple-element.66) | copy-start | bytes 1572868
  107.7 20.3 %all-to-all-start.3 = ((f32[16,4,128]{2,1,0:T(4,128)}), f32[16,4,128]{2,1,0:T(4,128)S(1)}, u32[]{:S(2)}, u32[]{:S(2)}) async-start(f32[16,4,128]{2,1,0:T(4,128)} %broadcast_in_dim.296), calls=%async_computation.3 | async-start | bytes 65536 | tf_op jit(solution)/shard_map/all_to_all | solution.py:32
  132.0 26.0 %copy-start.21 = (f32[18,128]{1,0:T(8,128)S(1)}, f32[18,128]{1,0:T(8,128)}, u32[]{:S(2)}) copy-start(f32[18,128]{1,0:T(8,128)} %copy-done.20) | copy-start | bytes 27652
  132.1 44.5 %copy-start.26 = (f32[8,1,130]{2,1,0:T(1,128)S(1)}, f32[8,1,130]{2,1,0:T(1,128)}, u32[]{:S(2)}) copy-start(f32[8,1,130]{2,1,0:T(1,128)} %copy.184) | copy-start | bytes 12484
  132.1 44.5 %copy-start.28 = (f32[8,1,130]{2,1,0:T(1,128)S(1)}, f32[8,1,130]{2,1,0:T(1,128)}, u32[]{:S(2)}) copy-start(f32[8,1,130]{2,1,0:T(1,128)} %copy.185) | copy-start | bytes 12484
  132.1 44.5 %copy-start.35 = (f32[8]{0:T(128)S(1)}, f32[8]{0:T(128)}, u32[]{:S(2)}) copy-start(f32[8]{0:T(128)} %param.23) | copy-start | bytes 100
  133.4 20.3 %all-to-all-start.4 = ((f32[64,1,896]{2,1,0:T(1,128)}), f32[64,1,896]{2,1,0:T(1,128)S(1)}, u32[]{:S(2)}, u32[]{:S(2)}) async-start(f32[64,1,896]{2,1,0:T(1,128)} %reshape.418), calls=%async_computation.4 | async-start | bytes 458752 | tf_op jit(solution)/shard_map/all_to_all | solution.py:32
  154.6 15.1 %all-to-all-start.5 = ((f32[16,1,896]{2,1,0:T(1,128)}), f32[16,1,896]{2,1,0:T(1,128)S(1)}, u32[]{:S(2)}, u32[]{:S(2)}) async-start(f32[16,1,896]{2,1,0:T(1,128)} %broadcast_in_dim.309), calls=%async_computation.5 | async-start | bytes 114688 | tf_op jit(solution)/shard_map/all_to_all | solution.py:32
  170.6 16.6 %all-to-all-start.6 = ((f32[64,1,384]{2,1,0:T(1,128)}), f32[64,1,384]{2,1,0:T(1,128)S(1)}, u32[]{:S(2)}, u32[]{:S(2)}) async-start(f32[64,1,384]{2,1,0:T(1,128)} %broadcast_in_dim.311), calls=%async_computation.6 | async-start | bytes 196608 | tf_op jit(solution)/shard_map/all_to_all | solution.py:32
  (28 other events, 129.5 us)

commit v3 on v2

--- a/solution.py
+++ b/solution.py
@@ -64,14 +64,30 @@
     return (a + b) + (c + d)
 
 
-def coarse_column(tiles, groups, vector):
+def coarse_column(tiles, start, vector):
+    acc = tiles[start] * vector[0:1]
+    for k in range(1, vector.shape[0]):
+        acc = acc + tiles[start + k] * vector[k : k + 1]
+    return jnp.sum(acc, axis=1, keepdims=True)
+
+
+def coarse_columns(gathered, left, coarse, right, above, below):
+    vector = gathered[...]
     count = vector.shape[0]
+    middle = [coarse_column(tiles, 0, vector) for tiles in (left, coarse, right)]
+    outer = [[coarse_column(tiles, k * count, vector) for k in range(3)] for tiles in (above, below)]
+    return outer[0], middle, outer[1]
+
+
+def ring_fields(gathered, inner, above, below):
+    start = 3 * gathered.shape[0]
+    row = lax.broadcasted_iota(jnp.int32, (8, LANES), 0)
     out = []
-    for group in range(groups):
-        acc = tiles[group * count] * vector[0:1]
-        for k in range(1, count):
-            acc = acc + tiles[group * count + k] * vector[k : k + 1]
-        out.append(jnp.sum(acc, axis=1, keepdims=True))
+    for k in range(inner.shape[0]):
+        at = start + 2 * k
+        low = jnp.concatenate([below[at], below[at + 1]], axis=1)
+        high = jnp.concatenate([above[at], above[at + 1]], axis=1)
+        out.append(jnp.concatenate([inner[k], jnp.where(row < 4, low, high)], axis=0))
     return out
 
 
@@ -104,38 +120,31 @@
     return jnp.sum(jnp.where(lane == first + row, sums, 0.0), axis=0, keepdims=True)
 
 
-def solve_first(place, gathered, tiles_own, tiles_below, tiles_above, fields, w_ref, f_ref, z_ref, row_ref, sum_ref):
-    vector = gathered[...]
-    rhs, damp, wet, agg = (fields[k] for k in range(4))
+def solve_first(place, gathered, left, coarse, right, above, below, inner, valid_ref, w_ref, f_ref, row_ref, sum_ref):
+    rhs, damp, wet, agg = ring_fields(gathered, inner, above, below)
     diagonal = 4.0 + damp
-    middle = coarse_column(tiles_own, 3, vector)
-    below = coarse_column(tiles_below, 3, vector)
-    above = coarse_column(tiles_above, 3, vector)
-    z = rhs / diagonal + coarse_field(agg, above, middle, below)
+    columns = coarse_columns(gathered, left, coarse, right, above, below)
+    z = rhs / diagonal + coarse_field(agg, *columns)
     spread = side_sum(wet * z)
     w = diagonal * z - wet * spread
     w_ref[...] = w
-    f_ref[...] = spread - 4.0 * wet * z
+    f_ref[...] = (spread - 4.0 * wet * z) * valid_ref[...]
     own = (slice(0, CLON), slice(0, CLAT))
     z_own, w_own = z[own], w[own]
-    z_ref[...] = z_own
     row_ref[...] = restricted(w_own, agg[own], place[0])
     lane = lax.broadcasted_iota(jnp.int32, (1, 128), 1)
     sum_ref[...] = jnp.where(lane == 0, total(rhs[own] * z_own), 0.0) + jnp.where(lane == 1, total(z_own * w_own), 0.0)
 
 
 def solve_second(
-    gathered, tiles_own, tiles_below, tiles_above, fields, w_ref, f_ref, visc_ref, valid_ref, weight_ref,
-    slope_ref, first_ref, sum_in, grad_ref, spread_ref, sum_ref,
+    gathered, left, coarse, right, above, below, inner, valid_ref, w_ref, f_ref, weight_ref, slope_ref, first_ref,
+    sum_in, grad_ref, force_ref, sum_ref,
 ):
-    vector = gathered[...]
-    rhs, damp, wet, agg = (fields[k] for k in range(4))
+    rhs, damp, wet, agg = ring_fields(gathered, inner, above, below)
     diagonal = 4.0 + damp
     w = w_ref[...]
-    middle = coarse_column(tiles_own, 3, vector)
-    below = coarse_column(tiles_below, 3, vector)
-    above = coarse_column(tiles_above, 3, vector)
-    y = w / diagonal + coarse_field(agg, above, middle, below)
+    columns = coarse_columns(gathered, left, coarse, right, above, below)
+    y = w / diagonal + coarse_field(agg, *columns)
     around = side_sum(wet * y)
     image = diagonal * y - wet * around
     own = (slice(0, CLON), slice(0, CLAT))
@@ -145,25 +154,31 @@
     for at, value in ((2, rhs[own] * y_own), (3, w[own] * y_own), (4, y_own * image[own])):
         sums = sums + jnp.where(lane == at, total(value), 0.0)
     sum_ref[...] = sums
-    visc = visc_ref[...]
-    visc_own = visc[own]
-    visc_sides = [0.5 * (visc_own + side[own]) for side in sides(visc)]
-    valid = valid_ref[...]
     weight = weight_ref[...]
     grad_ref[0] = first_ref[...] * weight
-    for at, force in ((0, f_ref[...] * valid), (1, (around - 4.0 * wet * y) * valid)):
+    second = (around - 4.0 * wet * y) * valid_ref[...]
+    force_ref[...] = second
+    for at, force in ((1, f_ref[...]), (2, second)):
+        force_own = force[own]
+        slope = jnp.zeros((CLON, CLAT), jnp.float32)
+        for n, side in enumerate(sides(force)):
+            slope = slope + slope_ref[n] * (side[own] - force_own)
+        grad_ref[at] = slope * weight
+
+
+def diffuse(visc_ref, first, second, spread_ref):
+    own = (slice(0, CLON), slice(0, CLAT))
+    visc = visc_ref[...]
+    visc_sides = [0.5 * (visc[own] + side[own]) for side in sides(visc)]
+    for at, force in ((0, first[...]), (1, second[...])):
         force_own = force[own]
         bend = jnp.zeros((CLON, CLAT), jnp.float32)
-        slope = jnp.zeros((CLON, CLAT), jnp.float32)
-        for n, side in enumerate(sides(force)):
-            change = side[own] - force_own
-            bend = bend + visc_sides[n] * change
-            slope = slope + slope_ref[n] * change
+        for visc_side, side in zip(visc_sides, sides(force)):
+            bend = bend + visc_side * (side[own] - force_own)
         spread_ref[at] = force_own + time_step * bend
-        grad_ref[at + 1] = slope * weight
-
-
-def finish(parts, spreads, mine_ref, spread_ref):
+
+
+def finish(parts, mine_ref, on_ref):
     row = jnp.sum(parts[...], axis=0)
     main, tail = 2 * 128, 6 * 128
 
@@ -184,7 +199,8 @@
     last = row[:, tail:]
     back = last + on_z * roll(last, -SPARE, 1) + on_y * roll(last, -2 * SPARE, 1)
     mine_ref[...] = jnp.concatenate([front, back], axis=1)
-    spread_ref[...] = on_z * spreads[0] + on_y * spreads[1]
+    lane = lax.broadcasted_iota(jnp.int32, (1, 128), 1)
+    on_ref[...] = jnp.where(lane == 0, on_z, on_y)
 
 
 def neighbours(padded):
@@ -243,7 +259,6 @@
     rank = lax.axis_index(LAYER)
     slot = rank % 16
     place = (slot * AGG).astype(jnp.int32)
-    spot = jnp.where(slot < 8, 64, 0)
 
     single = jnp.concatenate([features.astype(f32), velocity, velocity_cot], axis=0)
     inner = features.astype(f32)
@@ -251,14 +266,15 @@
     n_single, n_several = single.shape[0], several.shape[0]
     coarse = tiles_of(coarse_inverse)
 
-    def side_tiles(line, block):
-        edge = jnp.concatenate([line, block.transpose(0, 2, 1).reshape(-1, CLON)], axis=0)
-        edge = jnp.pad(edge, ((0, 64 - edge.shape[0]), (0, 0))).reshape(1, 8, 128)
-        return jnp.concatenate([coarse, edge], axis=0)
+    whole_fields = several.reshape(-1, 8, 128)
+
+    def side_tiles(line):
+        edge = jnp.pad(line, ((0, 64 - line.shape[0]), (0, 0))).reshape(1, 8, 128)
+        return jnp.concatenate([coarse, whole_fields, edge], axis=0)
 
     forward, backward = shifted(single, LAT, False)
-    left = lax.ppermute(side_tiles(single[:, :, -1], several[:, :, -HALO:]), LAT, forward)
-    right = lax.ppermute(side_tiles(single[:, :, 0], several[:, :, :HALO]), LAT, backward)
+    left = lax.ppermute(side_tiles(single[:, :, -1]), LAT, forward)
+    right = lax.ppermute(side_tiles(single[:, :, 0]), LAT, backward)
 
     local = restricted(surface_cot, aggregate_map.astype(f32), place)
 
@@ -273,42 +289,36 @@
     row = merged(to_all(local, LAYER))
     row, left, right = lax.optimization_barrier((row, left, right))
 
-    def unpack(tiles):
-        edge = tiles[-1].reshape(64, CLON)
-        block = edge[n_single : n_single + n_several * HALO].reshape(n_several, HALO, CLON)
-        return tiles[:-1], edge[:n_single], block.transpose(0, 2, 1)
-
-    coarse_left, line_left, block_left = unpack(left)
-    coarse_right, line_right, block_right = unpack(right)
-    band = jnp.concatenate([coarse_left, coarse, coarse_right], axis=0)
-    several = ring_lanes(several, block_right, block_left)
+    count = coarse.shape[0]
+    line_left = left[-1].reshape(64, CLON)[:n_single]
+    line_right = right[-1].reshape(64, CLON)[:n_single]
+    lane = jnp.arange(CLAT)[None, None]
+    rest = jnp.where(lane < CLAT // 2, right[count:-1].reshape(several.shape), left[count:-1].reshape(several.shape))
+    several = jnp.concatenate([several, rest], axis=2)
+    band = jnp.concatenate([left[:count], coarse, right[:count]], axis=0)
 
     def end_tiles(at, second, block):
         line = ring_lanes(single[:, at, :], line_right[:, at : at + 1], line_left[:, at : at + 1])
         more = ring_lanes(
             inner[:, second, :], line_right[:CIN, second : second + 1], line_left[:CIN, second : second + 1]
         )
-        edge = jnp.concatenate([line, block.reshape(-1, LANES), more], axis=0)
-        edge = jnp.pad(edge, ((0, 96 - edge.shape[0]), (0, 0)))
+        edge = jnp.concatenate([block.reshape(-1, LANES), line, more], axis=0)
         return jnp.concatenate([band, tiles_of(edge)], axis=0)
 
     forward, backward = shifted(single, LON, True)
-    above = lax.ppermute(end_tiles(CLON - 1, CLON - 2, several[:, -HALO:]), LON, forward)
-    below = lax.ppermute(end_tiles(0, 1, several[:, :HALO]), LON, backward)
+    above = lax.ppermute(end_tiles(CLON - 1, CLON - 2, several[:, -8:]), LON, forward)
+    below = lax.ppermute(end_tiles(0, 1, several[:, :8]), LON, backward)
     gathered = to_all(row, DEPTH).reshape(-1, 128)
     gathered, above, below = lax.optimization_barrier((gathered, above, below))
 
-    count = band.shape[0]
-
     def unpack_rows(tiles):
-        edge = rows_of(tiles[count:], 96)
-        last = n_single + n_several * HALO
-        block = edge[n_single:last].reshape(n_several, HALO, LANES)
-        return tiles[:count], edge[:n_single], block, edge[last : last + CIN]
-
-    band_above, line_above, block_above, more_above = unpack_rows(above)
-    band_below, line_below, block_below, more_below = unpack_rows(below)
-    fields = ring_rows(several, block_below, block_above)
+        edge = rows_of(tiles[3 * count + 2 * n_several :], n_single + CIN)
+        return edge[:n_single], edge[n_single:]
+
+    line_above, more_above = unpack_rows(above)
+    line_below, more_below = unpack_rows(below)
+    lane = jnp.arange(LANES)[None]
+    valid = jnp.where(lane < CLAT, 1.0, jnp.where(lane < CLAT + LANES // 4, lat < n_lat - 1, lat > 0).astype(f32))
 
     def unringed(line):
         return jnp.concatenate([line[:, -1:], line[:, : CLAT + 1]], axis=1)[:, None]
@@ -327,17 +337,11 @@
     vel_pad = padded(CIN, CIN + levels)
     cot_pad = padded(CIN + levels, CIN + 2 * levels)
 
-    w, force, z, row, sums = kernel_call(
-        solve_first,
-        [(ROWS, LANES), (ROWS, LANES), (CLON, CLAT), (1, 128), (1, 128)],
-        place[None],
-        gathered,
-        band,
-        band_below,
-        band_above,
-        fields,
-        smem=1,
+    tiles = (left, coarse, right, above, below, several, valid)
+    w, force, row, sums = kernel_call(
+        solve_first, [(ROWS, LANES), (ROWS, LANES), (1, 128), (1, 128)], place[None], gathered, *tiles, smem=1
     )
+    gathered = to_all(merged(to_all(row, LAYER)), DEPTH).reshape(-1, 128)
 
     around = patches_of(feat_pad)
     hidden = jnp.tanh(jnp.dot(conv_weight, around, preferred_element_type=f32) + conv_bias[:, None])
@@ -346,61 +350,23 @@
     logits, viscosity = logits[1:-1], visc_rows[1:-1]
     columns, hidden = around[:, CLAT:-CLAT], hidden[:, CLAT:-CLAT]
 
-    to = jnp.arange(n_layer)[:, None]
-    before, after = (to == rank - 1) & (lat > 0), (to == rank + 1) & (lat < n_lat - 1)
-
-    def at_spot(line):
-        line = jnp.pad(line, (0, 64 - CLON))
-        blank = jnp.zeros_like(line)
-        return jnp.where(spot > 0, jnp.concatenate([blank, line]), jnp.concatenate([line, blank]))[None]
-
-    edge = jnp.where(after, at_spot(viscosity[:, -1]), 0.0) + jnp.where(before, at_spot(viscosity[:, 0]), 0.0)
-    got = exchange((row + edge)[:, None], LAYER)
-
-    def from_spot(mask):
-        line = jnp.sum(jnp.where(mask, got[:, 0], 0.0), axis=0)
-        return jnp.where(spot > 0, line[64 : 64 + CLON], line[:CLON])[:, None]
-
-    visc_left, visc_right = from_spot(before), from_spot(after)
-    gathered = to_all(merged(got), DEPTH).reshape(-1, 128)
-    visc_above, visc_below = visc_rows[:1], visc_rows[-1:]
-
-    def rim(line):
-        return jnp.pad(line, ((0, 0), (0, LANES - CLAT)))
-
-    visc = ring_rows(ring_lanes(viscosity, visc_right, visc_left), rim(visc_below), rim(visc_above))
-    visc_pad = jnp.concatenate([visc[-1:], visc[: CLON + 1]], axis=0)
-    visc_pad = jnp.concatenate([visc_pad[:, -1:], visc_pad[:, : CLAT + 1]], axis=1)
-
-    lane = jnp.arange(LANES)[None]
-    valid = jnp.where(lane < CLAT, 1.0, jnp.where(lane < CLAT + LANES // 4, lat < n_lat - 1, lat > 0).astype(f32))
-
     level = level_weight[:, None, None]
-    base = jnp.zeros_like(velocity_cot)
     first = jnp.zeros_like(viscosity)
     slopes = []
-    for visc_side, vel_side, cot_side in zip(neighbours(visc_pad), neighbours(vel_pad), neighbours(cot_pad)):
-        change = cot_side - velocity_cot
+    for vel_side, cot_side in zip(neighbours(vel_pad), neighbours(cot_pad)):
         slope = vel_side - velocity
-        base = base + 0.5 * (viscosity + visc_side)[None] * change
-        first = first + jnp.sum(slope * change, axis=0)
+        first = first + jnp.sum(slope * (cot_side - velocity_cot), axis=0)
         slopes.append(jnp.sum(level * slope, axis=0))
-    base = velocity_cot + time_step * base
     cells_all = CLON * CLAT * n_lon * n_lat
     weight = jax.nn.sigmoid(logits) * (-0.5 * time_step / math.sqrt(cells_all))
 
-    grads, spreads, sums = kernel_call(
+    grads, second, sums = kernel_call(
         solve_second,
-        [(3, CLON, CLAT), (2, CLON, CLAT), (1, 128)],
+        [(3, CLON, CLAT), (ROWS, LANES), (1, 128)],
         gathered,
-        band,
-        band_below,
-        band_above,
-        fields,
+        *tiles,
         w,
         force,
-        visc,
-        valid,
         weight,
         jnp.stack(slopes),
         first,
@@ -421,17 +387,40 @@
         )
 
     weight_grad = (against(high) + against(low)).reshape(3, HID, TAPS)
+    each = HID // n_layer
+    to = (jnp.arange(HID) // each)[:, None]
+    edge = jnp.where((to == rank - 1) & (lat > 0), viscosity[None, :, 0], 0.0)
+    edge = edge + jnp.where((to == rank + 1) & (lat < n_lat - 1), viscosity[None, :, -1], 0.0)
+    edge = jnp.pad(edge, ((0, 0), (0, 128 - 3 * SPARE - 5 - CLON)))
     rest = jnp.concatenate([weight_grad[..., 256:], bias_grad[..., None], out_grad[..., None]], axis=2)
     table = jnp.concatenate(
         [weight_grad[k, :, :256] for k in range(3)]
         + [rest[k] for k in range(3)]
-        + [jnp.broadcast_to(sums[:, : 128 - 3 * SPARE], (HID, 128 - 3 * SPARE))],
+        + [jnp.broadcast_to(sums[:, :5], (HID, 5)), edge],
         axis=1,
     )
-    each = HID // n_layer
-    part = jnp.sum(exchange(table.reshape(n_layer, each, table.shape[1]), LAYER), axis=0)
-    mine, spread = kernel_call(finish, [(each, 384), (CLON, CLAT)], to_all(part, DEPTH), spreads)
+    got = exchange(table.reshape(n_layer, each, table.shape[1]), LAYER)
+    part = jnp.sum(got, axis=0)
+    mine, on = kernel_call(finish, [(each, 384), (1, 128)], to_all(part, DEPTH))
+
+    to = jnp.arange(n_layer)[:, None]
+    lines = got[:, 0, 6 * 128 + 3 * SPARE + 5 :][:, :CLON]
+    visc_left = jnp.sum(jnp.where((to == rank - 1) & (lat > 0), lines, 0.0), axis=0)[:, None]
+    visc_right = jnp.sum(jnp.where((to == rank + 1) & (lat < n_lat - 1), lines, 0.0), axis=0)[:, None]
+
+    def rim(line):
+        return jnp.pad(line, ((0, 0), (0, LANES - CLAT)))
+
+    visc = ring_rows(ring_lanes(viscosity, visc_right, visc_left), rim(visc_rows[-1:]), rim(visc_rows[:1]))
+    visc_pad = jnp.concatenate([visc[-1:], visc[: CLON + 1]], axis=0)
+    visc_pad = jnp.concatenate([visc_pad[:, -1:], visc_pad[:, : CLAT + 1]], axis=1)
+    (spreads,) = kernel_call(diffuse, [(2, CLON, CLAT)], visc, force, second)
+    base = jnp.zeros_like(velocity_cot)
+    for visc_side, cot_side in zip(neighbours(visc_pad), neighbours(cot_pad)):
+        base = base + 0.5 * (viscosity + visc_side)[None] * (cot_side - velocity_cot)
+    base = velocity_cot + time_step * base
     final = to_all(mine, LAYER).reshape(HID, 384)
+    spread = on[:, :1] * spreads[0] + on[:, 1:2] * spreads[1]
     grad_velocity = base + level * spread[None]
     return (grad_velocity, final[:, :TAPS], final[:, TAPS], final[:, TAPS + 1])
 

time: 189 us -> 184 us (0.974)
  local copies, waits for them, and re-layouts: 27.5 us -> 19.6 us
  other arithmetic: 16.6 us -> 19.2 us
  starting transfers between devices: 78.9 us -> 81.3 us
    all_to_all x7, waiting for transfers between devices: 55.1 us -> 52.6 us  [exchange(): return lax.all_to_all(values, axes, 0, 0, tiled=True)]
    all_to_all x7, starting transfers between devices: 57.8 us -> 60.2 us  [exchange(): return lax.all_to_all(values, axes, 0, 0, tiled=True)]
    pad x2, local copies, waits for them, and re-layouts: 2.34 us -> 0.01 us  [rim(): return jnp.pad(line, ((0, 0), (0, LANES - CLAT)))]
    unnamed x97 -> x61, local copies, waits for them, and re-layouts: 4.43 us -> 3.2 us
    broadcast_in_dim x5 -> x6, local copies, waits for them, and re-layouts: 3.21 us -> 3.85 us  [to_all(): jnp.broadcast_to(block[None], (lax.axis_size(axes),) + block.shape)]
where the time goes in v3:
time: 184 us; the launch traced here: 183 us
  starting transfers between devices  81.3 us (44%)
  waiting for transfers between devices  58.6 us (32%)
  local copies, waits for them, and re-layouts  19.6 us (11%)
  other arithmetic  19.2 us (10%)
    all_to_all x7, starting transfers between devices, exchange(): return lax.all_to_all(values, axes, 0, 0, tiled=True)  60.2 us
    all_to_all x7, waiting for transfers between devices, exchange(): return lax.all_to_all(values, axes, 0, 0, tiled=True)  52.6 us
    ppermute x1, starting transfers between devices, shards(): below = lax.ppermute(end_tiles(0, 1, several[:, :8]), LON, backward)  12.5 us
    ppermute x1, waiting for transfers between devices, shards(): right = lax.ppermute(side_tiles(single[:, :, 0]), LAT, backward)  4.4 us
    broadcast_in_dim x6, local copies, waits for them, and re-layouts, to_all(): jnp.broadcast_to(block[None], (lax.axis_size(axes),) + block.shape)  3.85 us
  transfers between devices with their start and end apart: 11, of which 8 were waited for; matrix products, arithmetic and copies ran while one was open for 11% of the time, Pallas kernels for 0%

profile of v3, /device:TPU:1, one launch (start us, length us, event | category | flops | bytes accessed | tf_op | source)
XLA Modules:
  0.0 183.2 jit_solution(10898728774947778346)
XLA Ops:
  2.3 18.2 %all-to-all-start = ((f32[64,1,128]{2,1,0:T(1,128)}), f32[64,1,128]{2,1,0:T(1,128)S(1)}, u32[]{:S(2)}, u32[]{:S(2)}) async-start(f32[64,1,128]{2,1,0:T(1,128)} %broadcast_in_dim.276), calls=%async_computation | async-start | bytes 65536 | tf_op jit(solution)/shard_map/all_to_all | solution.py:32
  24.3 3.5 %collective-permute-start = (f32[73,8,128]{2,1,0:T(8,128)S(1)}, f32[73,8,128]{2,1,0:T(8,128)S(1)}, u32[]{:S(2)}, u32[]{:S(2)}) collective-permute-start(f32[73,8,128]{2,1,0:T(8,128)S(1)} %get-tuple-element.80), channel_id=1, source_target_pairs={{0,1},{1,2},{2,3},{3,4},{4,5},{5,6},{6,7},{8,9},{9,10},{10,11},{11... | collective-permute-start | bytes 897032 | tf_op jit(solution)/shard_map/ppermute | solution.py:276
  27.9 1.9 %collective-permute-start.1 = (f32[73,8,128]{2,1,0:T(8,128)S(1)}, f32[73,8,128]{2,1,0:T(8,128)S(1)}, u32[]{:S(2)}, u32[]{:S(2)}) collective-permute-start(f32[73,8,128]{2,1,0:T(8,128)S(1)} %get-tuple-element.79), channel_id=1, source_target_pairs={{1,0},{2,1},{3,2},{4,3},{5,4},{6,5},{7,6},{9,8},{10,9},{11,10},{12... | collective-permute-start | bytes 897032 | tf_op jit(solution)/shard_map/ppermute | solution.py:277
  30.0 1.6 collective-permute-done.left
  31.5 4.4 %collective-permute-done.1.right = f32[73,8,128]{2,1,0:T(8,128)S(1)} collective-permute-done((f32[73,8,128]{2,1,0:T(8,128)S(1)}, f32[73,8,128]{2,1,0:T(8,128)S(1)}, u32[]{:S(2)}, u32[]{:S(2)}) %collective-permute-start.1) | collective-permute-done | bytes 299040 | tf_op jit(solution)/shard_map/ppermute | solution.py:277
  36.7 1.4 pad_maximum_fusion.2
  38.0 3.1 %collective-permute-start.2 = (f32[220,8,128]{2,1,0:T(8,128)}, f32[220,8,128]{2,1,0:T(8,128)S(1)}, u32[]{:S(2)}, u32[]{:S(2)}) collective-permute-start(f32[220,8,128]{2,1,0:T(8,128)} %get-tuple-element.65), channel_id=1, source_target_pairs={{0,8},{8,16},{16,24},{24,32},{32,40},{40,48},{48,56},{56,64},{64,7... | collective-permute-start | bytes 2703368 | tf_op jit(solution)/shard_map/ppermute | solution.py:309
  41.2 12.5 %collective-permute-start.3 = (f32[220,8,128]{2,1,0:T(8,128)}, f32[220,8,128]{2,1,0:T(8,128)S(1)}, u32[]{:S(2)}, u32[]{:S(2)}) collective-permute-start(f32[220,8,128]{2,1,0:T(8,128)} %get-tuple-element.64), channel_id=1, source_target_pairs={{8,0},{16,8},{24,16},{32,24},{40,32},{48,40},{56,48},{64,56},{72,6... | collective-permute-start | bytes 2703368 | tf_op jit(solution)/shard_map/ppermute | solution.py:310
  54.9 4.9 %all-to-all-start.1 = ((f32[16,4,128]{2,1,0:T(4,128)}), f32[16,4,128]{2,1,0:T(4,128)S(1)}, u32[]{:S(2)}, u32[]{:S(2)}) async-start(f32[16,4,128]{2,1,0:T(4,128)} %broadcast_in_dim.278), calls=%async_computation.1 | async-start | bytes 65536 | tf_op jit(solution)/shard_map/all_to_all | solution.py:32
  63.8 7.6 %all-to-all-done.1 = f32[16,4,128]{2,1,0:T(4,128)S(1)} async-done(((f32[16,4,128]{2,1,0:T(4,128)}), f32[16,4,128]{2,1,0:T(4,128)S(1)}, u32[]{:S(2)}, u32[]{:S(2)}) %all-to-all-start.1) | async-done | bytes 32800 | tf_op jit(solution)/shard_map/all_to_all | solution.py:32
  79.6 8.9 %all-to-all-start.2 = ((f32[64,1,128]{2,1,0:T(1,128)}), f32[64,1,128]{2,1,0:T(1,128)}, u32[]{:S(2)}, u32[]{:S(2)}) async-start(f32[64,1,128]{2,1,0:T(1,128)} %broadcast_in_dim.292), calls=%async_computation.2 | async-start | bytes 65536 | tf_op jit(solution)/shard_map/all_to_all | solution.py:32
  88.5 1.7 fusion.48
  90.2 1.9 %fusion.22 = (f32[8,16,128]{2,1,0:T(8,128)S(1)}, f32[8,16,128]{2,1,0:T(8,128)S(1)}, f32[16,128]{1,0:T(8,128)}, f32[16,128]{1,0:T(8,128)S(1)}) fusion(f32[8,16,128]{2,1,0:T(8,128)} %param.13, f32[8,1,130]{2,1,0:T(1,128)} %copy.159, f32[8,16,1]{2,1,0:T(8,128)} %broadcast_in_dim.322, f32[8,16,1]{2,1,0:T(8,128)} %broadcast_in_dim.321, f32[8,1,130]{2,1,0:T(1,128)} %copy.160, ...), kind=kLoop, calls=%fused_computation.73 | loop fusion | flops 258048 | bytes 288416 | tf_op jit(solution)/shard_map/sub | solution.py:357
  92.0 1.8 multiply_reduce_fusion.4
  94.7 3.2 %all-to-all-done.2 = f32[64,1,128]{2,1,0:T(1,128)} async-done(((f32[64,1,128]{2,1,0:T(1,128)}), f32[64,1,128]{2,1,0:T(1,128)}, u32[]{:S(2)}, u32[]{:S(2)}) %all-to-all-start.2) | async-done | bytes 32800 | tf_op jit(solution)/shard_map/all_to_all | solution.py:32
  99.3 10.3 %all-to-all-start.3 = ((f32[16,4,128]{2,1,0:T(4,128)}), f32[16,4,128]{2,1,0:T(4,128)S(1)}, u32[]{:S(2)}, u32[]{:S(2)}) async-start(f32[16,4,128]{2,1,0:T(4,128)} %broadcast_in_dim.293), calls=%async_computation.3 | async-start | bytes 65536 | tf_op jit(solution)/shard_map/all_to_all | solution.py:32
  111.7 9.4 %all-to-all-done.3 = f32[16,4,128]{2,1,0:T(4,128)S(1)} async-done(((f32[16,4,128]{2,1,0:T(4,128)}), f32[16,4,128]{2,1,0:T(4,128)S(1)}, u32[]{:S(2)}, u32[]{:S(2)}) %all-to-all-start.3) | async-done | bytes 32800 | tf_op jit(solution)/shard_map/all_to_all | solution.py:32
  126.6 8.5 %all-to-all-start.4 = ((f32[64,1,896]{2,1,0:T(1,128)}), f32[64,1,896]{2,1,0:T(1,128)S(1)}, u32[]{:S(2)}, u32[]{:S(2)}) async-start(f32[64,1,896]{2,1,0:T(1,128)} %reshape.317), calls=%async_computation.4 | async-start | bytes 458752 | tf_op jit(solution)/shard_map/all_to_all | solution.py:32
  135.2 12.4 %all-to-all-done.4 = f32[64,1,896]{2,1,0:T(1,128)S(1)} async-done(((f32[64,1,896]{2,1,0:T(1,128)}), f32[64,1,896]{2,1,0:T(1,128)S(1)}, u32[]{:S(2)}, u32[]{:S(2)}) %all-to-all-start.4) | async-done | bytes 229408 | tf_op jit(solution)/shard_map/all_to_all | solution.py:32
  149.2 3.5 %all-to-all-start.5 = ((f32[16,1,896]{2,1,0:T(1,128)}), f32[16,1,896]{2,1,0:T(1,128)S(1)}, u32[]{:S(2)}, u32[]{:S(2)}) async-start(f32[16,1,896]{2,1,0:T(1,128)} %broadcast_in_dim.315), calls=%async_computation.5 | async-start | bytes 114688 | tf_op jit(solution)/shard_map/all_to_all | solution.py:32
  152.9 11.4 %all-to-all-done.5.parts = f32[16,1,896]{2,1,0:T(1,128)S(1)} async-done(((f32[16,1,896]{2,1,0:T(1,128)}), f32[16,1,896]{2,1,0:T(1,128)S(1)}, u32[]{:S(2)}, u32[]{:S(2)}) %all-to-all-start.5) | async-done | bytes 57376 | tf_op jit(solution)/shard_map/all_to_all | solution.py:32
  165.8 5.9 %all-to-all-start.6 = ((f32[64,1,384]{2,1,0:T(1,128)}), f32[64,1,384]{2,1,0:T(1,128)S(1)}, u32[]{:S(2)}, u32[]{:S(2)}) async-start(f32[64,1,384]{2,1,0:T(1,128)} %broadcast_in_dim.318), calls=%async_computation.6 | async-start | bytes 196608 | tf_op jit(solution)/shard_map/all_to_all | solution.py:32
  171.7 1.3 fusion.34
  173.9 8.6 %all-to-all-done.6 = f32[64,1,384]{2,1,0:T(1,128)S(1)} async-done(((f32[64,1,384]{2,1,0:T(1,128)}), f32[64,1,384]{2,1,0:T(1,128)S(1)}, u32[]{:S(2)}, u32[]{:S(2)}) %all-to-all-start.6) | async-done | bytes 98336 | tf_op jit(solution)/shard_map/all_to_all | solution.py:32
  (204 shorter events, 33.8 us)
Async XLA Ops:
  0.6 73.9 %copy-start = (bf16[64,288]{1,0:T(8,128)(2,1)S(1)}, bf16[64,288]{1,0:T(8,128)(2,1)}, u32[]{:S(2)}) copy-start(bf16[64,288]{1,0:T(8,128)(2,1)} %param.20) | copy-start | bytes 110596
  2.3 27.6 %all-to-all-start = ((f32[64,1,128]{2,1,0:T(1,128)}), f32[64,1,128]{2,1,0:T(1,128)S(1)}, u32[]{:S(2)}, u32[]{:S(2)}) async-start(f32[64,1,128]{2,1,0:T(1,128)} %broadcast_in_dim.276), calls=%async_computation | async-start | bytes 65536 | tf_op jit(solution)/shard_map/all_to_all | solution.py:32
  23.1 6.7 %copy-start.6 = (f32[8,16,128]{2,1,0:T(8,128)S(1)}, f32[8,16,128]{2,1,0:T(8,128)}, u32[]{:S(2)}) copy-start(f32[8,16,128]{2,1,0:T(8,128)} %param.14) | copy-start | bytes 196612
  24.3 7.2 %collective-permute-start = (f32[73,8,128]{2,1,0:T(8,128)S(1)}, f32[73,8,128]{2,1,0:T(8,128)S(1)}, u32[]{:S(2)}, u32[]{:S(2)}) collective-permute-start(f32[73,8,128]{2,1,0:T(8,128)S(1)} %get-tuple-element.80), channel_id=1, source_target_pairs={{0,1},{1,2},{2,3},{3,4},{4,5},{5,6},{6,7},{8,9},{9,10},{10,11},{11... | collective-permute-start | bytes 897032 | tf_op jit(solution)/shard_map/ppermute | solution.py:276
  27.9 8.1 %collective-permute-start.1 = (f32[73,8,128]{2,1,0:T(8,128)S(1)}, f32[73,8,128]{2,1,0:T(8,128)S(1)}, u32[]{:S(2)}, u32[]{:S(2)}) collective-permute-start(f32[73,8,128]{2,1,0:T(8,128)S(1)} %get-tuple-element.79), channel_id=1, source_target_pairs={{1,0},{2,1},{3,2},{4,3},{5,4},{6,5},{7,6},{9,8},{10,9},{11,10},{12... | collective-permute-start | bytes 897032 | tf_op jit(solution)/shard_map/ppermute | solution.py:277
  29.9 8.1 %copy-start.18 = (pred[16,128]{1,0:T(8,128)(4,1)}, pred[16,128]{1,0:T(8,128)(4,1)S(1)}, u32[]{:S(2)}) copy-start(pred[16,128]{1,0:T(8,128)(4,1)S(1)} %iota_compare_fusion) | copy-start | bytes 6148
  38.0 33.4 %collective-permute-start.2 = (f32[220,8,128]{2,1,0:T(8,128)}, f32[220,8,128]{2,1,0:T(8,128)S(1)}, u32[]{:S(2)}, u32[]{:S(2)}) collective-permute-start(f32[220,8,128]{2,1,0:T(8,128)} %get-tuple-element.65), channel_id=1, source_target_pairs={{0,8},{8,16},{16,24},{24,32},{32,40},{40,48},{48,56},{56,64},{64,7... | collective-permute-start | bytes 2703368 | tf_op jit(solution)/shard_map/ppermute | solution.py:309
  41.2 30.3 %collective-permute-start.3 = (f32[220,8,128]{2,1,0:T(8,128)}, f32[220,8,128]{2,1,0:T(8,128)S(1)}, u32[]{:S(2)}, u32[]{:S(2)}) collective-permute-start(f32[220,8,128]{2,1,0:T(8,128)} %get-tuple-element.64), channel_id=1, source_target_pairs={{8,0},{16,8},{24,16},{32,24},{40,32},{48,40},{56,48},{64,56},{72,6... | collective-permute-start | bytes 2703368 | tf_op jit(solution)/shard_map/ppermute | solution.py:310
  54.9 16.5 %all-to-all-start.1 = ((f32[16,4,128]{2,1,0:T(4,128)}), f32[16,4,128]{2,1,0:T(4,128)S(1)}, u32[]{:S(2)}, u32[]{:S(2)}) async-start(f32[16,4,128]{2,1,0:T(4,128)} %broadcast_in_dim.278), calls=%async_computation.1 | async-start | bytes 65536 | tf_op jit(solution)/shard_map/all_to_all | solution.py:32
  75.3 14.9 %copy-start.13 = (f32[2304]{0:T(1024)}, f32[2304]{0:T(1024)S(1)}, u32[]{:S(2)}) copy-start(f32[2304]{0:T(1024)S(1)} %get-tuple-element.117) | copy-start | bytes 27652
  78.9 13.1 %copy-start.14 = (f32[8,1,130]{2,1,0:T(1,128)S(1)}, f32[8,1,130]{2,1,0:T(1,128)}, u32[]{:S(2)}) copy-start(f32[8,1,130]{2,1,0:T(1,128)} %copy.166) | copy-start | bytes 12484
  79.0 13.1 %copy-start.19 = (f32[8]{0:T(128)S(1)}, f32[8]{0:T(128)}, u32[]{:S(2)}) copy-start(f32[8]{0:T(128)} %param.23) | copy-start | bytes 100
  79.6 18.3 %all-to-all-start.2 = ((f32[64,1,128]{2,1,0:T(1,128)}), f32[64,1,128]{2,1,0:T(1,128)}, u32[]{:S(2)}, u32[]{:S(2)}) async-start(f32[64,1,128]{2,1,0:T(1,128)} %broadcast_in_dim.292), calls=%async_computation.2 | async-start | bytes 65536 | tf_op jit(solution)/shard_map/all_to_all | solution.py:32
  93.9 27.7 %copy-start.4 = (f32[64,2048]{1,0:T(8,128)S(1)}, f32[64,2048]{1,0:T(8,128)}, u32[]{:S(2)}) copy-start(f32[64,2048]{1,0:T(8,128)} %get-tuple-element.66) | copy-start | bytes 1572868
  99.3 21.8 %all-to-all-start.3 = ((f32[16,4,128]{2,1,0:T(4,128)}), f32[16,4,128]{2,1,0:T(4,128)S(1)}, u32[]{:S(2)}, u32[]{:S(2)}) async-start(f32[16,4,128]{2,1,0:T(4,128)} %broadcast_in_dim.293), calls=%async_computation.3 | async-start | bytes 65536 | tf_op jit(solution)/shard_map/all_to_all | solution.py:32
  125.2 22.6 %copy-start.21 = (pred[64]{0:T(512)(128)(4,1)S(1)}, pred[64]{0:T(512)(128)(4,1)}, u32[]{:S(2)}) copy-start(pred[64]{0:T(512)(128)(4,1)} %get-tuple-element.121) | copy-start | bytes 196
  125.2 22.6 %copy-start.22 = (pred[64]{0:T(512)(128)(4,1)S(1)}, pred[64]{0:T(512)(128)(4,1)}, u32[]{:S(2)}) copy-start(pred[64]{0:T(512)(128)(4,1)} %get-tuple-element.122) | copy-start | bytes 196
  125.3 47.7 %copy-start.8 = (f32[8,16,1]{2,1,0:T(8,128)S(1)}, f32[8,16,1]{2,1,0:T(8,128)}, u32[]{:S(2)}) copy-start(f32[8,16,1]{2,1,0:T(8,128)} %broadcast_in_dim.323) | copy-start | bytes 1540
  125.4 47.7 %copy-start.10 = (f32[8,16,1]{2,1,0:T(8,128)S(1)}, f32[8,16,1]{2,1,0:T(8,128)}, u32[]{:S(2)}) copy-start(f32[8,16,1]{2,1,0:T(8,128)} %broadcast_in_dim.324) | copy-start | bytes 1540
  125.4 47.7 %copy-start.15 = (f32[8,1,130]{2,1,0:T(1,128)S(1)}, f32[8,1,130]{2,1,0:T(1,128)}, u32[]{:S(2)}) copy-start(f32[8,1,130]{2,1,0:T(1,128)} %copy.166) | copy-start | bytes 12484
  125.4 47.7 %copy-start.20 = (f32[8]{0:T(128)S(1)}, f32[8]{0:T(128)}, u32[]{:S(2)}) copy-start(f32[8]{0:T(128)} %param.23) | copy-start | bytes 100
  126.6 21.0 %all-to-all-start.4 = ((f32[64,1,896]{2,1,0:T(1,128)}), f32[64,1,896]{2,1,0:T(1,128)S(1)}, u32[]{:S(2)}, u32[]{:S(2)}) async-start(f32[64,1,896]{2,1,0:T(1,128)} %reshape.317), calls=%async_computation.4 | async-start | bytes 458752 | tf_op jit(solution)/shard_map/all_to_all | solution.py:32
  149.2 15.1 %all-to-all-start.5 = ((f32[16,1,896]{2,1,0:T(1,128)}), f32[16,1,896]{2,1,0:T(1,128)S(1)}, u32[]{:S(2)}, u32[]{:S(2)}) async-start(f32[16,1,896]{2,1,0:T(1,128)} %broadcast_in_dim.315), calls=%async_computation.5 | async-start | bytes 114688 | tf_op jit(solution)/shard_map/all_to_all | solution.py:32
  165.8 16.6 %all-to-all-start.6 = ((f32[64,1,384]{2,1,0:T(1,128)}), f32[64,1,384]{2,1,0:T(1,128)S(1)}, u32[]{:S(2)}, u32[]{:S(2)}) async-start(f32[64,1,384]{2,1,0:T(1,128)} %broadcast_in_dim.318), calls=%async_computation.6 | async-start | bytes 196608 | tf_op jit(solution)/shard_map/all_to_all | solution.py:32
  (12 other events, 29.2 us)

commit v4 on v3

--- a/solution.py
+++ b/solution.py
@@ -62,6 +62,27 @@
 def side_sum(value):
     a, b, c, d = sides(value)
     return (a + b) + (c + d)
+
+
+def restrict_first(place, rhs, agg, row_ref):
+    row = restricted(rhs[...], agg[...].astype(jnp.float32), place[0])
+    row_ref[...] = jnp.broadcast_to(row[None], row_ref.shape)
+
+
+def merge(got, out_ref):
+    value = got[...].reshape(got.shape[0], 128)
+    lane = lax.broadcasted_iota(jnp.int32, value.shape, 1)
+    row = lax.broadcasted_iota(jnp.int32, value.shape, 0)
+    value = jnp.where(lane // AGG == row % 16, value, 0.0)
+    for k in range(out_ref.shape[1]):
+        part = jnp.sum(value[16 * k : 16 * k + 16], axis=0, keepdims=True)
+        for partner in range(out_ref.shape[0]):
+            out_ref[partner, k : k + 1] = part
+
+
+def add_parts(got, out_ref):
+    part = jnp.sum(got[...], axis=0, keepdims=True)
+    out_ref[...] = jnp.broadcast_to(part, out_ref.shape)
 
 
 def coarse_column(tiles, start, vector):
@@ -131,7 +152,8 @@
     f_ref[...] = (spread - 4.0 * wet * z) * valid_ref[...]
     own = (slice(0, CLON), slice(0, CLAT))
     z_own, w_own = z[own], w[own]
-    row_ref[...] = restricted(w_own, agg[own], place[0])
+    row = restricted(w_own, agg[own], place[0])
+    row_ref[...] = jnp.broadcast_to(row[None], row_ref.shape)
     lane = lax.broadcasted_iota(jnp.int32, (1, 128), 1)
     sum_ref[...] = jnp.where(lane == 0, total(rhs[own] * z_own), 0.0) + jnp.where(lane == 1, total(z_own * w_own), 0.0)
 
@@ -198,7 +220,8 @@
     front = row[:, :main] + on_z * row[:, main : 2 * main] + on_y * row[:, 2 * main : 3 * main]
     last = row[:, tail:]
     back = last + on_z * roll(last, -SPARE, 1) + on_y * roll(last, -2 * SPARE, 1)
-    mine_ref[...] = jnp.concatenate([front, back], axis=1)
+    mine = jnp.concatenate([front, back], axis=1)
+    mine_ref[...] = jnp.broadcast_to(mine[None], mine_ref.shape)
     lane = lax.broadcasted_iota(jnp.int32, (1, 128), 1)
     on_ref[...] = jnp.where(lane == 0, on_z, on_y)
 
@@ -276,17 +299,11 @@
     left = lax.ppermute(side_tiles(single[:, :, -1]), LAT, forward)
     right = lax.ppermute(side_tiles(single[:, :, 0]), LAT, backward)
 
-    local = restricted(surface_cot, aggregate_map.astype(f32), place)
-
-    def merged(got):
-        lane_slot = jnp.arange(128)[None, None] // AGG
-        kept = jnp.where(lane_slot == jnp.arange(16)[None, :, None], got.reshape(-1, 16, 128), 0.0)
-        return jnp.sum(kept, axis=1)
-
-    def to_all(block, axes):
-        return exchange(jnp.broadcast_to(block[None], (lax.axis_size(axes),) + block.shape), axes)
-
-    row = merged(to_all(local, LAYER))
+    every = (n_layer, 1, 128)
+    dense = (n_depth, n_layer * AGG // 128, 128)
+    (local,) = kernel_call(restrict_first, [every], place[None], surface_cot, aggregate_map, smem=1)
+
+    (row,) = kernel_call(merge, [dense], exchange(local, LAYER))
     row, left, right = lax.optimization_barrier((row, left, right))
 
     count = coarse.shape[0]
@@ -308,7 +325,7 @@
     forward, backward = shifted(single, LON, True)
     above = lax.ppermute(end_tiles(CLON - 1, CLON - 2, several[:, -8:]), LON, forward)
     below = lax.ppermute(end_tiles(0, 1, several[:, :8]), LON, backward)
-    gathered = to_all(row, DEPTH).reshape(-1, 128)
+    gathered = exchange(row, DEPTH).reshape(-1, 128)
     gathered, above, below = lax.optimization_barrier((gathered, above, below))
 
     def unpack_rows(tiles):
@@ -323,7 +340,7 @@
     def unringed(line):
         return jnp.concatenate([line[:, -1:], line[:, : CLAT + 1]], axis=1)[:, None]
 
-    def padded(first, last):
+    def padded(first, last, line_left, line_right):
         def ends(line):
             return unringed(line[first:last])
 
@@ -332,16 +349,20 @@
         )
         return jnp.concatenate([ends(line_above), middle, ends(line_below)], axis=1)
 
-    levels = velocity.shape[0]
-    feat_pad = jnp.concatenate([unringed(more_above), padded(0, CIN), unringed(more_below)], axis=1).astype(jnp.bfloat16)
-    vel_pad = padded(CIN, CIN + levels)
-    cot_pad = padded(CIN + levels, CIN + 2 * levels)
-
     tiles = (left, coarse, right, above, below, several, valid)
     w, force, row, sums = kernel_call(
-        solve_first, [(ROWS, LANES), (ROWS, LANES), (1, 128), (1, 128)], place[None], gathered, *tiles, smem=1
+        solve_first, [(ROWS, LANES), (ROWS, LANES), every, (1, 128)], place[None], gathered, *tiles, smem=1
     )
-    gathered = to_all(merged(to_all(row, LAYER)), DEPTH).reshape(-1, 128)
+    row, line_left, line_right = lax.optimization_barrier((row, line_left, line_right))
+    feat_pad = jnp.concatenate(
+        [unringed(more_above), padded(0, CIN, line_left, line_right), unringed(more_below)], axis=1
+    ).astype(jnp.bfloat16)
+    (row,) = kernel_call(merge, [dense], exchange(row, LAYER))
+    row, line_left, line_right = lax.optimization_barrier((row, line_left, line_right))
+    levels = velocity.shape[0]
+    vel_pad = padded(CIN, CIN + levels, line_left, line_right)
+    cot_pad = padded(CIN + levels, CIN + 2 * levels, line_left, line_right)
+    gathered = exchange(row, DEPTH).reshape(-1, 128)
 
     around = patches_of(feat_pad)
     hidden = jnp.tanh(jnp.dot(conv_weight, around, preferred_element_type=f32) + conv_bias[:, None])
@@ -400,8 +421,8 @@
         axis=1,
     )
     got = exchange(table.reshape(n_layer, each, table.shape[1]), LAYER)
-    part = jnp.sum(got, axis=0)
-    mine, on = kernel_call(finish, [(each, 384), (1, 128)], to_all(part, DEPTH))
+    (part,) = kernel_call(add_parts, [(n_depth, each, table.shape[1])], got)
+    mine, on = kernel_call(finish, [(n_layer, each, 384), (1, 128)], exchange(part, DEPTH))
 
     to = jnp.arange(n_layer)[:, None]
     lines = got[:, 0, 6 * 128 + 3 * SPARE + 5 :][:, :CLON]
@@ -419,7 +440,7 @@
     for visc_side, cot_side in zip(neighbours(visc_pad), neighbours(cot_pad)):
         base = base + 0.5 * (viscosity + visc_side)[None] * (cot_side - velocity_cot)
     base = velocity_cot + time_step * base
-    final = to_all(mine, LAYER).reshape(HID, 384)
+    final = exchange(mine, LAYER).reshape(HID, 384)
     spread = on[:, :1] * spreads[0] + on[:, 1:2] * spreads[1]
     grad_velocity = base + level * spread[None]
     return (grad_velocity, final[:, :TAPS], final[:, TAPS], final[:, TAPS + 1])

time: 184 us -> 190 us (1.033)
  waiting for transfers between devices: 58.6 us -> 62.7 us
  Pallas kernels: 1.2 us -> 5.22 us
  other arithmetic: 19.2 us -> 17 us
    ppermute x1, waiting for transfers between devices: 0.01 us -> 7.15 us  [shards(): lax.ppermute(end_tiles(CLON - 1, CLON - 2, several[:, -8:]), LON, forward)]
    pallas_call x4 -> x8, Pallas kernels: 1.2 us -> 5.22 us  [kernel_call(): pl.pallas_call(body, out_shape=[jax.ShapeDtypeStruct(shape, jnp.float32)...]
    broadcast_in_dim x6 -> x0, local copies, waits for them, and re-layouts: 3.85 us -> none  [to_all(): jnp.broadcast_to(block[None], (lax.axis_size(axes),) + block.shape)]
    slice x8, local copies, waits for them, and re-layouts: 0.59 us -> 3.31 us  [unringed(): return jnp.concatenate([line[:, -1:], line[:, :CLAT + 1]], axis=1)[:, None]]
    ppermute x1, waiting for transfers between devices: 4.4 us -> 1.72 us  [shards(): right = lax.ppermute(side_tiles(single[:, :, 0]), LAT, backward)]
    broadcast_in_dim x8, other arithmetic: 0.62 us -> 2.7 us  [unringed(): return jnp.concatenate([line[:, -1:], line[:, :CLAT + 1]], axis=1)[:, None]]
    reduce_sum x6 -> x0, other arithmetic: 1.92 us -> none  [the longest x2 0.8 us: merged(): return jnp.sum(kept, axis=1)]
    unnamed x61 -> x69, local copies, waits for them, and re-layouts: 3.2 us -> 4.96 us
where the time goes in v4:
time: 190 us; the launch traced here: 189 us
  starting transfers between devices  80.8 us (43%)
  waiting for transfers between devices  62.7 us (33%)
  local copies, waits for them, and re-layouts  20 us (11%)
  other arithmetic  17 us (9%)
  Pallas kernels  5.22 us (3%)
    all_to_all x7, starting transfers between devices, exchange(): return lax.all_to_all(values, axes, 0, 0, tiled=True)  59.3 us
    all_to_all x7, waiting for transfers between devices, exchange(): return lax.all_to_all(values, axes, 0, 0, tiled=True)  52.6 us
    ppermute x1, starting transfers between devices, shards(): below = lax.ppermute(end_tiles(0, 1, several[:, :8]), LON, backward)  13.9 us
    ppermute x1, waiting for transfers between devices, shards(): lax.ppermute(end_tiles(CLON - 1, CLON - 2, several[:, -8:]), LON, forward)  7.15 us
    pallas_call x8, Pallas kernels, kernel_call(): pl.pallas_call(body, out_shape=[jax.ShapeDtypeStruct(shape, jnp.float32)...  5.22 us
    unnamed x69, local copies, waits for them, and re-layouts  4.96 us
  transfers between devices with their start and end apart: 11, of which 8 were waited for; matrix products, arithmetic and copies ran while one was open for 11% of the time, Pallas kernels for 0%

profile of v4, /device:TPU:1, one launch (start us, length us, event | category | flops | bytes accessed | tf_op | source)
XLA Modules:
  0.0 189.0 jit_solution(9904092738839508868)
XLA Ops:
  2.8 18.2 %all-to-all-start = ((f32[64,1,128]{2,1,0:T(1,128)}), f32[64,1,128]{2,1,0:T(1,128)S(1)}, u32[]{:S(2)}, u32[]{:S(2)}) async-start(f32[64,1,128]{2,1,0:T(1,128)} %shard_map.147), calls=%async_computation | async-start | bytes 65536 | tf_op jit(solution)/shard_map/all_to_all | solution.py:32
  24.8 2.5 %collective-permute-start.1 = (f32[73,8,128]{2,1,0:T(8,128)S(1)}, f32[73,8,128]{2,1,0:T(8,128)S(1)}, u32[]{:S(2)}, u32[]{:S(2)}) collective-permute-start(f32[73,8,128]{2,1,0:T(8,128)S(1)} %get-tuple-element.79), channel_id=1, source_target_pairs={{1,0},{2,1},{3,2},{4,3},{5,4},{6,5},{7,6},{9,8},{10,9},{11,10},{12... | collective-permute-start | bytes 897032 | tf_op jit(solution)/shard_map/ppermute | solution.py:300
  27.3 3.1 %collective-permute-start = (f32[73,8,128]{2,1,0:T(8,128)S(1)}, f32[73,8,128]{2,1,0:T(8,128)S(1)}, u32[]{:S(2)}, u32[]{:S(2)}) collective-permute-start(f32[73,8,128]{2,1,0:T(8,128)S(1)} %get-tuple-element.80), channel_id=1, source_target_pairs={{0,1},{1,2},{2,3},{3,4},{4,5},{5,6},{6,7},{8,9},{9,10},{10,11},{11... | collective-permute-start | bytes 897032 | tf_op jit(solution)/shard_map/ppermute | solution.py:299
  31.2 1.7 collective-permute-done.1.right
  32.9 1.2 collective-permute-done.left
  34.6 1.4 pad_maximum_fusion.2
  36.0 13.9 %collective-permute-start.3 = (f32[220,8,128]{2,1,0:T(8,128)}, f32[220,8,128]{2,1,0:T(8,128)S(1)}, u32[]{:S(2)}, u32[]{:S(2)}) collective-permute-start(f32[220,8,128]{2,1,0:T(8,128)} %get-tuple-element.64), channel_id=1, source_target_pairs={{8,0},{16,8},{24,16},{32,24},{40,32},{48,40},{56,48},{64,56},{72,6... | collective-permute-start | bytes 2703368 | tf_op jit(solution)/shard_map/ppermute | solution.py:327
  49.9 1.9 %collective-permute-start.2 = (f32[220,8,128]{2,1,0:T(8,128)}, f32[220,8,128]{2,1,0:T(8,128)S(1)}, u32[]{:S(2)}, u32[]{:S(2)}) collective-permute-start(f32[220,8,128]{2,1,0:T(8,128)} %get-tuple-element.65), channel_id=1, source_target_pairs={{0,8},{8,16},{16,24},{24,32},{32,40},{40,48},{48,56},{56,64},{64,7... | collective-permute-start | bytes 2703368 | tf_op jit(solution)/shard_map/ppermute | solution.py:326
  51.9 3.5 %all-to-all-start.1 = ((f32[16,4,128]{2,1,0:T(4,128)}), f32[16,4,128]{2,1,0:T(4,128)S(1)}, u32[]{:S(2)}, u32[]{:S(2)}) async-start(f32[16,4,128]{2,1,0:T(4,128)} %shard_map.148), calls=%async_computation.1 | async-start | bytes 65536 | tf_op jit(solution)/shard_map/all_to_all | solution.py:32
  55.9 12.5 %all-to-all-done.1 = f32[16,4,128]{2,1,0:T(4,128)S(1)} async-done(((f32[16,4,128]{2,1,0:T(4,128)}), f32[16,4,128]{2,1,0:T(4,128)S(1)}, u32[]{:S(2)}, u32[]{:S(2)}) %all-to-all-start.1) | async-done | bytes 32800 | tf_op jit(solution)/shard_map/all_to_all | solution.py:32
  68.5 7.2 %collective-permute-done.2.above = f32[220,8,128]{2,1,0:T(8,128)S(1)} collective-permute-done((f32[220,8,128]{2,1,0:T(8,128)}, f32[220,8,128]{2,1,0:T(8,128)S(1)}, u32[]{:S(2)}, u32[]{:S(2)}) %collective-permute-start.2) | collective-permute-done | bytes 901152 | tf_op jit(solution)/shard_map/ppermute | solution.py:326
  83.2 9.5 %all-to-all-start.2 = ((f32[64,1,128]{2,1,0:T(1,128)}), f32[64,1,128]{2,1,0:T(1,128)S(1)}, u32[]{:S(2)}, u32[]{:S(2)}) async-start(f32[64,1,128]{2,1,0:T(1,128)} %get-tuple-element.34), calls=%async_computation.2 | async-start | bytes 65536 | tf_op jit(solution)/shard_map/all_to_all | solution.py:32
  100.9 1.7 fusion.48
  105.4 7.1 %all-to-all-start.3 = ((f32[16,4,128]{2,1,0:T(4,128)}), f32[16,4,128]{2,1,0:T(4,128)S(1)}, u32[]{:S(2)}, u32[]{:S(2)}) async-start(f32[16,4,128]{2,1,0:T(4,128)} %shard_map.150), calls=%async_computation.3 | async-start | bytes 65536 | tf_op jit(solution)/shard_map/all_to_all | solution.py:32
  113.6 1.1 fusion.22
  114.8 1.2 multiply_reduce_fusion.4
  116.1 7.9 %all-to-all-done.3 = f32[16,4,128]{2,1,0:T(4,128)S(1)} async-done(((f32[16,4,128]{2,1,0:T(4,128)}), f32[16,4,128]{2,1,0:T(4,128)S(1)}, u32[]{:S(2)}, u32[]{:S(2)}) %all-to-all-start.3) | async-done | bytes 32800 | tf_op jit(solution)/shard_map/all_to_all | solution.py:32
  129.5 11.7 %all-to-all-start.4 = ((f32[64,1,896]{2,1,0:T(1,128)}), f32[64,1,896]{2,1,0:T(1,128)S(1)}, u32[]{:S(2)}, u32[]{:S(2)}) async-start(f32[64,1,896]{2,1,0:T(1,128)} %reshape.208), calls=%async_computation.4 | async-start | bytes 458752 | tf_op jit(solution)/shard_map/all_to_all | solution.py:32
  141.3 12.4 %all-to-all-done.4.got = f32[64,1,896]{2,1,0:T(1,128)S(1)} async-done(((f32[64,1,896]{2,1,0:T(1,128)}), f32[64,1,896]{2,1,0:T(1,128)S(1)}, u32[]{:S(2)}, u32[]{:S(2)}) %all-to-all-start.4) | async-done | bytes 229408 | tf_op jit(solution)/shard_map/all_to_all | solution.py:32
  155.1 3.5 %all-to-all-start.5 = ((f32[16,1,896]{2,1,0:T(1,128)}), f32[16,1,896]{2,1,0:T(1,128)S(1)}, u32[]{:S(2)}, u32[]{:S(2)}) async-start(f32[16,1,896]{2,1,0:T(1,128)} %shard_map.152), calls=%async_computation.5 | async-start | bytes 114688 | tf_op jit(solution)/shard_map/all_to_all | solution.py:32
  158.9 11.3 %all-to-all-done.5.parts = f32[16,1,896]{2,1,0:T(1,128)S(1)} async-done(((f32[16,1,896]{2,1,0:T(1,128)}), f32[16,1,896]{2,1,0:T(1,128)S(1)}, u32[]{:S(2)}, u32[]{:S(2)}) %all-to-all-start.5) | async-done | bytes 57376 | tf_op jit(solution)/shard_map/all_to_all | solution.py:32
  171.6 5.9 %all-to-all-start.6 = ((f32[64,1,384]{2,1,0:T(1,128)}), f32[64,1,384]{2,1,0:T(1,128)S(1)}, u32[]{:S(2)}, u32[]{:S(2)}) async-start(f32[64,1,384]{2,1,0:T(1,128)} %get-tuple-element.45), calls=%async_computation.6 | async-start | bytes 196608 | tf_op jit(solution)/shard_map/all_to_all | solution.py:32
  177.5 1.3 fusion.34
  179.7 8.5 %all-to-all-done.6 = f32[64,1,384]{2,1,0:T(1,128)S(1)} async-done(((f32[64,1,384]{2,1,0:T(1,128)}), f32[64,1,384]{2,1,0:T(1,128)S(1)}, u32[]{:S(2)}, u32[]{:S(2)}) %all-to-all-start.6) | async-done | bytes 98336 | tf_op jit(solution)/shard_map/all_to_all | solution.py:32
  (197 shorter events, 37.2 us)
Async XLA Ops:
  0.6 80.9 %copy-start = (bf16[64,288]{1,0:T(8,128)(2,1)S(1)}, bf16[64,288]{1,0:T(8,128)(2,1)}, u32[]{:S(2)}) copy-start(bf16[64,288]{1,0:T(8,128)(2,1)} %param.20) | copy-start | bytes 110596
  2.8 27.7 %all-to-all-start = ((f32[64,1,128]{2,1,0:T(1,128)}), f32[64,1,128]{2,1,0:T(1,128)S(1)}, u32[]{:S(2)}, u32[]{:S(2)}) async-start(f32[64,1,128]{2,1,0:T(1,128)} %shard_map.147), calls=%async_computation | async-start | bytes 65536 | tf_op jit(solution)/shard_map/all_to_all | solution.py:32
  23.6 6.8 %copy-start.13 = (bf16[32,16,128]{2,1,0:T(8,128)(2,1)S(1)}, bf16[32,16,128]{2,1,0:T(8,128)(2,1)}, u32[]{:S(2)}) copy-start(bf16[32,16,128]{2,1,0:T(8,128)(2,1)} %param.12) | copy-start | bytes 393220
  24.8 8.1 %collective-permute-start.1 = (f32[73,8,128]{2,1,0:T(8,128)S(1)}, f32[73,8,128]{2,1,0:T(8,128)S(1)}, u32[]{:S(2)}, u32[]{:S(2)}) collective-permute-start(f32[73,8,128]{2,1,0:T(8,128)S(1)} %get-tuple-element.79), channel_id=1, source_target_pairs={{1,0},{2,1},{3,2},{4,3},{5,4},{6,5},{7,6},{9,8},{10,9},{11,10},{12... | collective-permute-start | bytes 897032 | tf_op jit(solution)/shard_map/ppermute | solution.py:300
  27.3 6.8 %collective-permute-start = (f32[73,8,128]{2,1,0:T(8,128)S(1)}, f32[73,8,128]{2,1,0:T(8,128)S(1)}, u32[]{:S(2)}, u32[]{:S(2)}) collective-permute-start(f32[73,8,128]{2,1,0:T(8,128)S(1)} %get-tuple-element.80), channel_id=1, source_target_pairs={{0,1},{1,2},{2,3},{3,4},{4,5},{5,6},{6,7},{8,9},{9,10},{10,11},{11... | collective-permute-start | bytes 897032 | tf_op jit(solution)/shard_map/ppermute | solution.py:299
  34.2 46.0 %copy-start.14 = (f32[48,16]{1,0:T(8,128)}, f32[48,16]{1,0:T(8,128)S(1)}, u32[]{:S(2)}) copy-start(f32[48,16]{1,0:T(8,128)S(1)} %slice.413) | copy-start | bytes 9220
  36.0 32.5 %collective-permute-start.3 = (f32[220,8,128]{2,1,0:T(8,128)}, f32[220,8,128]{2,1,0:T(8,128)S(1)}, u32[]{:S(2)}, u32[]{:S(2)}) collective-permute-start(f32[220,8,128]{2,1,0:T(8,128)} %get-tuple-element.64), channel_id=1, source_target_pairs={{8,0},{16,8},{24,16},{32,24},{40,32},{48,40},{56,48},{64,56},{72,6... | collective-permute-start | bytes 2703368 | tf_op jit(solution)/shard_map/ppermute | solution.py:327
  49.9 25.7 %collective-permute-start.2 = (f32[220,8,128]{2,1,0:T(8,128)}, f32[220,8,128]{2,1,0:T(8,128)S(1)}, u32[]{:S(2)}, u32[]{:S(2)}) collective-permute-start(f32[220,8,128]{2,1,0:T(8,128)} %get-tuple-element.65), channel_id=1, source_target_pairs={{0,8},{8,16},{16,24},{24,32},{32,40},{40,48},{48,56},{56,64},{64,7... | collective-permute-start | bytes 2703368 | tf_op jit(solution)/shard_map/ppermute | solution.py:326
  51.9 16.6 %all-to-all-start.1 = ((f32[16,4,128]{2,1,0:T(4,128)}), f32[16,4,128]{2,1,0:T(4,128)S(1)}, u32[]{:S(2)}, u32[]{:S(2)}) async-start(f32[16,4,128]{2,1,0:T(4,128)} %shard_map.148), calls=%async_computation.1 | async-start | bytes 65536 | tf_op jit(solution)/shard_map/all_to_all | solution.py:32
  83.2 20.8 %all-to-all-start.2 = ((f32[64,1,128]{2,1,0:T(1,128)}), f32[64,1,128]{2,1,0:T(1,128)S(1)}, u32[]{:S(2)}, u32[]{:S(2)}) async-start(f32[64,1,128]{2,1,0:T(1,128)} %get-tuple-element.34), calls=%async_computation.2 | async-start | bytes 65536 | tf_op jit(solution)/shard_map/all_to_all | solution.py:32
  92.8 10.6 %copy-start.22 = (f32[8,256]{1,0:T(8,128)S(1)}, f32[8,256]{1,0:T(8,128)}, u32[]{:S(2)}) copy-start(f32[8,256]{1,0:T(8,128)} %get-tuple-element.91) | copy-start | bytes 24580
  105.4 18.5 %all-to-all-start.3 = ((f32[16,4,128]{2,1,0:T(4,128)}), f32[16,4,128]{2,1,0:T(4,128)S(1)}, u32[]{:S(2)}, u32[]{:S(2)}) async-start(f32[16,4,128]{2,1,0:T(4,128)} %shard_map.150), calls=%async_computation.3 | async-start | bytes 65536 | tf_op jit(solution)/shard_map/all_to_all | solution.py:32
  114.8 9.6 %copy-start.7 = (f32[64,2048]{1,0:T(8,128)S(1)}, f32[64,2048]{1,0:T(8,128)}, u32[]{:S(2)}) copy-start(f32[64,2048]{1,0:T(8,128)} %get-tuple-element.66) | copy-start | bytes 1572868
  128.0 13.2 %copy-start.18 = (f32[18,128]{1,0:T(8,128)S(1)}, f32[18,128]{1,0:T(8,128)}, u32[]{:S(2)}) copy-start(f32[18,128]{1,0:T(8,128)} %compare_select_fusion) | copy-start | bytes 27652
  128.0 25.8 %copy-start.25 = (pred[64]{0:T(512)(128)(4,1)S(1)}, pred[64]{0:T(512)(128)(4,1)}, u32[]{:S(2)}) copy-start(pred[64]{0:T(512)(128)(4,1)} %get-tuple-element.127) | copy-start | bytes 196
  128.0 25.8 %copy-start.26 = (pred[64]{0:T(512)(128)(4,1)S(1)}, pred[64]{0:T(512)(128)(4,1)}, u32[]{:S(2)}) copy-start(pred[64]{0:T(512)(128)(4,1)} %get-tuple-element.128) | copy-start | bytes 196
  128.1 50.7 %copy-start.12 = (f32[8,16,1]{2,1,0:T(8,128)S(1)}, f32[8,16,1]{2,1,0:T(8,128)}, u32[]{:S(2)}) copy-start(f32[8,16,1]{2,1,0:T(8,128)} %copy-done.11) | copy-start | bytes 1540
  128.1 50.7 %copy-start.15 = (f32[8,16,1]{2,1,0:T(8,128)S(1)}, f32[8,16,1]{2,1,0:T(8,128)}, u32[]{:S(2)}) copy-start(f32[8,16,1]{2,1,0:T(8,128)} %copy.163) | copy-start | bytes 1540
  128.1 50.7 %copy-start.20 = (f32[8,1,130]{2,1,0:T(1,128)S(1)}, f32[8,1,130]{2,1,0:T(1,128)}, u32[]{:S(2)}) copy-start(f32[8,1,130]{2,1,0:T(1,128)} %copy.165) | copy-start | bytes 12484
  128.1 50.7 %copy-start.21 = (f32[8,1,130]{2,1,0:T(1,128)S(1)}, f32[8,1,130]{2,1,0:T(1,128)}, u32[]{:S(2)}) copy-start(f32[8,1,130]{2,1,0:T(1,128)} %copy.164) | copy-start | bytes 12484
  128.2 50.7 %copy-start.24 = (f32[8]{0:T(128)S(1)}, f32[8]{0:T(128)}, u32[]{:S(2)}) copy-start(f32[8]{0:T(128)} %param.23) | copy-start | bytes 100
  129.5 24.2 %all-to-all-start.4 = ((f32[64,1,896]{2,1,0:T(1,128)}), f32[64,1,896]{2,1,0:T(1,128)S(1)}, u32[]{:S(2)}, u32[]{:S(2)}) async-start(f32[64,1,896]{2,1,0:T(1,128)} %reshape.208), calls=%async_computation.4 | async-start | bytes 458752 | tf_op jit(solution)/shard_map/all_to_all | solution.py:32
  155.1 15.1 %all-to-all-start.5 = ((f32[16,1,896]{2,1,0:T(1,128)}), f32[16,1,896]{2,1,0:T(1,128)S(1)}, u32[]{:S(2)}, u32[]{:S(2)}) async-start(f32[16,1,896]{2,1,0:T(1,128)} %shard_map.152), calls=%async_computation.5 | async-start | bytes 114688 | tf_op jit(solution)/shard_map/all_to_all | solution.py:32
  171.6 16.6 %all-to-all-start.6 = ((f32[64,1,384]{2,1,0:T(1,128)}), f32[64,1,384]{2,1,0:T(1,128)S(1)}, u32[]{:S(2)}, u32[]{:S(2)}) async-start(f32[64,1,384]{2,1,0:T(1,128)} %get-tuple-element.45), calls=%async_computation.6 | async-start | bytes 196608 | tf_op jit(solution)/shard_map/all_to_all | solution.py:32
  (16 other events, 32.6 us)

commit v5 on v3

--- a/solution.py
+++ b/solution.py
@@ -71,24 +71,16 @@
     return jnp.sum(acc, axis=1, keepdims=True)
 
 
-def coarse_columns(gathered, left, coarse, right, above, below):
-    vector = gathered[...]
-    count = vector.shape[0]
-    middle = [coarse_column(tiles, 0, vector) for tiles in (left, coarse, right)]
-    outer = [[coarse_column(tiles, k * count, vector) for k in range(3)] for tiles in (above, below)]
-    return outer[0], middle, outer[1]
-
-
-def ring_fields(gathered, inner, above, below):
-    start = 3 * gathered.shape[0]
+def solve_start(rhs, damp, wet, agg, columns):
+    diagonal = 4.0 + damp
+    z = rhs / diagonal + coarse_field(agg, *columns)
+    spread = side_sum(wet * z)
+    return z, diagonal * z - wet * spread, spread - 4.0 * wet * z
+
+
+def ring_fields(inner, low, high):
     row = lax.broadcasted_iota(jnp.int32, (8, LANES), 0)
-    out = []
-    for k in range(inner.shape[0]):
-        at = start + 2 * k
-        low = jnp.concatenate([below[at], below[at + 1]], axis=1)
-        high = jnp.concatenate([above[at], above[at + 1]], axis=1)
-        out.append(jnp.concatenate([inner[k], jnp.where(row < 4, low, high)], axis=0))
-    return out
+    return [jnp.concatenate([inner[k], jnp.where(row < 4, low[k], high[k])], axis=0) for k in range(inner.shape[0])]
 
 
 def coarse_field(agg, above, middle, below):
@@ -120,15 +112,19 @@
     return jnp.sum(jnp.where(lane == first + row, sums, 0.0), axis=0, keepdims=True)
 
 
-def solve_first(place, gathered, left, coarse, right, above, below, inner, valid_ref, w_ref, f_ref, row_ref, sum_ref):
-    rhs, damp, wet, agg = ring_fields(gathered, inner, above, below)
-    diagonal = 4.0 + damp
-    columns = coarse_columns(gathered, left, coarse, right, above, below)
-    z = rhs / diagonal + coarse_field(agg, *columns)
-    spread = side_sum(wet * z)
-    w = diagonal * z - wet * spread
-    w_ref[...] = w
-    f_ref[...] = (spread - 4.0 * wet * z) * valid_ref[...]
+def solve_first(place, gathered, left, coarse, right, above, below, inner, row_ref, sum_ref):
+    vector = gathered[...]
+    count = vector.shape[0]
+
+    def outer(tiles):
+        blank = jnp.zeros((8, LANES - CLAT), jnp.float32)
+        return [jnp.concatenate([tiles[count + k], blank], axis=1) for k in range(inner.shape[0])]
+
+    rhs, damp, wet, agg = ring_fields(inner, outer(below), outer(above))
+    none = jnp.zeros((AGG, 1), jnp.float32)
+    middle = [coarse_column(tiles, 0, vector) for tiles in (left, coarse, right)]
+    ends = [[none, coarse_column(tiles, 0, vector), none] for tiles in (above, below)]
+    z, w, force = solve_start(rhs, damp, wet, agg, (ends[0], middle, ends[1]))
     own = (slice(0, CLON), slice(0, CLAT))
     z_own, w_own = z[own], w[own]
     row_ref[...] = restricted(w_own, agg[own], place[0])
@@ -137,14 +133,30 @@
 
 
 def solve_second(
-    gathered, left, coarse, right, above, below, inner, valid_ref, w_ref, f_ref, weight_ref, slope_ref, first_ref,
-    sum_in, grad_ref, force_ref, sum_ref,
+    gathered_first, gathered, left, coarse, right, above, below, far_above, far_below, inner, valid_ref, weight_ref,
+    slope_ref, first_ref, sum_in, grad_ref, force_ref, sum_ref,
 ):
-    rhs, damp, wet, agg = ring_fields(gathered, inner, above, below)
+    count = gathered.shape[0]
+
+    def outer(tiles):
+        at = 2 * count
+        return [
+            jnp.concatenate([tiles[at + 2 * k], tiles[at + 2 * k + 1]], axis=1) for k in range(inner.shape[0])
+        ]
+
+    def columns_of(ref):
+        vector = ref[...]
+        middle = [coarse_column(tiles, 0, vector) for tiles in (left, coarse, right)]
+        ends = [
+            [coarse_column(far, 0, vector), coarse_column(near, 0, vector), coarse_column(far, count, vector)]
+            for near, far in ((above, far_above), (below, far_below))
+        ]
+        return ends[0], middle, ends[1]
+
+    rhs, damp, wet, agg = ring_fields(inner, outer(far_below), outer(far_above))
     diagonal = 4.0 + damp
-    w = w_ref[...]
-    columns = coarse_columns(gathered, left, coarse, right, above, below)
-    y = w / diagonal + coarse_field(agg, *columns)
+    z, w, leading = solve_start(rhs, damp, wet, agg, columns_of(gathered_first))
+    y = w / diagonal + coarse_field(agg, *columns_of(gathered))
     around = side_sum(wet * y)
     image = diagonal * y - wet * around
     own = (slice(0, CLON), slice(0, CLAT))
@@ -156,9 +168,9 @@
     sum_ref[...] = sums
     weight = weight_ref[...]
     grad_ref[0] = first_ref[...] * weight
-    second = (around - 4.0 * wet * y) * valid_ref[...]
-    force_ref[...] = second
-    for at, force in ((1, f_ref[...]), (2, second)):
+    forces = (leading * valid_ref[...], (around - 4.0 * wet * y) * valid_ref[...])
+    for at, force in enumerate(forces, 1):
+        force_ref[at - 1] = force
         force_own = force[own]
         slope = jnp.zeros((CLON, CLAT), jnp.float32)
         for n, side in enumerate(sides(force)):
@@ -166,11 +178,12 @@
         grad_ref[at] = slope * weight
 
 
-def diffuse(visc_ref, first, second, spread_ref):
+def diffuse(visc_ref, forces, spread_ref):
     own = (slice(0, CLON), slice(0, CLAT))
     visc = visc_ref[...]
     visc_sides = [0.5 * (visc[own] + side[own]) for side in sides(visc)]
-    for at, force in ((0, first[...]), (1, second[...])):
+    for at in range(2):
+        force = forces[at]
         force_own = force[own]
         bend = jnp.zeros((CLON, CLAT), jnp.float32)
         for visc_side, side in zip(visc_sides, sides(force)):
@@ -276,6 +289,10 @@
     left = lax.ppermute(side_tiles(single[:, :, -1]), LAT, forward)
     right = lax.ppermute(side_tiles(single[:, :, 0]), LAT, backward)
 
+    forward_lon, backward_lon = shifted(single, LON, True)
+    above = lax.ppermute(jnp.concatenate([coarse, several[:, 8:]], axis=0), LON, forward_lon)
+    below = lax.ppermute(jnp.concatenate([coarse, several[:, :8]], axis=0), LON, backward_lon)
+
     local = restricted(surface_cot, aggregate_map.astype(f32), place)
 
     def merged(got):
@@ -287,7 +304,8 @@
         return exchange(jnp.broadcast_to(block[None], (lax.axis_size(axes),) + block.shape), axes)
 
     row = merged(to_all(local, LAYER))
-    row, left, right = lax.optimization_barrier((row, left, right))
+    gathered_first = to_all(row, DEPTH).reshape(-1, 128)
+    gathered_first, left, right, above, below = lax.optimization_barrier((gathered_first, left, right, above, below))
 
     count = coarse.shape[0]
     line_left = left[-1].reshape(64, CLON)[:n_single]
@@ -295,7 +313,21 @@
     lane = jnp.arange(CLAT)[None, None]
     rest = jnp.where(lane < CLAT // 2, right[count:-1].reshape(several.shape), left[count:-1].reshape(several.shape))
     several = jnp.concatenate([several, rest], axis=2)
-    band = jnp.concatenate([left[:count], coarse, right[:count]], axis=0)
+    row, sums = kernel_call(
+        solve_first,
+        [(1, 128), (1, 128)],
+        place[None],
+        gathered_first,
+        left,
+        coarse,
+        right,
+        above,
+        below,
+        several,
+        smem=1,
+    )
+    row, line_left, line_right = lax.optimization_barrier((row, line_left, line_right))
+    band = jnp.concatenate([left[:count], right[:count]], axis=0)
 
     def end_tiles(at, second, block):
         line = ring_lanes(single[:, at, :], line_right[:, at : at + 1], line_left[:, at : at + 1])
@@ -305,18 +337,15 @@
         edge = jnp.concatenate([block.reshape(-1, LANES), line, more], axis=0)
         return jnp.concatenate([band, tiles_of(edge)], axis=0)
 
-    forward, backward = shifted(single, LON, True)
-    above = lax.ppermute(end_tiles(CLON - 1, CLON - 2, several[:, -8:]), LON, forward)
-    below = lax.ppermute(end_tiles(0, 1, several[:, :8]), LON, backward)
-    gathered = to_all(row, DEPTH).reshape(-1, 128)
-    gathered, above, below = lax.optimization_barrier((gathered, above, below))
+    far_above = lax.ppermute(end_tiles(CLON - 1, CLON - 2, several[:, -8:]), LON, forward_lon)
+    far_below = lax.ppermute(end_tiles(0, 1, several[:, :8]), LON, backward_lon)
 
     def unpack_rows(tiles):
-        edge = rows_of(tiles[3 * count + 2 * n_several :], n_single + CIN)
+        edge = rows_of(tiles[2 * count + 2 * n_several :], n_single + CIN)
         return edge[:n_single], edge[n_single:]
 
-    line_above, more_above = unpack_rows(above)
-    line_below, more_below = unpack_rows(below)
+    line_above, more_above = unpack_rows(far_above)
+    line_below, more_below = unpack_rows(far_below)
     lane = jnp.arange(LANES)[None]
     valid = jnp.where(lane < CLAT, 1.0, jnp.where(lane < CLAT + LANES // 4, lat < n_lat - 1, lat > 0).astype(f32))
 
@@ -337,10 +366,6 @@
     vel_pad = padded(CIN, CIN + levels)
     cot_pad = padded(CIN + levels, CIN + 2 * levels)
 
-    tiles = (left, coarse, right, above, below, several, valid)
-    w, force, row, sums = kernel_call(
-        solve_first, [(ROWS, LANES), (ROWS, LANES), (1, 128), (1, 128)], place[None], gathered, *tiles, smem=1
-    )
     gathered = to_all(merged(to_all(row, LAYER)), DEPTH).reshape(-1, 128)
 
     around = patches_of(feat_pad)
@@ -360,13 +385,20 @@
     cells_all = CLON * CLAT * n_lon * n_lat
     weight = jax.nn.sigmoid(logits) * (-0.5 * time_step / math.sqrt(cells_all))
 
-    grads, second, sums = kernel_call(
+    grads, forces, sums = kernel_call(
         solve_second,
-        [(3, CLON, CLAT), (ROWS, LANES), (1, 128)],
+        [(3, CLON, CLAT), (2, ROWS, LANES), (1, 128)],
+        gathered_first,
         gathered,
-        *tiles,
-        w,
-        force,
+        left,
+        coarse,
+        right,
+        above,
+        below,
+        far_above,
+        far_below,
+        several,
+        valid,
         weight,
         jnp.stack(slopes),
         first,
@@ -414,7 +446,7 @@
     visc = ring_rows(ring_lanes(viscosity, visc_right, visc_left), rim(visc_rows[-1:]), rim(visc_rows[:1]))
     visc_pad = jnp.concatenate([visc[-1:], visc[: CLON + 1]], axis=0)
     visc_pad = jnp.concatenate([visc_pad[:, -1:], visc_pad[:, : CLAT + 1]], axis=1)
-    (spreads,) = kernel_call(diffuse, [(2, CLON, CLAT)], visc, force, second)
+    (spreads,) = kernel_call(diffuse, [(2, CLON, CLAT)], visc, forces)
     base = jnp.zeros_like(velocity_cot)
     for visc_side, cot_side in zip(neighbours(visc_pad), neighbours(cot_pad)):
         base = base + 0.5 * (viscosity + visc_side)[None] * (cot_side - velocity_cot)

time: 184 us -> 175 us (0.951)
  local copies, waits for them, and re-layouts: 19.6 us -> 13.9 us
  other arithmetic: 19.2 us -> 14.3 us
  starting transfers between devices: 81.3 us -> 83.5 us
    ppermute x2 -> x4, starting transfers between devices: 15.7 us -> 21.2 us  [the longest x1 12.5 us: shards(): lax.ppermute(jnp.concatenate([coarse, several[:, :8]], axis=0), LON, back...]
    ppermute x1, waiting for transfers between devices: 4.4 us -> 0.01 us  [shards(): right = lax.ppermute(side_tiles(single[:, :, 0]), LAT, backward)]
    all_to_all x7, waiting for transfers between devices: 52.6 us -> 56.9 us  [exchange(): return lax.all_to_all(values, axes, 0, 0, tiled=True)]
    all_to_all x7, starting transfers between devices: 60.2 us -> 56.8 us  [exchange(): return lax.all_to_all(values, axes, 0, 0, tiled=True)]
  transfers between devices with their start and end apart: 11 -> 13, of which waited for: 8 -> 6; matrix products, arithmetic and copies ran while one was open for 11% -> 10% of each run, Pallas kernels for 0% -> 0%
where the time goes in v5:
time: 175 us; the launch traced here: 174 us
  starting transfers between devices  83.5 us (48%)
  waiting for transfers between devices  56.9 us (33%)
  other arithmetic  14.3 us (8%)
  local copies, waits for them, and re-layouts  13.9 us (8%)
  matrix products  2.61 us (1%)
    all_to_all x7, waiting for transfers between devices, exchange(): return lax.all_to_all(values, axes, 0, 0, tiled=True)  56.9 us
    all_to_all x7, starting transfers between devices, exchange(): return lax.all_to_all(values, axes, 0, 0, tiled=True)  56.8 us
    ppermute x1, starting transfers between devices, shards(): lax.ppermute(jnp.concatenate([coarse, several[:, :8]], axis=0), LON, back...  12.5 us
    broadcast_in_dim x6, local copies, waits for them, and re-layouts, to_all(): jnp.broadcast_to(block[None], (lax.axis_size(axes),) + block.shape)  3.87 us
    ppermute x1, starting transfers between devices, shards(): left = lax.ppermute(side_tiles(single[:, :, -1]), LAT, forward)  3.63 us
  transfers between devices with their start and end apart: 13, of which 6 were waited for; matrix products, arithmetic and copies ran while one was open for 10% of the time, Pallas kernels for 0%

profile of v5, /device:TPU:1, one launch (start us, length us, event | category | flops | bytes accessed | tf_op | source)
XLA Modules:
  0.0 174.0 jit_solution(2173512271420876097)
XLA Ops:
  2.3 18.2 %all-to-all-start = ((f32[64,1,128]{2,1,0:T(1,128)}), f32[64,1,128]{2,1,0:T(1,128)S(1)}, u32[]{:S(2)}, u32[]{:S(2)}) async-start(f32[64,1,128]{2,1,0:T(1,128)} %broadcast_in_dim.276), calls=%async_computation | async-start | bytes 65536 | tf_op jit(solution)/shard_map/all_to_all | solution.py:32
  22.9 3.3 %collective-permute-start.2 = (f32[68,8,128]{2,1,0:T(8,128)S(1)}, f32[68,8,128]{2,1,0:T(8,128)S(1)}, u32[]{:S(2)}, u32[]{:S(2)}) collective-permute-start(f32[68,8,128]{2,1,0:T(8,128)S(1)} %get-tuple-element.78), channel_id=1, source_target_pairs={{0,8},{8,16},{16,24},{24,32},{32,40},{40,48},{48,56},{56,64},{64,7... | collective-permute-start | bytes 835592 | tf_op jit(solution)/shard_map/ppermute | solution.py:293
  26.3 12.5 %collective-permute-start.3 = (f32[68,8,128]{2,1,0:T(8,128)S(1)}, f32[68,8,128]{2,1,0:T(8,128)S(1)}, u32[]{:S(2)}, u32[]{:S(2)}) collective-permute-start(f32[68,8,128]{2,1,0:T(8,128)S(1)} %get-tuple-element.77), channel_id=1, source_target_pairs={{8,0},{16,8},{24,16},{32,24},{40,32},{48,40},{56,48},{64,56},{72,6... | collective-permute-start | bytes 835592 | tf_op jit(solution)/shard_map/ppermute | solution.py:294
  41.9 3.6 %collective-permute-start = (f32[73,8,128]{2,1,0:T(8,128)S(1)}, f32[73,8,128]{2,1,0:T(8,128)S(1)}, u32[]{:S(2)}, u32[]{:S(2)}) collective-permute-start(f32[73,8,128]{2,1,0:T(8,128)S(1)} %get-tuple-element.76), channel_id=1, source_target_pairs={{0,1},{1,2},{2,3},{3,4},{4,5},{5,6},{6,7},{8,9},{9,10},{10,11},{11... | collective-permute-start | bytes 897032 | tf_op jit(solution)/shard_map/ppermute | solution.py:289
  45.5 1.9 %collective-permute-start.1 = (f32[73,8,128]{2,1,0:T(8,128)S(1)}, f32[73,8,128]{2,1,0:T(8,128)S(1)}, u32[]{:S(2)}, u32[]{:S(2)}) collective-permute-start(f32[73,8,128]{2,1,0:T(8,128)S(1)} %get-tuple-element.75), channel_id=1, source_target_pairs={{1,0},{2,1},{3,2},{4,3},{5,4},{6,5},{7,6},{9,8},{10,9},{11,10},{12... | collective-permute-start | bytes 897032 | tf_op jit(solution)/shard_map/ppermute | solution.py:290
  48.2 5.2 %all-to-all-start.1 = ((f32[16,4,128]{2,1,0:T(4,128)}), f32[16,4,128]{2,1,0:T(4,128)S(1)}, u32[]{:S(2)}, u32[]{:S(2)}) async-start(f32[16,4,128]{2,1,0:T(4,128)} %broadcast_in_dim.278), calls=%async_computation.1 | async-start | bytes 65536 | tf_op jit(solution)/shard_map/all_to_all | solution.py:32
  53.5 11.4 %all-to-all-done.1 = f32[16,4,128]{2,1,0:T(4,128)S(1)} async-done(((f32[16,4,128]{2,1,0:T(4,128)}), f32[16,4,128]{2,1,0:T(4,128)S(1)}, u32[]{:S(2)}, u32[]{:S(2)}) %all-to-all-start.1) | async-done | bytes 32800 | tf_op jit(solution)/shard_map/all_to_all | solution.py:32
  67.2 1.9 %collective-permute-start.5 = (f32[156,8,128]{2,1,0:T(8,128)}, f32[156,8,128]{2,1,0:T(8,128)S(1)}, u32[]{:S(2)}, u32[]{:S(2)}) collective-permute-start(f32[156,8,128]{2,1,0:T(8,128)} %get-tuple-element.63), channel_id=1, source_target_pairs={{8,0},{16,8},{24,16},{32,24},{40,32},{48,40},{56,48},{64,56},{72,6... | collective-permute-start | bytes 1916936 | tf_op jit(solution)/shard_map/ppermute | solution.py:341
  69.1 3.4 %collective-permute-start.4 = (f32[156,8,128]{2,1,0:T(8,128)}, f32[156,8,128]{2,1,0:T(8,128)S(1)}, u32[]{:S(2)}, u32[]{:S(2)}) collective-permute-start(f32[156,8,128]{2,1,0:T(8,128)} %get-tuple-element.64), channel_id=1, source_target_pairs={{0,8},{8,16},{16,24},{24,32},{32,40},{40,48},{48,56},{56,64},{64,7... | collective-permute-start | bytes 1916936 | tf_op jit(solution)/shard_map/ppermute | solution.py:340
  73.1 10.3 %all-to-all-start.2 = ((f32[64,1,128]{2,1,0:T(1,128)}), f32[64,1,128]{2,1,0:T(1,128)S(1)}, u32[]{:S(2)}, u32[]{:S(2)}) async-start(f32[64,1,128]{2,1,0:T(1,128)} %broadcast_in_dim.289), calls=%async_computation.2 | async-start | bytes 65536 | tf_op jit(solution)/shard_map/all_to_all | solution.py:32
  85.1 8.4 %all-to-all-done.2 = f32[64,1,128]{2,1,0:T(1,128)S(1)} async-done(((f32[64,1,128]{2,1,0:T(1,128)}), f32[64,1,128]{2,1,0:T(1,128)S(1)}, u32[]{:S(2)}, u32[]{:S(2)}) %all-to-all-start.2) | async-done | bytes 32800 | tf_op jit(solution)/shard_map/all_to_all | solution.py:32
  94.2 3.8 %all-to-all-start.3 = ((f32[16,4,128]{2,1,0:T(4,128)}), f32[16,4,128]{2,1,0:T(4,128)S(1)}, u32[]{:S(2)}, u32[]{:S(2)}) async-start(f32[16,4,128]{2,1,0:T(4,128)} %broadcast_in_dim.290), calls=%async_computation.3 | async-start | bytes 65536 | tf_op jit(solution)/shard_map/all_to_all | solution.py:32
  98.8 2.0 %pad_maximum_fusion.5 = (bf16[32,18,130]{2,1,0:T(8,128)(2,1)S(1)}, bf16[32,18,130]{2,1,0:T(8,128)(2,1)S(1)}, bf16[32,18,130]{2,1,0:T(8,128)(2,1)S(1)}) fusion(bf16[32,1,130]{2,1,0:T(2,128)(2,1)S(1)} %copy.156, bf16[32,1,130]{2,1,0:T(2,128)(2,1)S(1)} %copy.154, bf16[32,16,1]{2,1,0:T(8,128)(2,1)} %copy.150, bf16[32,16,128]{2,1,0:T(8,128)(2,1)S(1)} %copy-done.6, ...), kind=kLoop, calls=%fused_computation.21 | loop fusion | flops 2246400 | bytes 615680 | tf_op jit(solution)/shard_map/concatenate | solution.py:365
  102.5 1.3 multiply_reduce_fusion.1
  104.9 4.6 %all-to-all-done.3 = f32[16,4,128]{2,1,0:T(4,128)S(1)} async-done(((f32[16,4,128]{2,1,0:T(4,128)}), f32[16,4,128]{2,1,0:T(4,128)S(1)}, u32[]{:S(2)}, u32[]{:S(2)}) %all-to-all-start.3) | async-done | bytes 32800 | tf_op jit(solution)/shard_map/all_to_all | solution.py:32
  110.2 1.1 fusion.50
  111.9 1.1 copy-done.3
  116.0 7.1 %all-to-all-start.4 = ((f32[64,1,896]{2,1,0:T(1,128)}), f32[64,1,896]{2,1,0:T(1,128)S(1)}, u32[]{:S(2)}, u32[]{:S(2)}) async-start(f32[64,1,896]{2,1,0:T(1,128)} %reshape.305), calls=%async_computation.4 | async-start | bytes 458752 | tf_op jit(solution)/shard_map/all_to_all | solution.py:32
  123.3 12.4 %all-to-all-done.4 = f32[64,1,896]{2,1,0:T(1,128)S(1)} async-done(((f32[64,1,896]{2,1,0:T(1,128)}), f32[64,1,896]{2,1,0:T(1,128)S(1)}, u32[]{:S(2)}, u32[]{:S(2)}) %all-to-all-start.4) | async-done | bytes 229408 | tf_op jit(solution)/shard_map/all_to_all | solution.py:32
  137.3 6.1 %all-to-all-start.5 = ((f32[16,1,896]{2,1,0:T(1,128)}), f32[16,1,896]{2,1,0:T(1,128)S(1)}, u32[]{:S(2)}, u32[]{:S(2)}) async-start(f32[16,1,896]{2,1,0:T(1,128)} %broadcast_in_dim.315), calls=%async_computation.5 | async-start | bytes 114688 | tf_op jit(solution)/shard_map/all_to_all | solution.py:32
  143.5 11.5 %all-to-all-done.5.parts = f32[16,1,896]{2,1,0:T(1,128)S(1)} async-done(((f32[16,1,896]{2,1,0:T(1,128)}), f32[16,1,896]{2,1,0:T(1,128)S(1)}, u32[]{:S(2)}, u32[]{:S(2)}) %all-to-all-start.5) | async-done | bytes 57376 | tf_op jit(solution)/shard_map/all_to_all | solution.py:32
  156.5 6.1 %all-to-all-start.6 = ((f32[64,1,384]{2,1,0:T(1,128)}), f32[64,1,384]{2,1,0:T(1,128)S(1)}, u32[]{:S(2)}, u32[]{:S(2)}) async-start(f32[64,1,384]{2,1,0:T(1,128)} %broadcast_in_dim.318), calls=%async_computation.6 | async-start | bytes 196608 | tf_op jit(solution)/shard_map/all_to_all | solution.py:32
  162.6 1.3 fusion.36
  164.7 8.6 %all-to-all-done.6 = f32[64,1,384]{2,1,0:T(1,128)S(1)} async-done(((f32[64,1,384]{2,1,0:T(1,128)}), f32[64,1,384]{2,1,0:T(1,128)S(1)}, u32[]{:S(2)}, u32[]{:S(2)}) %all-to-all-start.6) | async-done | bytes 98336 | tf_op jit(solution)/shard_map/all_to_all | solution.py:32
  (186 shorter events, 25.3 us)
Async XLA Ops:
  0.6 101.6 %copy-start = (bf16[64,288]{1,0:T(8,128)(2,1)S(1)}, bf16[64,288]{1,0:T(8,128)(2,1)}, u32[]{:S(2)}) copy-start(bf16[64,288]{1,0:T(8,128)(2,1)} %param.20) | copy-start | bytes 110596
  2.3 45.3 %all-to-all-start = ((f32[64,1,128]{2,1,0:T(1,128)}), f32[64,1,128]{2,1,0:T(1,128)S(1)}, u32[]{:S(2)}, u32[]{:S(2)}) async-start(f32[64,1,128]{2,1,0:T(1,128)} %broadcast_in_dim.276), calls=%async_computation | async-start | bytes 65536 | tf_op jit(solution)/shard_map/all_to_all | solution.py:32
  22.9 42.0 %collective-permute-start.2 = (f32[68,8,128]{2,1,0:T(8,128)S(1)}, f32[68,8,128]{2,1,0:T(8,128)S(1)}, u32[]{:S(2)}, u32[]{:S(2)}) collective-permute-start(f32[68,8,128]{2,1,0:T(8,128)S(1)} %get-tuple-element.78), channel_id=1, source_target_pairs={{0,8},{8,16},{16,24},{24,32},{32,40},{40,48},{48,56},{56,64},{64,7... | collective-permute-start | bytes 835592 | tf_op jit(solution)/shard_map/ppermute | solution.py:293
  26.3 38.6 %collective-permute-start.3 = (f32[68,8,128]{2,1,0:T(8,128)S(1)}, f32[68,8,128]{2,1,0:T(8,128)S(1)}, u32[]{:S(2)}, u32[]{:S(2)}) collective-permute-start(f32[68,8,128]{2,1,0:T(8,128)S(1)} %get-tuple-element.77), channel_id=1, source_target_pairs={{8,0},{16,8},{24,16},{32,24},{40,32},{48,40},{56,48},{64,56},{72,6... | collective-permute-start | bytes 835592 | tf_op jit(solution)/shard_map/ppermute | solution.py:294
  39.7 2.1 %copy-start.1 = (f32[8,8192]{1,0:T(8,128)S(1)}, f32[8,8192]{1,0:T(8,128)}, u32[]{:S(2)}) copy-start(f32[8,8192]{1,0:T(8,128)} %param.19) | copy-start | bytes 786436
  40.7 6.8 %copy-start.6 = (bf16[32,16,128]{2,1,0:T(8,128)(2,1)S(1)}, bf16[32,16,128]{2,1,0:T(8,128)(2,1)}, u32[]{:S(2)}) copy-start(bf16[32,16,128]{2,1,0:T(8,128)(2,1)} %param.12) | copy-start | bytes 393220
  40.7 12.7 %copy-start.4 = (f32[8,16,128]{2,1,0:T(8,128)S(1)}, f32[8,16,128]{2,1,0:T(8,128)}, u32[]{:S(2)}) copy-start(f32[8,16,128]{2,1,0:T(8,128)} %param.14) | copy-start | bytes 196612
  40.7 12.7 %copy-start.5 = (f32[8,16,128]{2,1,0:T(8,128)S(1)}, f32[8,16,128]{2,1,0:T(8,128)}, u32[]{:S(2)}) copy-start(f32[8,16,128]{2,1,0:T(8,128)} %param.13) | copy-start | bytes 196612
  40.9 24.0 %copy-start.8 = (f32[16,128]{1,0:T(8,128)S(1)}, f32[16,128]{1,0:T(8,128)}, u32[]{:S(2)}) copy-start(f32[16,128]{1,0:T(8,128)} %param.15) | copy-start | bytes 24580
  40.9 24.0 %copy-start.9 = (f32[16,128]{1,0:T(8,128)S(1)}, f32[16,128]{1,0:T(8,128)}, u32[]{:S(2)}) copy-start(f32[16,128]{1,0:T(8,128)} %param.16) | copy-start | bytes 24580
  41.9 23.0 %collective-permute-start = (f32[73,8,128]{2,1,0:T(8,128)S(1)}, f32[73,8,128]{2,1,0:T(8,128)S(1)}, u32[]{:S(2)}, u32[]{:S(2)}) collective-permute-start(f32[73,8,128]{2,1,0:T(8,128)S(1)} %get-tuple-element.76), channel_id=1, source_target_pairs={{0,1},{1,2},{2,3},{3,4},{4,5},{5,6},{6,7},{8,9},{9,10},{10,11},{11... | collective-permute-start | bytes 897032 | tf_op jit(solution)/shard_map/ppermute | solution.py:289
  45.5 19.4 %collective-permute-start.1 = (f32[73,8,128]{2,1,0:T(8,128)S(1)}, f32[73,8,128]{2,1,0:T(8,128)S(1)}, u32[]{:S(2)}, u32[]{:S(2)}) collective-permute-start(f32[73,8,128]{2,1,0:T(8,128)S(1)} %get-tuple-element.75), channel_id=1, source_target_pairs={{1,0},{2,1},{3,2},{4,3},{5,4},{6,5},{7,6},{9,8},{10,9},{11,10},{12... | collective-permute-start | bytes 897032 | tf_op jit(solution)/shard_map/ppermute | solution.py:290
  48.2 16.7 %all-to-all-start.1 = ((f32[16,4,128]{2,1,0:T(4,128)}), f32[16,4,128]{2,1,0:T(4,128)S(1)}, u32[]{:S(2)}, u32[]{:S(2)}) async-start(f32[16,4,128]{2,1,0:T(4,128)} %broadcast_in_dim.278), calls=%async_computation.1 | async-start | bytes 65536 | tf_op jit(solution)/shard_map/all_to_all | solution.py:32
  67.2 30.8 %collective-permute-start.5 = (f32[156,8,128]{2,1,0:T(8,128)}, f32[156,8,128]{2,1,0:T(8,128)S(1)}, u32[]{:S(2)}, u32[]{:S(2)}) collective-permute-start(f32[156,8,128]{2,1,0:T(8,128)} %get-tuple-element.63), channel_id=1, source_target_pairs={{8,0},{16,8},{24,16},{32,24},{40,32},{48,40},{56,48},{64,56},{72,6... | collective-permute-start | bytes 1916936 | tf_op jit(solution)/shard_map/ppermute | solution.py:341
  69.1 28.9 %collective-permute-start.4 = (f32[156,8,128]{2,1,0:T(8,128)}, f32[156,8,128]{2,1,0:T(8,128)S(1)}, u32[]{:S(2)}, u32[]{:S(2)}) collective-permute-start(f32[156,8,128]{2,1,0:T(8,128)} %get-tuple-element.64), channel_id=1, source_target_pairs={{0,8},{8,16},{16,24},{24,32},{32,40},{40,48},{48,56},{56,64},{64,7... | collective-permute-start | bytes 1916936 | tf_op jit(solution)/shard_map/ppermute | solution.py:340
  73.1 20.4 %all-to-all-start.2 = ((f32[64,1,128]{2,1,0:T(1,128)}), f32[64,1,128]{2,1,0:T(1,128)S(1)}, u32[]{:S(2)}, u32[]{:S(2)}) async-start(f32[64,1,128]{2,1,0:T(1,128)} %broadcast_in_dim.289), calls=%async_computation.2 | async-start | bytes 65536 | tf_op jit(solution)/shard_map/all_to_all | solution.py:32
  94.2 15.3 %all-to-all-start.3 = ((f32[16,4,128]{2,1,0:T(4,128)}), f32[16,4,128]{2,1,0:T(4,128)S(1)}, u32[]{:S(2)}, u32[]{:S(2)}) async-start(f32[16,4,128]{2,1,0:T(4,128)} %broadcast_in_dim.290), calls=%async_computation.3 | async-start | bytes 65536 | tf_op jit(solution)/shard_map/all_to_all | solution.py:32
  102.2 2.7 %copy-start.2 = (bf16[36,8,18,128]{3,1,2,0:T(8,128)(2,1)}, bf16[36,8,18,128]{3,1,2,0:T(8,128)(2,1)S(1)}, u32[]{:S(2)}) copy-start(bf16[36,8,18,128]{3,1,2,0:T(8,128)(2,1)S(1)} %copy.188) | copy-start | bytes 3981316
  102.2 2.2 %copy-start.10 = (f32[8]{0:T(128)S(1)}, f32[8]{0:T(128)}, u32[]{:S(2)}) copy-start(f32[8]{0:T(128)} %param.23) | copy-start | bytes 100
  111.7 1.3 copy-start.3
  116.0 19.7 %all-to-all-start.4 = ((f32[64,1,896]{2,1,0:T(1,128)}), f32[64,1,896]{2,1,0:T(1,128)S(1)}, u32[]{:S(2)}, u32[]{:S(2)}) async-start(f32[64,1,896]{2,1,0:T(1,128)} %reshape.305), calls=%async_computation.4 | async-start | bytes 458752 | tf_op jit(solution)/shard_map/all_to_all | solution.py:32
  137.3 17.8 %all-to-all-start.5 = ((f32[16,1,896]{2,1,0:T(1,128)}), f32[16,1,896]{2,1,0:T(1,128)S(1)}, u32[]{:S(2)}, u32[]{:S(2)}) async-start(f32[16,1,896]{2,1,0:T(1,128)} %broadcast_in_dim.315), calls=%async_computation.5 | async-start | bytes 114688 | tf_op jit(solution)/shard_map/all_to_all | solution.py:32
  156.5 16.8 %all-to-all-start.6 = ((f32[64,1,384]{2,1,0:T(1,128)}), f32[64,1,384]{2,1,0:T(1,128)S(1)}, u32[]{:S(2)}, u32[]{:S(2)}) async-start(f32[64,1,384]{2,1,0:T(1,128)} %broadcast_in_dim.318), calls=%async_computation.6 | async-start | bytes 196608 | tf_op jit(solution)/shard_map/all_to_all | solution.py:32
  173.3 0.7 copy-start.7
  (2 other events, 1.3 us)

commit v6 on v5

--- a/solution.py
+++ b/solution.py
@@ -305,7 +305,7 @@
 
     row = merged(to_all(local, LAYER))
     gathered_first = to_all(row, DEPTH).reshape(-1, 128)
-    gathered_first, left, right, above, below = lax.optimization_barrier((gathered_first, left, right, above, below))
+    unused, left, right = lax.optimization_barrier((row, left, right))
 
     count = coarse.shape[0]
     line_left = left[-1].reshape(64, CLON)[:n_single]
@@ -326,7 +326,6 @@
         several,
         smem=1,
     )
-    row, line_left, line_right = lax.optimization_barrier((row, line_left, line_right))
     band = jnp.concatenate([left[:count], right[:count]], axis=0)
 
     def end_tiles(at, second, block):

time: 175 us -> 179 us (1.023)
  waiting for transfers between devices: 56.9 us -> 59.8 us
    ppermute x1, starting transfers between devices: 1.91 us -> 13.8 us  [shards(): far_below = lax.ppermute(end_tiles(0, 1, several[:, :8]), LON, backward_lon)]
    ppermute x1, starting transfers between devices: 12.5 us -> 6.68 us  [shards(): lax.ppermute(jnp.concatenate([coarse, several[:, :8]], axis=0), LON, back...]
    ppermute x1, waiting for transfers between devices: 0.01 us -> 4.4 us  [shards(): right = lax.ppermute(side_tiles(single[:, :, 0]), LAT, backward)]
    all_to_all x7, waiting for transfers between devices: 56.9 us -> 53.8 us  [exchange(): return lax.all_to_all(values, axes, 0, 0, tiled=True)]
    all_to_all x7, starting transfers between devices: 56.8 us -> 54.9 us  [exchange(): return lax.all_to_all(values, axes, 0, 0, tiled=True)]
  transfers between devices with their start and end apart: 13 -> 13, of which waited for: 6 -> 8; matrix products, arithmetic and copies ran while one was open for 10% -> 10% of each run, Pallas kernels for 0% -> 0%
where the time goes in v6:
time: 179 us; the launch traced here: 178 us
  starting transfers between devices  84.7 us (47%)
  waiting for transfers between devices  59.8 us (33%)
  local copies, waits for them, and re-layouts  14.2 us (8%)
  other arithmetic  13.5 us (8%)
  matrix products  2.6 us (1%)
    all_to_all x7, starting transfers between devices, exchange(): return lax.all_to_all(values, axes, 0, 0, tiled=True)  54.9 us
    all_to_all x7, waiting for transfers between devices, exchange(): return lax.all_to_all(values, axes, 0, 0, tiled=True)  53.8 us
    ppermute x1, starting transfers between devices, shards(): far_below = lax.ppermute(end_tiles(0, 1, several[:, :8]), LON, backward_lon)  13.8 us
    ppermute x1, starting transfers between devices, shards(): lax.ppermute(jnp.concatenate([coarse, several[:, :8]], axis=0), LON, back...  6.68 us
    ppermute x1, waiting for transfers between devices, shards(): right = lax.ppermute(side_tiles(single[:, :, 0]), LAT, backward)  4.4 us
    broadcast_in_dim x6, local copies, waits for them, and re-layouts, to_all(): jnp.broadcast_to(block[None], (lax.axis_size(axes),) + block.shape)  3.87 us
  transfers between devices with their start and end apart: 13, of which 8 were waited for; matrix products, arithmetic and copies ran while one was open for 10% of the time, Pallas kernels for 0%

profile of v6, /device:TPU:1, one launch (start us, length us, event | category | flops | bytes accessed | tf_op | source)
XLA Modules:
  0.0 177.7 jit_solution(7898270427815693696)
XLA Ops:
  2.3 18.2 %all-to-all-start = ((f32[64,1,128]{2,1,0:T(1,128)}), f32[64,1,128]{2,1,0:T(1,128)S(1)}, u32[]{:S(2)}, u32[]{:S(2)}) async-start(f32[64,1,128]{2,1,0:T(1,128)} %broadcast_in_dim.276), calls=%async_computation | async-start | bytes 65536 | tf_op jit(solution)/shard_map/all_to_all | solution.py:32
  24.3 3.5 %collective-permute-start = (f32[73,8,128]{2,1,0:T(8,128)S(1)}, f32[73,8,128]{2,1,0:T(8,128)S(1)}, u32[]{:S(2)}, u32[]{:S(2)}) collective-permute-start(f32[73,8,128]{2,1,0:T(8,128)S(1)} %get-tuple-element.68), channel_id=1, source_target_pairs={{0,1},{1,2},{2,3},{3,4},{4,5},{5,6},{6,7},{8,9},{9,10},{10,11},{11... | collective-permute-start | bytes 897032 | tf_op jit(solution)/shard_map/ppermute | solution.py:289
  27.9 1.9 %collective-permute-start.1 = (f32[73,8,128]{2,1,0:T(8,128)S(1)}, f32[73,8,128]{2,1,0:T(8,128)S(1)}, u32[]{:S(2)}, u32[]{:S(2)}) collective-permute-start(f32[73,8,128]{2,1,0:T(8,128)S(1)} %get-tuple-element.67), channel_id=1, source_target_pairs={{1,0},{2,1},{3,2},{4,3},{5,4},{6,5},{7,6},{9,8},{10,9},{11,10},{12... | collective-permute-start | bytes 897032 | tf_op jit(solution)/shard_map/ppermute | solution.py:290
  30.0 1.6 collective-permute-done.left
  31.5 4.4 %collective-permute-done.1.right = f32[73,8,128]{2,1,0:T(8,128)S(1)} collective-permute-done((f32[73,8,128]{2,1,0:T(8,128)S(1)}, f32[73,8,128]{2,1,0:T(8,128)S(1)}, u32[]{:S(2)}, u32[]{:S(2)}) %collective-permute-start.1) | collective-permute-done | bytes 299040 | tf_op jit(solution)/shard_map/ppermute | solution.py:290
  37.8 13.8 %collective-permute-start.3 = (f32[156,8,128]{2,1,0:T(8,128)}, f32[156,8,128]{2,1,0:T(8,128)S(1)}, u32[]{:S(2)}, u32[]{:S(2)}) collective-permute-start(f32[156,8,128]{2,1,0:T(8,128)} %get-tuple-element.55), channel_id=1, source_target_pairs={{8,0},{16,8},{24,16},{32,24},{40,32},{48,40},{56,48},{64,56},{72,6... | collective-permute-start | bytes 1916936 | tf_op jit(solution)/shard_map/ppermute | solution.py:340
  52.4 1.9 %collective-permute-start.4 = (f32[68,8,128]{2,1,0:T(8,128)}, f32[68,8,128]{2,1,0:T(8,128)S(1)}, u32[]{:S(2)}, u32[]{:S(2)}) collective-permute-start(f32[68,8,128]{2,1,0:T(8,128)} %get-tuple-element.70), channel_id=1, source_target_pairs={{0,8},{8,16},{16,24},{24,32},{32,40},{40,48},{48,56},{56,64},{64,7... | collective-permute-start | bytes 835592 | tf_op jit(solution)/shard_map/ppermute | solution.py:293
  54.4 6.7 %collective-permute-start.5 = (f32[68,8,128]{2,1,0:T(8,128)}, f32[68,8,128]{2,1,0:T(8,128)S(1)}, u32[]{:S(2)}, u32[]{:S(2)}) collective-permute-start(f32[68,8,128]{2,1,0:T(8,128)} %get-tuple-element.69), channel_id=1, source_target_pairs={{8,0},{16,8},{24,16},{32,24},{40,32},{48,40},{56,48},{64,56},{72,6... | collective-permute-start | bytes 835592 | tf_op jit(solution)/shard_map/ppermute | solution.py:294
  61.7 3.5 %all-to-all-start.1 = ((f32[16,4,128]{2,1,0:T(4,128)}), f32[16,4,128]{2,1,0:T(4,128)S(1)}, u32[]{:S(2)}, u32[]{:S(2)}) async-start(f32[16,4,128]{2,1,0:T(4,128)} %broadcast_in_dim.286), calls=%async_computation.1 | async-start | bytes 65536 | tf_op jit(solution)/shard_map/all_to_all | solution.py:32
  65.2 1.9 %collective-permute-start.2 = (f32[156,8,128]{2,1,0:T(8,128)}, f32[156,8,128]{2,1,0:T(8,128)S(1)}, u32[]{:S(2)}, u32[]{:S(2)}) collective-permute-start(f32[156,8,128]{2,1,0:T(8,128)} %get-tuple-element.56), channel_id=1, source_target_pairs={{0,8},{8,16},{16,24},{24,32},{32,40},{40,48},{48,56},{56,64},{64,7... | collective-permute-start | bytes 1916936 | tf_op jit(solution)/shard_map/ppermute | solution.py:339
  68.6 8.0 %all-to-all-done.1 = f32[16,4,128]{2,1,0:T(4,128)S(1)} async-done(((f32[16,4,128]{2,1,0:T(4,128)}), f32[16,4,128]{2,1,0:T(4,128)S(1)}, u32[]{:S(2)}, u32[]{:S(2)}) %all-to-all-start.1) | async-done | bytes 32800 | tf_op jit(solution)/shard_map/all_to_all | solution.py:32
  77.6 5.9 %all-to-all-start.2 = ((f32[64,1,128]{2,1,0:T(1,128)}), f32[64,1,128]{2,1,0:T(1,128)S(1)}, u32[]{:S(2)}, u32[]{:S(2)}) async-start(f32[64,1,128]{2,1,0:T(1,128)} %broadcast_in_dim.289), calls=%async_computation.2 | async-start | bytes 65536 | tf_op jit(solution)/shard_map/all_to_all | solution.py:32
  84.1 8.7 %all-to-all-done.2 = f32[64,1,128]{2,1,0:T(1,128)S(1)} async-done(((f32[64,1,128]{2,1,0:T(1,128)}), f32[64,1,128]{2,1,0:T(1,128)S(1)}, u32[]{:S(2)}, u32[]{:S(2)}) %all-to-all-start.2) | async-done | bytes 32800 | tf_op jit(solution)/shard_map/all_to_all | solution.py:32
  93.4 8.1 %all-to-all-start.3 = ((f32[16,4,128]{2,1,0:T(4,128)}), f32[16,4,128]{2,1,0:T(4,128)S(1)}, u32[]{:S(2)}, u32[]{:S(2)}) async-start(f32[16,4,128]{2,1,0:T(4,128)} %broadcast_in_dim.290), calls=%async_computation.3 | async-start | bytes 65536 | tf_op jit(solution)/shard_map/all_to_all | solution.py:32
  102.5 2.0 %pad_maximum_fusion.5 = (bf16[32,18,130]{2,1,0:T(8,128)(2,1)S(1)}, bf16[32,18,130]{2,1,0:T(8,128)(2,1)S(1)}, bf16[32,18,130]{2,1,0:T(8,128)(2,1)S(1)}) fusion(bf16[32,1,130]{2,1,0:T(2,128)(2,1)S(1)} %copy.156, bf16[32,1,130]{2,1,0:T(2,128)(2,1)S(1)} %copy.154, bf16[32,16,1]{2,1,0:T(8,128)(2,1)} %broadcast_in_dim.320, bf16[32,16,128]{2,1,0:T(8,128)(2,1)S(1)} %copy-done.6, ...), kind=kLoop, calls=%fused_computation.21 | loop fusion | flops 2246400 | bytes 615680 | tf_op jit(solution)/shard_map/concatenate | solution.py:364
  106.1 1.3 multiply_reduce_fusion.1
  108.5 4.6 %all-to-all-done.3 = f32[16,4,128]{2,1,0:T(4,128)S(1)} async-done(((f32[16,4,128]{2,1,0:T(4,128)}), f32[16,4,128]{2,1,0:T(4,128)S(1)}, u32[]{:S(2)}, u32[]{:S(2)}) %all-to-all-start.3) | async-done | bytes 32800 | tf_op jit(solution)/shard_map/all_to_all | solution.py:32
  119.7 7.1 %all-to-all-start.4 = ((f32[64,1,896]{2,1,0:T(1,128)}), f32[64,1,896]{2,1,0:T(1,128)S(1)}, u32[]{:S(2)}, u32[]{:S(2)}) async-start(f32[64,1,896]{2,1,0:T(1,128)} %reshape.317), calls=%async_computation.4 | async-start | bytes 458752 | tf_op jit(solution)/shard_map/all_to_all | solution.py:32
  127.0 12.4 %all-to-all-done.4 = f32[64,1,896]{2,1,0:T(1,128)S(1)} async-done(((f32[64,1,896]{2,1,0:T(1,128)}), f32[64,1,896]{2,1,0:T(1,128)S(1)}, u32[]{:S(2)}, u32[]{:S(2)}) %all-to-all-start.4) | async-done | bytes 229408 | tf_op jit(solution)/shard_map/all_to_all | solution.py:32
  140.9 6.1 %all-to-all-start.5 = ((f32[16,1,896]{2,1,0:T(1,128)}), f32[16,1,896]{2,1,0:T(1,128)S(1)}, u32[]{:S(2)}, u32[]{:S(2)}) async-start(f32[16,1,896]{2,1,0:T(1,128)} %broadcast_in_dim.315), calls=%async_computation.5 | async-start | bytes 114688 | tf_op jit(solution)/shard_map/all_to_all | solution.py:32
  147.2 11.5 %all-to-all-done.5.parts = f32[16,1,896]{2,1,0:T(1,128)S(1)} async-done(((f32[16,1,896]{2,1,0:T(1,128)}), f32[16,1,896]{2,1,0:T(1,128)S(1)}, u32[]{:S(2)}, u32[]{:S(2)}) %all-to-all-start.5) | async-done | bytes 57376 | tf_op jit(solution)/shard_map/all_to_all | solution.py:32
  160.2 6.1 %all-to-all-start.6 = ((f32[64,1,384]{2,1,0:T(1,128)}), f32[64,1,384]{2,1,0:T(1,128)S(1)}, u32[]{:S(2)}, u32[]{:S(2)}) async-start(f32[64,1,384]{2,1,0:T(1,128)} %broadcast_in_dim.318), calls=%async_computation.6 | async-start | bytes 196608 | tf_op jit(solution)/shard_map/all_to_all | solution.py:32
  166.2 1.3 fusion.34
  168.4 8.6 %all-to-all-done.6 = f32[64,1,384]{2,1,0:T(1,128)S(1)} async-done(((f32[64,1,384]{2,1,0:T(1,128)}), f32[64,1,384]{2,1,0:T(1,128)S(1)}, u32[]{:S(2)}, u32[]{:S(2)}) %all-to-all-start.6) | async-done | bytes 98336 | tf_op jit(solution)/shard_map/all_to_all | solution.py:32
  (186 shorter events, 27.2 us)
Async XLA Ops:
  0.6 105.2 %copy-start = (bf16[64,288]{1,0:T(8,128)(2,1)S(1)}, bf16[64,288]{1,0:T(8,128)(2,1)}, u32[]{:S(2)}) copy-start(bf16[64,288]{1,0:T(8,128)(2,1)} %param.20) | copy-start | bytes 110596
  2.3 27.7 %all-to-all-start = ((f32[64,1,128]{2,1,0:T(1,128)}), f32[64,1,128]{2,1,0:T(1,128)S(1)}, u32[]{:S(2)}, u32[]{:S(2)}) async-start(f32[64,1,128]{2,1,0:T(1,128)} %broadcast_in_dim.276), calls=%async_computation | async-start | bytes 65536 | tf_op jit(solution)/shard_map/all_to_all | solution.py:32
  22.1 2.1 %copy-start.8 = (f32[16,128]{1,0:T(8,128)S(1)}, f32[16,128]{1,0:T(8,128)}, u32[]{:S(2)}) copy-start(f32[16,128]{1,0:T(8,128)} %param.15) | copy-start | bytes 24580
  22.1 2.1 %copy-start.9 = (f32[16,128]{1,0:T(8,128)S(1)}, f32[16,128]{1,0:T(8,128)}, u32[]{:S(2)}) copy-start(f32[16,128]{1,0:T(8,128)} %param.16) | copy-start | bytes 24580
  22.2 2.1 %copy-start.1 = (f32[8,8192]{1,0:T(8,128)S(1)}, f32[8,8192]{1,0:T(8,128)}, u32[]{:S(2)}) copy-start(f32[8,8192]{1,0:T(8,128)} %param.19) | copy-start | bytes 786436
  23.1 6.7 %copy-start.6 = (bf16[32,16,128]{2,1,0:T(8,128)(2,1)S(1)}, bf16[32,16,128]{2,1,0:T(8,128)(2,1)}, u32[]{:S(2)}) copy-start(bf16[32,16,128]{2,1,0:T(8,128)(2,1)} %param.12) | copy-start | bytes 393220
  23.1 6.7 %copy-start.4 = (f32[8,16,128]{2,1,0:T(8,128)S(1)}, f32[8,16,128]{2,1,0:T(8,128)}, u32[]{:S(2)}) copy-start(f32[8,16,128]{2,1,0:T(8,128)} %param.14) | copy-start | bytes 196612
  23.1 6.7 %copy-start.5 = (f32[8,16,128]{2,1,0:T(8,128)S(1)}, f32[8,16,128]{2,1,0:T(8,128)}, u32[]{:S(2)}) copy-start(f32[8,16,128]{2,1,0:T(8,128)} %param.13) | copy-start | bytes 196612
  24.3 7.2 %collective-permute-start = (f32[73,8,128]{2,1,0:T(8,128)S(1)}, f32[73,8,128]{2,1,0:T(8,128)S(1)}, u32[]{:S(2)}, u32[]{:S(2)}) collective-permute-start(f32[73,8,128]{2,1,0:T(8,128)S(1)} %get-tuple-element.68), channel_id=1, source_target_pairs={{0,1},{1,2},{2,3},{3,4},{4,5},{5,6},{6,7},{8,9},{9,10},{10,11},{11... | collective-permute-start | bytes 897032 | tf_op jit(solution)/shard_map/ppermute | solution.py:289
  27.9 8.1 %collective-permute-start.1 = (f32[73,8,128]{2,1,0:T(8,128)S(1)}, f32[73,8,128]{2,1,0:T(8,128)S(1)}, u32[]{:S(2)}, u32[]{:S(2)}) collective-permute-start(f32[73,8,128]{2,1,0:T(8,128)S(1)} %get-tuple-element.67), channel_id=1, source_target_pairs={{1,0},{2,1},{3,2},{4,3},{5,4},{6,5},{7,6},{9,8},{10,9},{11,10},{12... | collective-permute-start | bytes 897032 | tf_op jit(solution)/shard_map/ppermute | solution.py:290
  37.8 63.8 %collective-permute-start.3 = (f32[156,8,128]{2,1,0:T(8,128)}, f32[156,8,128]{2,1,0:T(8,128)S(1)}, u32[]{:S(2)}, u32[]{:S(2)}) collective-permute-start(f32[156,8,128]{2,1,0:T(8,128)} %get-tuple-element.55), channel_id=1, source_target_pairs={{8,0},{16,8},{24,16},{32,24},{40,32},{48,40},{56,48},{64,56},{72,6... | collective-permute-start | bytes 1916936 | tf_op jit(solution)/shard_map/ppermute | solution.py:340
  52.4 24.1 %collective-permute-start.4 = (f32[68,8,128]{2,1,0:T(8,128)}, f32[68,8,128]{2,1,0:T(8,128)S(1)}, u32[]{:S(2)}, u32[]{:S(2)}) collective-permute-start(f32[68,8,128]{2,1,0:T(8,128)} %get-tuple-element.70), channel_id=1, source_target_pairs={{0,8},{8,16},{16,24},{24,32},{32,40},{40,48},{48,56},{56,64},{64,7... | collective-permute-start | bytes 835592 | tf_op jit(solution)/shard_map/ppermute | solution.py:293
  54.4 22.2 %collective-permute-start.5 = (f32[68,8,128]{2,1,0:T(8,128)}, f32[68,8,128]{2,1,0:T(8,128)S(1)}, u32[]{:S(2)}, u32[]{:S(2)}) collective-permute-start(f32[68,8,128]{2,1,0:T(8,128)} %get-tuple-element.69), channel_id=1, source_target_pairs={{8,0},{16,8},{24,16},{32,24},{40,32},{48,40},{56,48},{64,56},{72,6... | collective-permute-start | bytes 835592 | tf_op jit(solution)/shard_map/ppermute | solution.py:294
  61.7 14.9 %all-to-all-start.1 = ((f32[16,4,128]{2,1,0:T(4,128)}), f32[16,4,128]{2,1,0:T(4,128)S(1)}, u32[]{:S(2)}, u32[]{:S(2)}) async-start(f32[16,4,128]{2,1,0:T(4,128)} %broadcast_in_dim.286), calls=%async_computation.1 | async-start | bytes 65536 | tf_op jit(solution)/shard_map/all_to_all | solution.py:32
  65.2 36.4 %collective-permute-start.2 = (f32[156,8,128]{2,1,0:T(8,128)}, f32[156,8,128]{2,1,0:T(8,128)S(1)}, u32[]{:S(2)}, u32[]{:S(2)}) collective-permute-start(f32[156,8,128]{2,1,0:T(8,128)} %get-tuple-element.56), channel_id=1, source_target_pairs={{0,8},{8,16},{16,24},{24,32},{32,40},{40,48},{48,56},{56,64},{64,7... | collective-permute-start | bytes 1916936 | tf_op jit(solution)/shard_map/ppermute | solution.py:339
  77.6 15.2 %all-to-all-start.2 = ((f32[64,1,128]{2,1,0:T(1,128)}), f32[64,1,128]{2,1,0:T(1,128)S(1)}, u32[]{:S(2)}, u32[]{:S(2)}) async-start(f32[64,1,128]{2,1,0:T(1,128)} %broadcast_in_dim.289), calls=%async_computation.2 | async-start | bytes 65536 | tf_op jit(solution)/shard_map/all_to_all | solution.py:32
  93.4 19.6 %all-to-all-start.3 = ((f32[16,4,128]{2,1,0:T(4,128)}), f32[16,4,128]{2,1,0:T(4,128)S(1)}, u32[]{:S(2)}, u32[]{:S(2)}) async-start(f32[16,4,128]{2,1,0:T(4,128)} %broadcast_in_dim.290), calls=%async_computation.3 | async-start | bytes 65536 | tf_op jit(solution)/shard_map/all_to_all | solution.py:32
  105.8 2.7 %copy-start.2 = (bf16[36,8,18,128]{3,1,2,0:T(8,128)(2,1)}, bf16[36,8,18,128]{3,1,2,0:T(8,128)(2,1)S(1)}, u32[]{:S(2)}) copy-start(bf16[36,8,18,128]{3,1,2,0:T(8,128)(2,1)S(1)} %copy.188) | copy-start | bytes 3981316
  105.8 2.2 %copy-start.10 = (f32[8]{0:T(128)S(1)}, f32[8]{0:T(128)}, u32[]{:S(2)}) copy-start(f32[8]{0:T(128)} %param.23) | copy-start | bytes 100
  115.4 1.3 copy-start.3
  119.7 19.7 %all-to-all-start.4 = ((f32[64,1,896]{2,1,0:T(1,128)}), f32[64,1,896]{2,1,0:T(1,128)S(1)}, u32[]{:S(2)}, u32[]{:S(2)}) async-start(f32[64,1,896]{2,1,0:T(1,128)} %reshape.317), calls=%async_computation.4 | async-start | bytes 458752 | tf_op jit(solution)/shard_map/all_to_all | solution.py:32
  140.9 17.7 %all-to-all-start.5 = ((f32[16,1,896]{2,1,0:T(1,128)}), f32[16,1,896]{2,1,0:T(1,128)S(1)}, u32[]{:S(2)}, u32[]{:S(2)}) async-start(f32[16,1,896]{2,1,0:T(1,128)} %broadcast_in_dim.315), calls=%async_computation.5 | async-start | bytes 114688 | tf_op jit(solution)/shard_map/all_to_all | solution.py:32
  160.2 16.8 %all-to-all-start.6 = ((f32[64,1,384]{2,1,0:T(1,128)}), f32[64,1,384]{2,1,0:T(1,128)S(1)}, u32[]{:S(2)}, u32[]{:S(2)}) async-start(f32[64,1,384]{2,1,0:T(1,128)} %broadcast_in_dim.318), calls=%async_computation.6 | async-start | bytes 196608 | tf_op jit(solution)/shard_map/all_to_all | solution.py:32
  177.0 0.7 copy-start.7
  (2 other events, 1.3 us)
